TPU v7x, 32 devices: a whole 2x2x4 slice. The times are simulated.
32 devices in a mesh: dp: 8 (over z, y), hid: 4 (over x, core).
Axes of the slice: x: 2, y: 2, z: 4, core: 2. Of those that a mesh axis runs over, the one named last changes fastest.
Arguments:
- gate_pre: bfloat16 [1024, 2, 8192], P('dp', None, 'hid'), may hold values from -6 to 6
- up_pre: bfloat16 [1024, 2, 8192], P('dp', None, 'hid'), may hold values from -6 to 6
- out_grad: bfloat16 [1024, 6144], P('dp'), may hold values from -6 to 6
- combine: float32 [1024, 2], P('dp'), may hold values from 0.1 to 0.9
- expert_ids: int32 [1024, 2], P('dp'), may hold values from 0 to 7, all different within a row; in each aligned block of 128 rows (0 to 127, 128 to 255, ...) at most 48 rows name the same one
- down_weight: bfloat16 [8, 8192, 6144], P('dp', 'hid'), may hold values from -0.0625 to 0.0625
Outputs:
- mixed: bfloat16 [1024, 1, 6144], P('dp', None, 'hid')
- combine_grad: float32 [1024, 2], P('dp')
- gate_grad: bfloat16 [1024, 2, 8192], P('dp', None, 'hid')
- up_grad: bfloat16 [1024, 2, 8192], P('dp', None, 'hid')
- weight_grad: bfloat16 [8, 8192, 6144], P('dp', 'hid')
Inputs may be any that keep to these rules, and one draw needn't show every extreme that they name: `expert_ids`: each token names two different experts. Among the 128 tokens of one dp index no expert is named by more than 48 tokens, and in every draw some expert is named by exactly 48 of them.
All inputs are finite; a program needn't handle non-finite values.
Results may differ from a plain program's by a relative error of at most 0.0057.
Values may be sent and summed in bfloat16 or wider, within the bound.
No kernel may reach another device: no remote copies, remote signals or barrier semaphores. Data moves between devices by JAX's collectives and lax.ppermute only.
A program may use at most 448 MiB of HBM per device.

v0:
```python
import jax
import jax.numpy as jnp
from jax import lax
from jax.sharding import PartitionSpec as P

E = 8
TOP = 2
CAP = 48


def per_device(gate_pre, up_pre, out_grad, combine, expert_ids, down_weight):
    dp_count = lax.axis_size("dp")
    hid_count = lax.axis_size("hid")
    experts = E
    slices = dp_count // experts
    capacity = CAP
    tokens_here = gate_pre.shape[0]
    local_ff = gate_pre.shape[2]
    slice_width = down_weight.shape[2]
    quarter = slice_width // hid_count
    slot_count = tokens_here * TOP
    flat_ids = expert_ids.reshape(slot_count)
    onehot = (flat_ids[:, None] == jnp.arange(experts, dtype=jnp.int32)[None, :]).astype(jnp.int32)
    earlier = jnp.cumsum(onehot, axis=0) - onehot
    position = jnp.sum(earlier * onehot, axis=1)
    target = flat_ids * capacity + position
    routing_table = (
        target[None, :] == jnp.arange(experts * capacity, dtype=jnp.int32)[:, None]
    ).astype(jnp.int32)
    slot_numbers = jnp.arange(slot_count, dtype=jnp.int32)
    filled = jnp.sum(routing_table, axis=1)
    source_slot = jnp.sum(routing_table * slot_numbers[None, :], axis=1) + (1 - filled) * (
        slot_count * slices
    )
    source_slot = source_slot.reshape(experts, 1, capacity)
    slice_index = jnp.arange(slices, dtype=jnp.int32).reshape(1, slices, 1)
    gate_f = gate_pre.astype(jnp.float32)
    up_f = up_pre.astype(jnp.float32)
    sigmoid_gate = jax.nn.sigmoid(gate_f)
    hidden = (gate_f * sigmoid_gate * up_f).astype(jnp.bfloat16).reshape(slot_count, local_ff)
    scaled = (combine[:, :, None] * out_grad[:, None, :].astype(jnp.float32)).astype(jnp.bfloat16)
    scaled_rows = scaled.reshape(slot_count * slices, slice_width)
    hidden_index = jnp.broadcast_to(source_slot, (experts, slices, capacity)).reshape(
        dp_count * capacity
    )
    grad_index = (source_slot * slices + slice_index).reshape(dp_count * capacity)
    send_hidden = jnp.take(hidden, hidden_index, axis=0, mode="fill", fill_value=0).reshape(
        dp_count, capacity, local_ff
    )
    send_grad = jnp.take(scaled_rows, grad_index, axis=0, mode="fill", fill_value=0).reshape(
        dp_count, capacity, slice_width
    )
    got_hidden, got_grad = (
        lax.all_to_all(send_hidden, "dp", split_axis=0, concat_axis=0, tiled=True),
        lax.all_to_all(send_grad, "dp", split_axis=0, concat_axis=0, tiled=True),
    )
    hidden_rows = got_hidden.reshape(dp_count * capacity, local_ff)
    grad_rows = got_grad.reshape(dp_count * capacity, slice_width)
    weights = down_weight[0]
    expert_out = jnp.dot(hidden_rows, weights, preferred_element_type=jnp.float32)
    partial_back = lax.dot_general(
        grad_rows, weights, (((1,), (1,)), ((), ())), preferred_element_type=jnp.float32
    )
    weight_grad = lax.dot_general(
        hidden_rows, grad_rows, (((0,), (0,)), ((), ())), preferred_element_type=jnp.float32
    )
    weight_grad = weight_grad.astype(jnp.bfloat16)[None]
    partial_back = partial_back.reshape(dp_count, capacity, local_ff)
    return_index = (
        (flat_ids[:, None] * slices + jnp.arange(slices, dtype=jnp.int32)[None, :]) * capacity
        + position[:, None]
    ).reshape(slot_count * slices)
    back_out, back_grad = (
        lax.all_to_all(
            expert_out.reshape(dp_count, capacity, slice_width),
            "dp",
            split_axis=0,
            concat_axis=0,
            tiled=True,
        ),
        lax.all_to_all(partial_back, "dp", split_axis=0, concat_axis=0, tiled=True),
    )
    slot_part = jnp.take(back_out.reshape(dp_count * capacity, slice_width), return_index, axis=0)
    slot_part = slot_part.reshape(slot_count, slices, slice_width)
    slot_out = lax.psum_scatter(slot_part, "hid", scatter_dimension=2, tiled=True)
    grad_parts = jnp.take(back_grad.reshape(dp_count * capacity, local_ff), return_index, axis=0)
    hidden_grad = jnp.sum(grad_parts.reshape(slot_count, slices, local_ff), axis=1)
    slot_out = slot_out.reshape(tokens_here, TOP, slices, quarter)
    mixed = jnp.sum(combine[:, :, None, None] * slot_out, axis=1).astype(jnp.bfloat16)
    hid_index = lax.axis_index("hid")
    grad_view = out_grad.reshape(tokens_here, slices, hid_count, quarter)
    my_columns = lax.dynamic_index_in_dim(grad_view, hid_index, 2, keepdims=False).astype(
        jnp.float32
    )
    local_terms = jnp.sum(my_columns[:, None] * slot_out, axis=(2, 3))
    combine_grad = lax.psum(local_terms, "hid")
    hidden_grad = hidden_grad.reshape(tokens_here, TOP, local_ff)
    gate_grad = (hidden_grad * up_f * sigmoid_gate * (1.0 + gate_f * (1.0 - sigmoid_gate))).astype(
        jnp.bfloat16
    )
    up_grad = (hidden_grad * gate_f * sigmoid_gate).astype(jnp.bfloat16)
    return (mixed, combine_grad, gate_grad, up_grad, weight_grad)


def solution(mesh):
    return jax.shard_map(
        per_device,
        mesh=mesh,
        in_specs=(
            P("dp", None, "hid"),
            P("dp", None, "hid"),
            P("dp", None),
            P("dp", None),
            P("dp", None),
            P("dp", "hid", None),
        ),
        out_specs=(
            P("dp", None, "hid"),
            P("dp", None),
            P("dp", None, "hid"),
            P("dp", None, "hid"),
            P("dp", "hid", None),
        ),
        check_vma=False,
    )
```

profile of v0, /device:TPU:0, one launch (start us, length us, event | category | flops | bytes accessed | tf_op | source)
XLA Modules:
  0.0 623.0 jit_solution(3090309241580725283)
XLA Ops:
  7.2 0.8 copy.26
  8.0 0.1 broadcast_in_dim_reshape.4
  8.1 0.1 eq.39
  8.2 0.6 reduce-window.6
  8.8 0.2 slice_reduce_fusion
  9.1 0.1 fusion.16
  9.2 0.2 convert_reduce_fusion
  9.5 0.8 copy.25
  10.3 0.1 mul.164
  10.5 6.7 %mul.166 = f32[128,2,6144]{2,1,0:T(2,128)} broadcast(bf16[128,6144]{1,0:T(8,128)(2,1)} %param.8), dimensions={0,2} | broadcast | bytes 7864320 | tf_op jit(solution)/shard_map/mul | solution.py:41
  17.2 8.3 %mul.167 = f32[256,6144]{1,0:T(8,128)} reshape(f32[128,2,6144]{2,1,0:T(2,128)} %mul.166) | data formatting | bytes 12582912 | tf_op jit(solution)/shard_map/mul | solution.py:41
  25.6 3.4 multiply_convert_fusion
  29.0 5.5 gather_fusion.2
  34.6 2.7 broadcast_select_fusion
  37.3 111.6 %all_to_all.20 = bf16[8,48,6144]{2,1,0:T(8,128)(2,1)} all-to-all(bf16[8,48,6144]{2,1,0:T(8,128)(2,1)S(1)} %broadcast_select_fusion), channel_id=1, replica_groups=mesh['dp'=8,'hid'=4] {'dp'}, dimensions={0} | all-to-all | bytes 9437184 | tf_op jit(solution)/shard_map/all_to_all | solution.py:55
  148.9 17.2 %fusion = f32[8,48,2048]{2,1,0:T(8,128)} fusion(bf16[8,48,6144]{2,1,0:T(8,128)(2,1)} %all_to_all.20, bf16[1,2048,6144]{2,1,0:T(8,128)(2,1)} %param.11), kind=kOutput, calls=%fused_computation.5 | convolution fusion | flops 9663676416 | bytes 33030144 | tf_op jit(solution)/shard_map/dot_general | solution.py:61
  166.1 3.8 all-to-all-start.3
  169.9 0.2 reduce-scatter.2.cloned.1.call-start
  170.1 0.1 reduce_sum.62
  170.2 0.1 copy.28
  170.4 0.1 mul.157
  170.6 0.1 copy.30
  170.8 69.4 %all-to-all-done.3 = f32[8,48,2048]{2,1,0:T(8,128)S(1)} async-done(((f32[8,48,2048]{2,1,0:T(8,128)}), f32[8,48,2048]{2,1,0:T(8,128)S(1)}, u32[]{:S(2)}, u32[]{:S(2)}) %all-to-all-start.3) | async-done | bytes 3145760 | tf_op jit(solution)/shard_map/all_to_all | solution.py:81
  240.2 2.7 gather_fusion.3
  242.8 2.6 gather.31
  245.5 3.9 fusion.14
  249.4 4.9 fusion.8
  254.3 0.4 reshape.241
  254.7 2.5 gather_fusion
  257.2 0.2 broadcast_select_fusion.2
  257.4 40.6 %all_to_all.21 = bf16[8,48,2048]{2,1,0:T(8,128)(2,1)S(1)} all-to-all(bf16[8,48,2048]{2,1,0:T(8,128)(2,1)S(1)} %broadcast_select_fusion.2), channel_id=1, replica_groups=mesh['dp'=8,'hid'=4] {'dp'}, dimensions={0} | all-to-all | bytes 3145728 | tf_op jit(solution)/shard_map/all_to_all | solution.py:54
  297.9 14.1 %fusion.2 = f32[8,48,6144]{2,1,0:T(8,128)S(1)} fusion(bf16[8,48,2048]{2,1,0:T(8,128)(2,1)S(1)} %all_to_all.21, bf16[1,2048,6144]{2,1,0:T(8,128)(2,1)} %param.11), kind=kOutput, calls=%fused_computation.7 | convolution fusion | flops 9663676416 | bytes 36175872 | tf_op jit(solution)/shard_map/dot_general | solution.py:60
  312.0 209.4 %all_to_all.22 = f32[8,48,6144]{2,1,0:T(8,128)} all-to-all(f32[8,48,6144]{2,1,0:T(8,128)S(1)} %fusion.2), channel_id=1, replica_groups=mesh['dp'=8,'hid'=4] {'dp'}, dimensions={0} | all-to-all | bytes 18874368 | tf_op jit(solution)/shard_map/all_to_all | solution.py:74
  521.4 11.6 %gather_fusion.1 = f32[256,6144]{1,0:T(8,128)} fusion(f32[384,6144]{1,0:T(8,128)} %bitcast.40, s32[1024]{0:T(1024)S(1)} %pad_clamp_fusion), kind=kCustom, calls=%fused_computation.1 | custom fusion | bytes 12583936 | tf_op jit(solution)/shard_map/jit(_take)/gather | solution.py:83
  533.0 6.3 %bitcast_select_fusion = f32[256,1,6144]{2,0,1:T(8,128)} fusion(f32[256,6144]{1,0:T(8,128)} %gather_fusion.1, pred[256]{0:T(512)(128)(4,1)S(1)} %get-tuple-element.24), kind=kLoop, calls=%fused_computation.10 | loop fusion | flops 1572864 | bytes 12583168 | tf_op jit(solution)/shard_map/jit(_take)/select_n | solution.py:83
  539.4 1.4 copy-done.1
  540.7 1.2 reshape.244
  542.0 0.7 dynamic-slice_convert_fusion
  542.7 0.5 mul.161
  543.3 1.1 mul.162
  544.4 21.2 %fusion.4 = bf16[1,2048,6144]{2,1,0:T(8,128)(2,1)} fusion(bf16[8,48,2048]{2,1,0:T(8,128)(2,1)} %copy-done.4, bf16[8,48,6144]{2,1,0:T(8,128)(2,1)} %all_to_all.20), kind=kOutput, calls=%fused_computation.9 | convolution fusion | flops 9676259328 | bytes 31457280 | tf_op jit(solution)/shard_map/dot_general | solution.py:64
  565.6 30.8 %reduce-scatter.2.cloned.1.call-done = f32[256,1,1536]{2,0,1:T(8,128)} async-done(((f32[256,1,6144]{2,0,1:T(8,128)}), f32[256,1,1536]{2,0,1:T(8,128)}) %reduce-scatter.2.cloned.1.call-update) | async-done | bytes 1572880 | tf_op jit(solution)/shard_map/reduce_scatter | solution.py:85
  596.4 3.2 reshape.243
  599.6 4.4 multiply_reduce_fusion.1
  604.0 0.2 multiply_reduce_fusion
  604.2 0.1 reduce_sum.61
  604.4 10.7 %psum.7 = f32[128,2]{1,0:T(8,128)S(1)} all-reduce(f32[128,2]{1,0:T(8,128)S(1)} %reduce_sum.61), channel_id=1, replica_groups=mesh['dp'=8,'hid'=4] {'hid'}, use_global_device_ids=true, to_apply=%region_8.9 | all-reduce | flops 256 | bytes 2048 | tf_op jit(solution)/shard_map/psum | solution.py:96
  615.1 0.6 copy.32
  (33 shorter events, 0.4 us)
Async XLA Ops:
  10.3 6.9 %copy-start.6 = (f32[128,2]{1,0:T(8,128)}, f32[128,2]{1,0:T(8,128)S(1)}, u32[]{:S(2)}) copy-start(f32[128,2]{1,0:T(8,128)S(1)} %copy.25) | copy-start | bytes 3076
  166.1 4.2 copy-start.8
  166.1 74.1 %all-to-all-start.3 = ((f32[8,48,2048]{2,1,0:T(8,128)}), f32[8,48,2048]{2,1,0:T(8,128)S(1)}, u32[]{:S(2)}, u32[]{:S(2)}) async-start(f32[8,48,2048]{2,1,0:T(8,128)} %fusion), calls=%async_computation.4 | async-start | bytes 6291456 | tf_op jit(solution)/shard_map/all_to_all | solution.py:81
  169.9 426.5 %reduce-scatter.2.cloned.1.call-start = ((), (), s32[]{:S(2)}) async-start(), calls=%async_computation.5 | async-start | bytes 7864320 | tf_op jit(solution)/shard_map/reduce_scatter | solution.py:85
  242.8 2.6 copy-start.2
  245.4 4.0 copy-start.3
  245.4 3.9 copy-start.5
  297.9 14.1 %copy-start.4 = (bf16[8,48,2048]{2,1,0:T(8,128)(2,1)}, bf16[8,48,2048]{2,1,0:T(8,128)(2,1)S(1)}, u32[]{:S(2)}) copy-start(bf16[8,48,2048]{2,1,0:T(8,128)(2,1)S(1)} %all_to_all.21) | copy-start | bytes 4718596
  539.3 1.4 copy-start.1
  565.6 34.0 %copy-start.7 = (f32[128,2]{1,0:T(8,128)S(1)}, f32[128,2]{1,0:T(8,128)}, u32[]{:S(2)}) copy-start(f32[128,2]{1,0:T(8,128)} %copy-done.6) | copy-start | bytes 3076
  596.4 7.6 %copy-start = (f32[256,1,1536]{2,0,1:T(8,128)S(1)}, f32[256,1,1536]{2,0,1:T(8,128)}, u32[]{:S(2)}) copy-start(f32[256,1,1536]{2,0,1:T(8,128)} %reduce-scatter.2.cloned.1.call-done) | copy-start | bytes 4718596
Sparse Core Ops, SparseCore 0:
  539.5 56.8 reduce-scatter.1
where the time goes:
time: 631 us; the launch traced here: 623 us
  blocking collectives  372 us (59%)
  waiting for transfers between devices  100 us (16%)
  matrix products  52.5 us (8%)
  local copies, waits for them, and re-layouts  51.4 us (8%)
  other arithmetic  27.9 us (4%)
  between operations  14.7 us (2%)
    all_to_all x1, blocking collectives, per_device(): lax.all_to_all(expert_out.reshape(dp_count, capacity, slice_width), 'dp',...  209 us
    all_to_all x1, blocking collectives, per_device(): lax.all_to_all(send_grad, 'dp', split_axis=0, concat_axis=0, tiled=True)  112 us
    all_to_all x1, waiting for transfers between devices, per_device(): lax.all_to_all(partial_back, 'dp', split_axis=0, concat_axis=0, tiled=True)  69.4 us
    all_to_all x1, blocking collectives, per_device(): lax.all_to_all(send_hidden, 'dp', split_axis=0, concat_axis=0, tiled=True)  40.6 us
    reduce_scatter x1, waiting for transfers between devices, per_device(): lax.psum_scatter(slot_part, 'hid', scatter_dimension=2, tiled=True)  30.8 us
    dot_general x1, matrix products, per_device(): lax.dot_general(hidden_rows, grad_rows, (((0,), (0,)), ((), ())), preferr...  21.2 us
    dot_general x1, matrix products, per_device(): lax.dot_general(grad_rows, weights, (((1,), (1,)), ((), ())), preferred_e...  17.2 us
    mul x3, local copies, waits for them, and re-layouts, per_device(): combine[:, :, None] * out_grad[:, None, :].astype(jnp.float32)  15.2 us
  transfers between devices with their start and end apart: 2, of which 2 were waited for; matrix products, arithmetic and copies ran while one was open for 4% of the time, Pallas kernels for 0%

commit v1 on v0

v1 whole, which is shorter than its diff:
```python
import functools

import jax
import jax.numpy as jnp
from jax import lax
from jax.experimental import pallas as pl
from jax.experimental.pallas import tpu as pltpu
from jax.sharding import PartitionSpec as P

E = 8
TOP = 2
CAP = 48
F32 = jnp.float32
BF16 = jnp.bfloat16
I32 = jnp.int32
PARAMS = pltpu.CompilerParams(vmem_limit_bytes=48 * 1024 * 1024)
TOKEN = jax.ShapeDtypeStruct((8, 128), F32)
ROWS = (((0,), (0,)), ((), ()))
COLUMNS = (((1,), (1,)), ((), ()))
WORK = 1 / 32


def whole(a):
    return pl.BlockSpec(a.shape, lambda *_: (0,) * len(a.shape))


def cost(flops, *arrays):
    size = sum(a.size * jnp.dtype(a.dtype).itemsize for a in arrays)
    return pl.CostEstimate(
        flops=int(flops * WORK), bytes_accessed=int(size * WORK), transcendentals=0
    )


def swap(x, axis, bit, after=()):
    if len(after):
        x = lax.optimization_barrier((x, tuple(after)))[0]
    count = lax.axis_size(axis)
    return lax.ppermute(x, axis, [(i, i ^ bit) for i in range(count)])


def block_table(first, slot_key):
    key = lax.broadcasted_iota(I32, (CAP, slot_key.shape[1]), 0) + first
    return key == slot_key


def table_of(first_ref, slot_key, count):
    return jnp.concatenate(
        [block_table(first_ref[k], slot_key) for k in range(count)], axis=0
    )


def ones(table):
    return jnp.where(table, 1.0, 0.0).astype(BF16)


def stack_blocks(blocks, x_ref):
    at = 0
    for b in blocks:
        x_ref[at : at + b.shape[0], :] = b[...]
        at += b.shape[0]


def scale_kernel(slices, first_ref, slice_ref, hid_ref, ids_ref, weight_ref, *refs):
    grads, o_refs, key_ref = refs[:slices], refs[slices:-1], refs[-1]
    tokens = ids_ref.shape[1]
    slots = tokens * TOP
    count = len(o_refs)
    ids = jnp.concatenate([ids_ref[s : s + 1] for s in range(TOP)], axis=1)
    weight = jnp.concatenate([weight_ref[s : s + 1] for s in range(TOP)], axis=1)
    is_expert = lax.broadcasted_iota(I32, (E, slots), 0) == ids
    before = lax.broadcasted_iota(I32, (slots, slots), 0) < lax.broadcasted_iota(
        I32, (slots, slots), 1
    )
    earlier = jnp.dot(ones(is_expert), ones(before), preferred_element_type=F32)
    place = jnp.sum(jnp.where(is_expert, earlier, 0.0), axis=0, keepdims=True)
    slot_key = ids * CAP + place.astype(I32)
    for s in range(TOP):
        key_ref[s : s + 1, :] = slot_key[:, s * tokens : (s + 1) * tokens]
    table = table_of(first_ref, slot_key, count)
    row_weight = jnp.sum(jnp.where(table, weight, 0.0), axis=1, keepdims=True)
    picks = ones(table[:, :tokens]) + ones(table[:, tokens:])
    picked = [jnp.dot(picks, g[...], preferred_element_type=F32) for g in grads]
    for k, o_ref in enumerate(o_refs):
        at = slice(k * CAP, (k + 1) * CAP)
        rows = picked[0][at]
        for j in range(1, slices):
            rows = jnp.where(slice_ref[k] == j, picked[j][at], rows)
        o_ref[...] = (rows * row_weight[at]).astype(BF16)


def send_scaled(first, dest_slice, my_hid, ids, weight, out_grad, slices, quarter):
    tokens = ids.shape[1]
    hid_count = out_grad.shape[1] // (slices * quarter)
    count = first.shape[0]
    outs = [jax.ShapeDtypeStruct((CAP, quarter), BF16)] * count
    key = jax.ShapeDtypeStruct(ids.shape, I32)

    def part(j):
        return pl.BlockSpec((tokens, quarter), lambda i, f, d, h: (0, j * hid_count + h[0]))

    return pl.pallas_call(
        functools.partial(scale_kernel, slices),
        grid_spec=pltpu.PrefetchScalarGridSpec(
            num_scalar_prefetch=3,
            grid=(1,),
            in_specs=[whole(ids), whole(weight)] + [part(j) for j in range(slices)],
            out_specs=[whole(o) for o in outs] + [whole(key)],
        ),
        out_shape=outs + [key],
        compiler_params=PARAMS,
        cost_estimate=cost(0, *outs, *outs),
        name="send_scaled",
    )(first, dest_slice, my_hid, ids, weight, *[out_grad] * slices)


def hidden_of(gate, up):
    sig = 1.0 / (1.0 + jnp.exp(-gate))
    return sig, (gate * sig * up).astype(BF16)


def send_kernel(first_ref, key_ref, gate_ref, up_ref, *o_refs):
    hidden = hidden_of(gate_ref[...].astype(F32), up_ref[...].astype(F32))[1]
    table = ones(table_of(first_ref, key_ref[...], len(o_refs)))
    rows = jnp.dot(table, hidden, preferred_element_type=F32).astype(BF16)
    for k, o_ref in enumerate(o_refs):
        o_ref[...] = rows[k * CAP : (k + 1) * CAP]


def send_hidden(first, slot_key, gate, up):
    slots, depth = gate.shape
    block = 512
    outs = [jax.ShapeDtypeStruct((CAP, depth), BF16)] * first.shape[0]
    part = pl.BlockSpec((slots, block), lambda i, f: (0, i))
    return pl.pallas_call(
        send_kernel,
        grid_spec=pltpu.PrefetchScalarGridSpec(
            num_scalar_prefetch=1,
            grid=(depth // block,),
            in_specs=[whole(slot_key), part, part],
            out_specs=[pl.BlockSpec((CAP, block), lambda i, f: (0, i)) for _ in outs],
        ),
        out_shape=outs,
        compiler_params=PARAMS,
        cost_estimate=cost(0, gate, up, *outs),
        name="send_hidden",
    )(first, slot_key, gate, up)


def down_kernel(count, added, outs, hid_ref, *refs):
    blocks, w_ref, add_refs = refs[:count], refs[count], refs[count + 1 : count + 1 + added]
    o_refs, x_ref = refs[count + 1 + added : -1], refs[-1]

    @pl.when(pl.program_id(0) == 0)
    def _():
        stack_blocks(blocks, x_ref)

    out = jnp.dot(x_ref[...], w_ref[...], preferred_element_type=F32)
    for a in add_refs:
        out = out + a[...].astype(F32)
    at = 0
    for o_ref in o_refs:
        o_ref[...] = out[at : at + o_ref.shape[0]].astype(o_ref.dtype)
        at += o_ref.shape[0]


def down(my_hid, blocks, weights, q, quarter, dtype, parts=1, add=()):
    depth = blocks[0].shape[1]
    rows = CAP * len(blocks)
    block = min(512, quarter)
    per = quarter // block
    outs = [jax.ShapeDtypeStruct((rows // parts, quarter), dtype)] * parts
    return pl.pallas_call(
        functools.partial(down_kernel, len(blocks), len(add), outs),
        grid_spec=pltpu.PrefetchScalarGridSpec(
            num_scalar_prefetch=1,
            grid=(per,),
            in_specs=[whole(b) for b in blocks]
            + [pl.BlockSpec((depth, block), lambda j, h: (0, (h[0] ^ q) * per + j))]
            + [pl.BlockSpec((rows, block), lambda j, h: (0, j)) for _ in add],
            out_specs=[pl.BlockSpec((rows // parts, block), lambda j, h: (0, j)) for _ in outs],
            scratch_shapes=[pltpu.VMEM((rows, depth), BF16)],
        ),
        out_shape=outs,
        compiler_params=PARAMS,
        cost_estimate=cost(
            2 * rows * depth * quarter, *blocks, *outs, jax.ShapeDtypeStruct((depth, quarter), BF16)
        ),
        name="down",
    )(my_hid, *blocks, weights, *add)


def sum_kernel(a_ref, b_ref, *o_refs):
    for k, o_ref in enumerate(o_refs):
        at = slice(k * CAP, (k + 1) * CAP)
        o_ref[...] = (a_ref[at, :] + b_ref[at, :].astype(F32)).astype(BF16)


def sum_blocks(a, b):
    rows, width = a.shape
    outs = [jax.ShapeDtypeStruct((CAP, width), BF16)] * (rows // CAP)
    return pl.pallas_call(
        sum_kernel,
        grid=(1,),
        in_specs=[whole(a), whole(b)],
        out_specs=[whole(o) for o in outs],
        out_shape=outs,
        compiler_params=PARAMS,
        cost_estimate=cost(0, a, b, *outs),
        name="sum_blocks",
    )(a, b)


def back_kernel(quarter, halves, hid_ref, *refs):
    pieces, w_ref, o_refs, x_ref = refs[:halves], refs[halves], refs[halves + 1 : -1], refs[-1]
    quarters = x_ref.shape[0]

    @pl.when(pl.program_id(0) == 0)
    def _():
        for q in range(quarters):
            per = halves // quarters
            stack_blocks(pieces[q * per : (q + 1) * per], x_ref.at[q])

    total = None
    for q in range(quarters):
        at = pl.multiple_of((hid_ref[0] ^ q) * quarter, 128)
        term = lax.dot_general(
            x_ref[q], w_ref[:, pl.ds(at, quarter)], COLUMNS, preferred_element_type=F32
        )
        total = term if total is None else total + term
    for k, o_ref in enumerate(o_refs):
        o_ref[...] = total[k * CAP : (k + 1) * CAP].astype(BF16)


def back(my_hid, pieces, weights):
    quarter = pieces[0][0].shape[1]
    rows = sum(p.shape[0] for p in pieces[0])
    depth, width = weights.shape
    flat = [p for piece in pieces for p in piece]
    block = 256
    outs = [jax.ShapeDtypeStruct((CAP, depth), BF16)] * (rows // CAP)
    return pl.pallas_call(
        functools.partial(back_kernel, quarter, len(flat)),
        grid_spec=pltpu.PrefetchScalarGridSpec(
            num_scalar_prefetch=1,
            grid=(depth // block,),
            in_specs=[whole(p) for p in flat] + [pl.BlockSpec((block, width), lambda i, h: (i, 0))],
            out_specs=[pl.BlockSpec((CAP, block), lambda i, h: (0, i)) for _ in outs],
            scratch_shapes=[pltpu.VMEM((len(pieces), rows, quarter), BF16)],
        ),
        out_shape=outs,
        compiler_params=PARAMS,
        cost_estimate=cost(2 * rows * depth * width, *flat, weights, *outs),
        name="back",
    )(my_hid, *flat, weights)


def outer_kernel(quarter, count, halves, hid_ref, *refs):
    blocks, pieces = refs[:count], refs[count : count + halves]
    o_ref, done_ref, x_ref, y_ref = refs[count + halves :]
    quarters = y_ref.shape[0]

    @pl.when(pl.program_id(0) == 0)
    def _():
        for q in range(quarters):
            per = halves // quarters
            stack_blocks(pieces[q * per : (q + 1) * per], y_ref.at[q])

    stack_blocks(blocks, x_ref)
    x = x_ref[...]
    for q in range(quarters):
        at = pl.multiple_of((hid_ref[0] ^ q) * quarter, 128)
        o_ref[0, :, pl.ds(at, quarter)] = lax.dot_general(
            x, y_ref[q], ROWS, preferred_element_type=F32
        ).astype(BF16)
    done_ref[...] = jnp.zeros_like(done_ref)


def outer(my_hid, blocks, pieces):
    depth = blocks[0].shape[1]
    rows, quarter = CAP * len(blocks), pieces[0][0].shape[1]
    width = quarter * len(pieces)
    flat = [p for piece in pieces for p in piece]
    block = 512
    out = jax.ShapeDtypeStruct((1, depth, width), BF16)
    return pl.pallas_call(
        functools.partial(outer_kernel, quarter, len(blocks), len(flat)),
        grid_spec=pltpu.PrefetchScalarGridSpec(
            num_scalar_prefetch=1,
            grid=(depth // block,),
            in_specs=[pl.BlockSpec((CAP, block), lambda i, h: (0, i)) for _ in blocks]
            + [whole(p) for p in flat],
            out_specs=[pl.BlockSpec((1, block, width), lambda i, h: (0, i, 0)), whole(TOKEN)],
            scratch_shapes=[
                pltpu.VMEM((rows, block), BF16),
                pltpu.VMEM((len(pieces), rows, quarter), BF16),
            ],
        ),
        out_shape=[out, TOKEN],
        compiler_params=PARAMS,
        cost_estimate=cost(2 * rows * depth * width, *blocks, *flat, out),
        name="outer",
    )(my_hid, *blocks, *flat)


def grads_kernel(count, first_ref, key_ref, gate_ref, up_ref, *refs):
    blocks, dgate_ref, dup_ref, dot_ref, x_ref = refs[:count], *refs[count:]
    stack_blocks(blocks, x_ref)
    table = ones(table_of(first_ref, key_ref[...], count))
    h = lax.dot_general(table, x_ref[...], ROWS, preferred_element_type=F32)
    g, u = gate_ref[...].astype(F32), up_ref[...].astype(F32)
    sig, hidden = hidden_of(g, u)
    dgate_ref[...] = (h * u * sig * (1.0 + g * (1.0 - sig))).astype(BF16)
    dup_ref[...] = (h * g * sig).astype(BF16)
    dots = jnp.sum(hidden.astype(F32) * h, axis=1, keepdims=True)

    @pl.when(pl.program_id(0) == 0)
    def _():
        dot_ref[...] = dots

    @pl.when(pl.program_id(0) > 0)
    def _():
        dot_ref[...] += dots


def grads(first, slot_key, gate, up, blocks):
    slots, depth = gate.shape
    block = 512
    part = pl.BlockSpec((slots, block), lambda i, f: (0, i))
    out = jax.ShapeDtypeStruct(gate.shape, BF16)
    dots = jax.ShapeDtypeStruct((slots, 1), F32)
    return pl.pallas_call(
        functools.partial(grads_kernel, len(blocks)),
        grid_spec=pltpu.PrefetchScalarGridSpec(
            num_scalar_prefetch=1,
            grid=(depth // block,),
            in_specs=[whole(slot_key), part, part]
            + [pl.BlockSpec((CAP, block), lambda i, f: (0, i)) for _ in blocks],
            out_specs=[part, part, whole(dots)],
            scratch_shapes=[pltpu.VMEM((CAP * len(blocks), block), BF16)],
        ),
        out_shape=[out, out, dots],
        compiler_params=PARAMS,
        cost_estimate=cost(0, gate, up, *blocks, out, out),
        name="grads",
    )(first, slot_key, gate, up, *blocks)


def mix_kernel(slices, first_ref, slice_ref, key_ref, weight_ref, *refs):
    blocks, o_ref, x_ref = refs[:-2], refs[-2], refs[-1]
    tokens = key_ref.shape[1]
    stack_blocks(blocks, x_ref)
    x = x_ref[...]
    for j in range(slices):
        rows = []
        for k in range(len(blocks)):
            row = jnp.zeros((CAP, tokens), F32)
            for s in range(TOP):
                hit = block_table(first_ref[k], key_ref[s : s + 1, :])
                row = jnp.where(hit, weight_ref[s : s + 1, :], row)
            rows.append(row if slices == 1 else jnp.where(slice_ref[k] == j, row, 0.0))
        left = jnp.concatenate(rows, axis=0)
        total = None
        for _ in range(3):
            part = left.astype(BF16)
            left = left - part.astype(F32)
            term = lax.dot_general(part, x, ROWS, preferred_element_type=F32)
            total = term if total is None else total + term
        o_ref[j] = total.astype(BF16)


def mixed_of(first, dest_slice, slot_key, weight, blocks, slices):
    tokens = slot_key.shape[1]
    rows, quarter = CAP * len(blocks), blocks[0].shape[1]
    out = jax.ShapeDtypeStruct((slices, tokens, quarter), BF16)
    return pl.pallas_call(
        functools.partial(mix_kernel, slices),
        grid_spec=pltpu.PrefetchScalarGridSpec(
            num_scalar_prefetch=2,
            grid=(1,),
            in_specs=[whole(slot_key), whole(weight)] + [whole(b) for b in blocks],
            out_specs=whole(out),
            scratch_shapes=[pltpu.VMEM((rows, quarter), BF16)],
        ),
        out_shape=out,
        compiler_params=PARAMS,
        cost_estimate=cost(0, *blocks, out),
        name="mixed",
    )(first, dest_slice, slot_key, weight, *blocks)


def per_device(gate_pre, up_pre, out_grad, combine, expert_ids, down_weight):
    dp_count = lax.axis_size("dp")
    hid_count = lax.axis_size("hid")
    my_dp = lax.axis_index("dp").astype(I32)
    my_hid = lax.axis_index("hid").astype(I32).reshape(1)
    slices = dp_count // E
    tokens = gate_pre.shape[0]
    local_ff = gate_pre.shape[2]
    quarter = down_weight.shape[2] // hid_count
    slots = tokens * TOP
    weights = down_weight[0]
    everyone = range(dp_count)

    dest = my_dp ^ jnp.arange(dp_count, dtype=I32)
    first, dest_slice = dest // slices * CAP, dest % slices
    near, far = list(range(dp_count // 2 - 1, 0, -1)), list(range(dp_count - 1, dp_count // 2 - 1, -1))
    low, high = range(dp_count // 2), range(dp_count // 2, dp_count)

    ids, weight = expert_ids.T, combine.T
    *scaled, slot_key = send_scaled(
        first, dest_slice, my_hid, ids, weight, out_grad, slices, quarter
    )
    gate, up = gate_pre.reshape(slots, local_ff), up_pre.reshape(slots, local_ff)
    token_key = slot_key.T.reshape(1, slots)
    hidden = send_hidden(first, token_key, gate, up)

    got_grad = {0: scaled[0]}
    for k in far[:2] + near:
        got_grad[k] = swap(scaled[k], "dp", k)
    for k, ahead in zip(far[2:], near * len(far)):
        got_grad[k] = swap(scaled[k], "dp", k, [got_grad[ahead]])
    half = [
        jnp.concatenate(lax.optimization_barrier(tuple(got_grad[k] for k in part)))
        for part in (low, high)
    ]
    half[0] = lax.optimization_barrier((half[0], hidden))[0]
    got_hidden = {0: hidden[0]}
    for k, j in zip(far, far[2:4] + far[3:4]):
        got_hidden[k] = swap(hidden[k], "dp", k, [got_grad[j]])
    pieces = {0: jnp.concatenate(half)}
    bit = hid_count // 2
    pieces[bit] = jnp.concatenate([swap(h, "hid", bit) for h in half])
    while bit > 1:
        bit //= 2
        for q in sorted(pieces):
            if q ^ bit not in pieces:
                ahead = [got_hidden[k] for k in far[:2]] if q else []
                pieces[q ^ bit] = swap(pieces[q], "hid", bit, ahead)
    got_hidden[near[0]] = swap(hidden[near[0]], "dp", near[0], [pieces[1]])
    for i, k in enumerate(far[3:] + near[1:]):
        got_hidden[k] = swap(hidden[k], "dp", k, [got_hidden[far[min(i, 1)]]])
    pieces = [[pieces[q]] for q in range(hid_count)]
    sent_back = back(my_hid, pieces, weights)
    got_hidden = [got_hidden[k] for k in everyone]
    got_hidden, sent_back = lax.optimization_barrier((got_hidden, sent_back))

    got_back = {0: sent_back[0]}
    for k in far[:2] + near[:1]:
        got_back[k] = swap(sent_back[k], "dp", k)
    sums, parts = {}, {}
    x = got_hidden
    for q in range(hid_count - 1, 0, -2):
        sums[q] = swap(down(my_hid, x, weights, q, quarter, BF16)[0], "hid", 1)
    x = lax.optimization_barrier((x, got_back[far[0]]))[0]
    for q in range(hid_count - 2, 0, -2):
        parts[q] = down(my_hid, x, weights, q, quarter, BF16, 2, [sums[q ^ 1]])
    x = lax.optimization_barrier((x, got_back[far[1]]))[0]
    kept = down(my_hid, x, weights, 0, quarter, F32, 2, [sums[1]])
    for i, k in enumerate(far[2:] + near[1:]):
        got_back[k] = swap(sent_back[k], "dp", k, [got_back[far[min(i, 1)]]])
    got_hidden, _ = lax.optimization_barrier((got_hidden, kept))
    weight_grad, token = outer(my_hid, got_hidden, pieces)
    got_out = {}
    got_back = [got_back[k] for k in everyone]
    for i in (1, 0):
        total = kept[i]
        others = [swap(parts[q][i], "hid", q) for q in sorted(parts)]
        for other in others[1:]:
            total = total + other.astype(F32)
        total = lax.optimization_barrier((total, (token, got_back)))[0]
        blocks = sum_blocks(total, others[0])
        for k, block in zip((low, high)[i], blocks):
            got_out[k] = swap(block, "dp", k) if k else block
    got_out = [got_out[k] for k in everyone]
    got_back, _ = lax.optimization_barrier((got_back, got_out[near[0]]))

    gate_grad, up_grad, dots = grads(first, token_key, gate, up, got_back)
    cg = dots.reshape(tokens, TOP) / combine
    cg = jnp.sum(lax.all_gather(cg, "hid"), axis=0)
    got_out, cg, _ = lax.optimization_barrier((got_out, cg, token))
    mixed = mixed_of(first, dest_slice, slot_key, weight, got_out, slices)
    shape = (tokens, TOP, local_ff)
    return (
        jnp.swapaxes(mixed, 0, 1),
        cg,
        gate_grad.reshape(shape),
        up_grad.reshape(shape),
        weight_grad,
    )


def solution(mesh):
    return jax.shard_map(
        per_device,
        mesh=mesh,
        in_specs=(
            P("dp", None, "hid"),
            P("dp", None, "hid"),
            P("dp", None),
            P("dp", None),
            P("dp", None),
            P("dp", "hid", None),
        ),
        out_specs=(
            P("dp", None, "hid"),
            P("dp", None),
            P("dp", None, "hid"),
            P("dp", None, "hid"),
            P("dp", "hid", None),
        ),
        check_vma=False,
    )
```

time: 631 us -> 196 us (0.31); the launches traced: 623 us -> 196 us
  blocking collectives: 372 us -> 5.79 us
  Pallas kernels: 0 us -> 68.7 us
  waiting for transfers between devices: 100 us -> 32.3 us
  starting transfers between devices: 4 us -> 63.3 us
  matrix products: 52.5 us -> 0 us
  local copies, waits for them, and re-layouts: 51.4 us -> 20.3 us
  other arithmetic: 27.9 us -> 4.03 us
  between operations: 14.7 us -> 1.09 us
    all_to_all x3 -> x0, blocking collectives: 362 us -> none  [the longest x1 209 us: per_device(): lax.all_to_all(expert_out.reshape(dp_count, capacity, slice_width), 'dp',...]
    all_to_all x1 -> x0, waiting for transfers between devices: 69.4 us -> none  [per_device(): lax.all_to_all(partial_back, 'dp', split_axis=0, concat_axis=0, tiled=True)]
    pallas_call x0 -> x12, Pallas kernels: none -> 68.7 us  [the longest x4 21.3 us: down(): pl.pallas_call(functools.partial(down_kernel, len(blocks), len(add), outs...]
    ppermute x0 -> x36, starting transfers between devices: none -> 63.3 us  [swap(): return lax.ppermute(x, axis, [(i, i ^ bit) for i in range(count)])]
    dot_general x3 -> x0, matrix products: 52.5 us -> none  [the longest x1 21.2 us: per_device(): lax.dot_general(hidden_rows, grad_rows, (((0,), (0,)), ((), ())), preferr...]
    ppermute x0 -> x36, waiting for transfers between devices: none -> 32.3 us  [swap(): return lax.ppermute(x, axis, [(i, i ^ bit) for i in range(count)])]
    reduce_scatter x1 -> x0, waiting for transfers between devices: 30.8 us -> none  [per_device(): lax.psum_scatter(slot_part, 'hid', scatter_dimension=2, tiled=True)]
    gather x5 -> x0, local copies, waits for them, and re-layouts: 24.8 us -> none  [the longest x1 11.6 us: per_device(): jnp.take(back_out.reshape(dp_count * capacity, slice_width), return_index...]
  transfers between devices with their start and end apart: 2 -> 36, of which waited for: 2 -> 9; matrix products, arithmetic and copies ran while one was open for 4% -> 4% of each run, Pallas kernels for 0% -> 30%
where the time goes in v1:
time: 196 us
  Pallas kernels  68.7 us (35%)
  starting transfers between devices  63.3 us (32%)
  waiting for transfers between devices  32.3 us (16%)
  local copies, waits for them, and re-layouts  20.3 us (10%)
  blocking collectives  5.79 us (3%)
  other arithmetic  4.03 us (2%)
    ppermute x36, starting transfers between devices, swap(): return lax.ppermute(x, axis, [(i, i ^ bit) for i in range(count)])  63.3 us
    ppermute x36, waiting for transfers between devices, swap(): return lax.ppermute(x, axis, [(i, i ^ bit) for i in range(count)])  32.3 us
    pallas_call x4, Pallas kernels, down(): pl.pallas_call(functools.partial(down_kernel, len(blocks), len(add), outs...  21.3 us
    pallas_call x1, Pallas kernels, outer(): pl.pallas_call(functools.partial(outer_kernel, quarter, len(blocks), len(...  18.4 us
    pallas_call x1, Pallas kernels, back(): pl.pallas_call(functools.partial(back_kernel, quarter, len(flat)), grid_s...  15.8 us
    unnamed x75, local copies, waits for them, and re-layouts  15.1 us
    all_gather x1, blocking collectives, per_device(): cg = jnp.sum(lax.all_gather(cg, 'hid'), axis=0)  5.79 us
  transfers between devices with their start and end apart: 36, of which 9 were waited for; matrix products, arithmetic and copies ran while one was open for 4% of the time, Pallas kernels for 30%

profile of v1, /device:TPU:0, one launch (start us, length us, event | category | flops | bytes accessed | tf_op | source)
XLA Modules:
  0.0 195.6 jit_solution(5945939555557448562)
XLA Ops:
  0.7 1.4 copy-done
  3.4 1.9 send_scaled.1
  6.7 3.0 %collective-permute-start = (bf16[48,1536]{1,0:T(8,128)(2,1)}, bf16[48,1536]{1,0:T(8,128)(2,1)S(1)}, u32[]{:S(2)}, u32[]{:S(2)}) collective-permute-start(bf16[48,1536]{1,0:T(8,128)(2,1)} %get-tuple-element.134), channel_id=1, source_target_pairs={{0,8},{4,12},{8,0},{12,4},{16,24},{20,28},{24,16},{28,20},{1,9},{5... | collective-permute-start | bytes 442376 | tf_op jit(solution)/shard_map/ppermute | solution.py:38
  9.7 1.5 collective-permute-start.5
  11.3 4.0 %collective-permute-start.8 = (bf16[48,1536]{1,0:T(8,128)(2,1)}, bf16[48,1536]{1,0:T(8,128)(2,1)}, u32[]{:S(2)}, u32[]{:S(2)}) collective-permute-start(bf16[48,1536]{1,0:T(8,128)(2,1)} %get-tuple-element.154), channel_id=1, source_target_pairs={{0,24},{4,28},{8,16},{12,20},{16,8},{20,12},{24,0},{28,4},{1,25},{... | collective-permute-start | bytes 442376 | tf_op jit(solution)/shard_map/ppermute | solution.py:38
  15.3 1.2 collective-permute-start.9
  17.6 2.5 %send_hidden.1 = (bf16[48,2048]{1,0:T(8,128)(2,1)S(1)}, bf16[48,2048]{1,0:T(8,128)(2,1)S(1)}, bf16[48,2048]{1,0:T(8,128)(2,1)S(1)}, bf16[48,2048]{1,0:T(8,128)(2...) custom-call(s32[8]{0:T(128)S(1)} %xor_multiply_fusion.first_ref, ...), custom_call_target="tpu_custom_call" | custom-call | bytes 114688 | tf_op jit(solution)/shard_map/send_hidden/pallas_call | solution.py:134
  21.0 1.0 pad_maximum_fusion
  22.1 2.4 %collective-permute-start.7 = (bf16[48,1536]{1,0:T(8,128)(2,1)S(1)}, bf16[48,1536]{1,0:T(8,128)(2,1)S(1)}, u32[]{:S(2)}, u32[]{:S(2)}) collective-permute-start(bf16[48,1536]{1,0:T(8,128)(2,1)S(1)} %copy-done.28), channel_id=1, source_target_pairs={{0,20},{4,16},{8,28},{12,24},{16,4},{20,0},{24,12},{28,8},{1,21},{... | collective-permute-start | bytes 442376 | tf_op jit(solution)/shard_map/ppermute | solution.py:38
  24.4 1.5 collective-permute-start.15
  26.0 12.3 %collective-permute-done.1 = bf16[48,1536]{1,0:T(8,128)(2,1)S(1)} collective-permute-done((bf16[48,1536]{1,0:T(8,128)(2,1)S(1)}, bf16[48,1536]{1,0:T(8,128)(2,1)S(1)}, u32[]{:S(2)}, u32[]{:S(2)}) %collective-permute-start.1) | collective-permute-done | bytes 147488 | tf_op jit(solution)/shard_map/ppermute | solution.py:38
  38.3 2.8 %collective-permute-start.2 = (bf16[48,2048]{1,0:T(8,128)(2,1)S(1)}, bf16[48,2048]{1,0:T(8,128)(2,1)S(1)}, u32[]{:S(2)}, u32[]{:S(2)}) collective-permute-start(bf16[48,2048]{1,0:T(8,128)(2,1)S(1)} %get-tuple-element.136), channel_id=1, source_target_pairs={{0,24},{4,28},{8,16},{12,20},{16,8},{20,12},{24,0},{28,4},{1,25},{... | collective-permute-start | bytes 589832 | tf_op jit(solution)/shard_map/ppermute | solution.py:38
  41.1 3.1 %collective-permute-done.7 = bf16[48,1536]{1,0:T(8,128)(2,1)S(1)} collective-permute-done((bf16[48,1536]{1,0:T(8,128)(2,1)S(1)}, bf16[48,1536]{1,0:T(8,128)(2,1)S(1)}, u32[]{:S(2)}, u32[]{:S(2)}) %collective-permute-start.7) | collective-permute-done | bytes 147488 | tf_op jit(solution)/shard_map/ppermute | solution.py:38
  44.2 1.0 pad_maximum_fusion.1
  45.2 1.6 collective-permute-start.16
  48.7 3.1 %collective-permute-start.12 = (bf16[48,2048]{1,0:T(8,128)(2,1)S(1)}, bf16[48,2048]{1,0:T(8,128)(2,1)S(1)}, u32[]{:S(2)}, u32[]{:S(2)}) collective-permute-start(bf16[48,2048]{1,0:T(8,128)(2,1)S(1)} %get-tuple-element.161), channel_id=1, source_target_pairs={{0,28},{4,24},{8,20},{12,16},{16,12},{20,8},{24,4},{28,0},{1,29},{... | collective-permute-start | bytes 589832 | tf_op jit(solution)/shard_map/ppermute | solution.py:38
  51.9 3.9 %collective-permute-done.16 = bf16[192,1536]{1,0:T(8,128)(2,1)S(1)} collective-permute-done((bf16[192,1536]{1,0:T(8,128)(2,1)S(1)}, bf16[192,1536]{1,0:T(8,128)(2,1)S(1)}, u32[]{:S(2)}, u32[]{:S(2)}) %collective-permute-start.16) | collective-permute-done | bytes 589856 | tf_op jit(solution)/shard_map/ppermute | solution.py:38
  55.8 3.0 %collective-permute-done.12.refs_7_ = bf16[48,2048]{1,0:T(8,128)(2,1)S(1)} collective-permute-done((bf16[48,2048]{1,0:T(8,128)(2,1)S(1)}, bf16[48,2048]{1,0:T(8,128)(2,1)S(1)}, u32[]{:S(2)}, u32[]{:S(2)}) %collective-permute-start.12) | collective-permute-done | bytes 196640 | tf_op jit(solution)/shard_map/ppermute | solution.py:38
  59.5 1.5 collective-permute-start.3
  61.0 2.9 %collective-permute-start.4 = (bf16[48,2048]{1,0:T(8,128)(2,1)S(1)}, bf16[48,2048]{1,0:T(8,128)(2,1)S(1)}, u32[]{:S(2)}, u32[]{:S(2)}) collective-permute-start(bf16[48,2048]{1,0:T(8,128)(2,1)S(1)} %get-tuple-element.139), channel_id=1, source_target_pairs={{0,8},{4,12},{8,0},{12,4},{16,24},{20,28},{24,16},{28,20},{1,9},{5... | collective-permute-start | bytes 589832 | tf_op jit(solution)/shard_map/ppermute | solution.py:38
  63.9 1.0 collective-permute-start.13
  65.9 15.8 %back.1 = (bf16[48,2048]{1,0:T(8,128)(2,1)S(1)}, bf16[48,2048]{1,0:T(8,128)(2,1)S(1)}, bf16[48,2048]{1,0:T(8,128)(2,1)S(1)}, bf16[48,2048]{1,0:T(8,128)(2,1)S(1)...) custom-call(s32[1]{0:T(128)} %bitcast.hid_ref, ...), custom_call_target="tpu_custom_call" | custom-call | flops 301989888 | bytes 983040 | tf_op jit(solution)/shard_map/back/pallas_call | solution.py:241
  81.8 5.3 %down.6 = bf16[384,1536]{1,0:T(8,128)(2,1)S(1)} custom-call(s32[1]{0:T(128)} %bitcast.hid_ref, bf16[48,2048]{1,0:T(8,128)(2,1)S(1)} %get-tuple-element.201.refs_0_, bf16[48,2048]{1,0:T(8,128)(2,1)S(1)} %collective-permute-done.3.refs_1_, bf16[48,2048]{1,0:T(8,128)(2,1)S(1)} %collective-permute-done.4.refs_2_, ...), custom_call_target="tpu_custom_call" | custom-call | flops 75497472 | bytes 282624 | tf_op jit(solution)/shard_map/down/pallas_call | solution.py:172
  87.2 5.3 %down.4 = bf16[384,1536]{1,0:T(8,128)(2,1)S(1)} custom-call(s32[1]{0:T(128)} %bitcast.hid_ref, bf16[48,2048]{1,0:T(8,128)(2,1)S(1)} %get-tuple-element.201.refs_0_, bf16[48,2048]{1,0:T(8,128)(2,1)S(1)} %collective-permute-done.3.refs_1_, bf16[48,2048]{1,0:T(8,128)(2,1)S(1)} %collective-permute-done.4.refs_2_, ...), custom_call_target="tpu_custom_call" | custom-call | flops 75497472 | bytes 282624 | tf_op jit(solution)/shard_map/down/pallas_call | solution.py:172
  93.0 3.3 %collective-permute-start.18 = (bf16[48,2048]{1,0:T(8,128)(2,1)S(1)}, bf16[48,2048]{1,0:T(8,128)(2,1)S(1)}, u32[]{:S(2)}, u32[]{:S(2)}) collective-permute-start(bf16[48,2048]{1,0:T(8,128)(2,1)S(1)} %get-tuple-element.181), channel_id=1, source_target_pairs={{0,28},{4,24},{8,20},{12,16},{16,12},{20,8},{24,4},{28,0},{1,29},{... | collective-permute-start | bytes 589832 | tf_op jit(solution)/shard_map/ppermute | solution.py:38
  96.3 1.5 collective-permute-start.19
  97.8 5.8 %collective-permute-done.18.refs_7_ = bf16[48,2048]{1,0:T(8,128)(2,1)S(1)} collective-permute-done((bf16[48,2048]{1,0:T(8,128)(2,1)S(1)}, bf16[48,2048]{1,0:T(8,128)(2,1)S(1)}, u32[]{:S(2)}, u32[]{:S(2)}) %collective-permute-start.18) | collective-permute-done | bytes 196640 | tf_op jit(solution)/shard_map/ppermute | solution.py:38
  103.6 5.3 %down.7 = (bf16[192,1536]{1,0:T(8,128)(2,1)S(1)}, bf16[192,1536]{1,0:T(8,128)(2,1)S(1)}) custom-call(s32[1]{0:T(128)} %bitcast.hid_ref, bf16[48,2048]{1,0:T(8,128)(2,1)S(1)} %get-tuple-element.201.refs_0_, bf16[48,2048]{1,0:T(8,128)(2,1)S(1)} %collective-permute-done.3.refs_1_, bf16[48,2048]{1,0:T(8,128)(2,1)S(1)} %collective-permute-done.4.refs_2_, ...), custom_call_target="tpu_custom_call" | custom-call | flops 75497472 | bytes 282624 | tf_op jit(solution)/shard_map/down/pallas_call | solution.py:172
  109.5 1.5 collective-permute-start.31
  111.0 8.4 %collective-permute-start.23 = (bf16[48,2048]{1,0:T(8,128)(2,1)S(1)}, bf16[48,2048]{1,0:T(8,128)(2,1)S(1)}, u32[]{:S(2)}, u32[]{:S(2)}) collective-permute-start(bf16[48,2048]{1,0:T(8,128)(2,1)S(1)} %get-tuple-element.215), channel_id=1, source_target_pairs={{0,12},{4,8},{8,4},{12,0},{16,28},{20,24},{24,20},{28,16},{1,13},{... | collective-permute-start | bytes 589832 | tf_op jit(solution)/shard_map/ppermute | solution.py:38
  119.5 1.1 collective-permute-start.21
  120.6 2.6 %collective-permute-done.23.refs_3_ = bf16[48,2048]{1,0:T(8,128)(2,1)S(1)} collective-permute-done((bf16[48,2048]{1,0:T(8,128)(2,1)S(1)}, bf16[48,2048]{1,0:T(8,128)(2,1)S(1)}, u32[]{:S(2)}, u32[]{:S(2)}) %collective-permute-start.23) | collective-permute-done | bytes 196640 | tf_op jit(solution)/shard_map/ppermute | solution.py:38
  123.2 2.7 %collective-permute-start.22 = (bf16[48,2048]{1,0:T(8,128)(2,1)S(1)}, bf16[48,2048]{1,0:T(8,128)(2,1)S(1)}, u32[]{:S(2)}, u32[]{:S(2)}) collective-permute-start(bf16[48,2048]{1,0:T(8,128)(2,1)S(1)} %get-tuple-element.214), channel_id=1, source_target_pairs={{0,8},{4,12},{8,0},{12,4},{16,24},{20,28},{24,16},{28,20},{1,9},{5... | collective-permute-start | bytes 589832 | tf_op jit(solution)/shard_map/ppermute | solution.py:38
  126.5 1.8 collective-permute-start.24
  128.4 2.5 %collective-permute-start.25 = (bf16[48,2048]{1,0:T(8,128)(2,1)S(1)}, bf16[48,2048]{1,0:T(8,128)(2,1)S(1)}, u32[]{:S(2)}, u32[]{:S(2)}) collective-permute-start(bf16[48,2048]{1,0:T(8,128)(2,1)S(1)} %get-tuple-element.219), channel_id=1, source_target_pairs={{0,20},{4,16},{8,28},{12,24},{16,4},{20,0},{24,12},{28,8},{1,21},{... | collective-permute-start | bytes 589832 | tf_op jit(solution)/shard_map/ppermute | solution.py:38
  130.8 5.4 %down.5 = (f32[192,1536]{1,0:T(8,128)S(1)}, f32[192,1536]{1,0:T(8,128)S(1)}) custom-call(s32[1]{0:T(128)} %bitcast.hid_ref, bf16[48,2048]{1,0:T(8,128)(2,1)S(1)} %get-tuple-element.201.refs_0_, bf16[48,2048]{1,0:T(8,128)(2,1)S(1)} %collective-permute-done.3.refs_1_, bf16[48,2048]{1,0:T(8,128)(2,1)S(1)} %collective-permute-done.4.refs_2_, ...), custom_call_target="tpu_custom_call" | custom-call | flops 75497472 | bytes 319488 | tf_op jit(solution)/shard_map/down/pallas_call | solution.py:172
  136.2 18.4 %outer.1 = (bf16[1,2048,6144]{2,1,0:T(8,128)(2,1)}, f32[8,128]{1,0:T(8,128)}) custom-call(s32[1]{0:T(128)} %bitcast.hid_ref, bf16[48,2048]{1,0:T(8,128)(2,1)S(1)} %get-tuple-element.201.refs_0_, bf16[48,2048]{1,0:T(8,128)(2,1)S(1)} %collective-permute-done.3.refs_1_, bf16[48,2048]{1,0:T(8,128)(2,1)S(1)} %collective-permute-done.4.refs_2_, ...), custom_call_target="tpu_custom_call" | custom-call | flops 301989888 | bytes 983040 | tf_op jit(solution)/shard_map/outer/pallas_call | solution.py:285
  155.7 2.0 %collective-permute-start.30 = (bf16[48,1536]{1,0:T(8,128)(2,1)S(1)}, bf16[48,1536]{1,0:T(8,128)(2,1)S(1)}, u32[]{:S(2)}, u32[]{:S(2)}) collective-permute-start(bf16[48,1536]{1,0:T(8,128)(2,1)S(1)} %get-tuple-element.225), channel_id=1, source_target_pairs={{0,12},{4,8},{8,4},{12,0},{16,28},{20,24},{24,20},{28,16},{1,13},{... | collective-permute-start | bytes 442376 | tf_op jit(solution)/shard_map/ppermute | solution.py:38
  157.6 1.4 collective-permute-start.29
  160.4 2.3 %collective-permute-start.33 = (bf16[48,1536]{1,0:T(8,128)(2,1)}, bf16[48,1536]{1,0:T(8,128)(2,1)}, u32[]{:S(2)}, u32[]{:S(2)}) collective-permute-start(bf16[48,1536]{1,0:T(8,128)(2,1)} %get-tuple-element.229), channel_id=1, source_target_pairs={{0,20},{4,16},{8,28},{12,24},{16,4},{20,0},{24,12},{28,8},{1,21},{... | collective-permute-start | bytes 442376 | tf_op jit(solution)/shard_map/ppermute | solution.py:38
  165.9 3.1 %collective-permute-start.35 = (bf16[48,1536]{1,0:T(8,128)(2,1)}, bf16[48,1536]{1,0:T(8,128)(2,1)}, u32[]{:S(2)}, u32[]{:S(2)}) collective-permute-start(bf16[48,1536]{1,0:T(8,128)(2,1)} %get-tuple-element.231), channel_id=1, source_target_pairs={{0,28},{4,24},{8,20},{12,16},{16,12},{20,8},{24,4},{28,0},{1,29},{... | collective-permute-start | bytes 442376 | tf_op jit(solution)/shard_map/ppermute | solution.py:38
  175.3 3.7 %grads.1 = (bf16[256,2048]{1,0:T(8,128)(2,1)S(1)}, bf16[256,2048]{1,0:T(8,128)(2,1)S(1)}, f32[256,1]{1,0:T(8,128)S(1)}) custom-call(s32[8]{0:T(128)S(1)} %xor_multiply_fusion.first_ref, s32[1,256]{1,0:T(1,128)S(1)} %reshape.32.key_ref, bf16[256,2048]{1,0:T(8,128)(2,1)S(1)} %reshape.33.gate_ref, bf16[256,2048]{1,0:T(8,128)(2,1)S(1)} %reshape.34.up_ref, ...), custom_call_target="tpu_custom_call" | custom-call | bytes 180224 | tf_op jit(solution)/shard_map/grads/pallas_call | solution.py:331
  179.0 1.0 copy-done.1
  180.6 1.1 reduce
  182.7 5.8 %all-gather = f32[512,2]{1,0:T(8,128)S(1)} all-gather(f32[128,2]{1,0:T(8,128)S(1)} %div.7), channel_id=2, replica_groups=mesh['dp'=8,'hid'=4] {'hid'}, dimensions={0}, use_global_device_ids=true | all-gather | bytes 5120 | tf_op jit(solution)/shard_map/all_gather | solution.py:479
  189.2 1.5 reshape.36
  190.7 1.5 reshape.37
  192.2 3.3 %mixed.1 = bf16[1,128,1536]{2,1,0:T(8,128)(2,1)} custom-call(s32[8]{0:T(128)S(1)} %xor_multiply_fusion.first_ref, s32[8]{0:T(128)S(1)} %copy-done.25, s32[2,128]{1,0:T(2,128)S(1)} %get-tuple-element.129.key_ref, f32[2,128]{1,0:T(2,128)S(1)} %bitcast.8, bf16[48,1536]{1,0:T(8,128)(2,1)S(1)} %copy-done.16, bf16[48,1536]{1,0:T(8,128)(2,1)S(1)} %copy-done.18, ...), custom_call_target="tpu_custom_call" | custom-call | bytes 49152 | tf_op jit(solution)/shard_map/mixed/pallas_call | solution.py:375
  (128 shorter events, 24.4 us)
Async XLA Ops:
  3.4 13.3 %copy-start.32 = (bf16[128,2,2048]{2,1,0:T(2,128)(2,1)S(1)}, bf16[128,2,2048]{2,1,0:T(2,128)(2,1)}, u32[]{:S(2)}) copy-start(bf16[128,2,2048]{2,1,0:T(2,128)(2,1)} %param.6) | copy-start | bytes 3145732
  6.7 10.4 %copy-start.33 = (bf16[128,2,2048]{2,1,0:T(2,128)(2,1)S(1)}, bf16[128,2,2048]{2,1,0:T(2,128)(2,1)}, u32[]{:S(2)}) copy-start(bf16[128,2,2048]{2,1,0:T(2,128)(2,1)} %param.7) | copy-start | bytes 3145732
  6.7 13.4 %collective-permute-start = (bf16[48,1536]{1,0:T(8,128)(2,1)}, bf16[48,1536]{1,0:T(8,128)(2,1)S(1)}, u32[]{:S(2)}, u32[]{:S(2)}) collective-permute-start(bf16[48,1536]{1,0:T(8,128)(2,1)} %get-tuple-element.134), channel_id=1, source_target_pairs={{0,8},{4,12},{8,0},{12,4},{16,24},{20,28},{24,16},{28,20},{1,9},{5... | collective-permute-start | bytes 442376 | tf_op jit(solution)/shard_map/ppermute | solution.py:38
  9.7 11.3 %collective-permute-start.5 = (bf16[48,1536]{1,0:T(8,128)(2,1)}, bf16[48,1536]{1,0:T(8,128)(2,1)}, u32[]{:S(2)}, u32[]{:S(2)}) collective-permute-start(bf16[48,1536]{1,0:T(8,128)(2,1)} %get-tuple-element.142), channel_id=1, source_target_pairs={{0,4},{4,0},{8,12},{12,8},{16,20},{20,16},{24,28},{28,24},{1,5},{5... | collective-permute-start | bytes 442376 | tf_op jit(solution)/shard_map/ppermute | solution.py:38
  11.3 9.8 %collective-permute-start.6 = (bf16[48,1536]{1,0:T(8,128)(2,1)}, bf16[48,1536]{1,0:T(8,128)(2,1)}, u32[]{:S(2)}, u32[]{:S(2)}) collective-permute-start(bf16[48,1536]{1,0:T(8,128)(2,1)} %get-tuple-element.143), channel_id=1, source_target_pairs={{0,12},{4,8},{8,4},{12,0},{16,28},{20,24},{24,20},{28,16},{1,13},{... | collective-permute-start | bytes 442376 | tf_op jit(solution)/shard_map/ppermute | solution.py:38
  11.3 29.8 %collective-permute-start.8 = (bf16[48,1536]{1,0:T(8,128)(2,1)}, bf16[48,1536]{1,0:T(8,128)(2,1)}, u32[]{:S(2)}, u32[]{:S(2)}) collective-permute-start(bf16[48,1536]{1,0:T(8,128)(2,1)} %get-tuple-element.154), channel_id=1, source_target_pairs={{0,24},{4,28},{8,16},{12,20},{16,8},{20,12},{24,0},{28,4},{1,25},{... | collective-permute-start | bytes 442376 | tf_op jit(solution)/shard_map/ppermute | solution.py:38
  15.3 25.9 %collective-permute-start.9 = (bf16[48,1536]{1,0:T(8,128)(2,1)}, bf16[48,1536]{1,0:T(8,128)(2,1)}, u32[]{:S(2)}, u32[]{:S(2)}) collective-permute-start(bf16[48,1536]{1,0:T(8,128)(2,1)} %get-tuple-element.155), channel_id=1, source_target_pairs={{0,28},{4,24},{8,20},{12,16},{16,12},{20,8},{24,4},{28,0},{1,29},{... | collective-permute-start | bytes 442376 | tf_op jit(solution)/shard_map/ppermute | solution.py:38
  17.6 4.4 %copy-start.28 = (bf16[48,1536]{1,0:T(8,128)(2,1)S(1)}, bf16[48,1536]{1,0:T(8,128)(2,1)}, u32[]{:S(2)}) copy-start(bf16[48,1536]{1,0:T(8,128)(2,1)} %copy-done.27) | copy-start | bytes 442372
  20.2 18.1 %collective-permute-start.1 = (bf16[48,1536]{1,0:T(8,128)(2,1)S(1)}, bf16[48,1536]{1,0:T(8,128)(2,1)S(1)}, u32[]{:S(2)}, u32[]{:S(2)}) collective-permute-start(bf16[48,1536]{1,0:T(8,128)(2,1)S(1)} %copy-done.30), channel_id=1, source_target_pairs={{0,16},{4,20},{8,24},{12,28},{16,0},{20,4},{24,8},{28,12},{1,17},{... | collective-permute-start | bytes 442376 | tf_op jit(solution)/shard_map/ppermute | solution.py:38
  22.1 22.1 %collective-permute-start.7 = (bf16[48,1536]{1,0:T(8,128)(2,1)S(1)}, bf16[48,1536]{1,0:T(8,128)(2,1)S(1)}, u32[]{:S(2)}, u32[]{:S(2)}) collective-permute-start(bf16[48,1536]{1,0:T(8,128)(2,1)S(1)} %copy-done.28), channel_id=1, source_target_pairs={{0,20},{4,16},{8,28},{12,24},{16,4},{20,0},{24,12},{28,8},{1,21},{... | collective-permute-start | bytes 442376 | tf_op jit(solution)/shard_map/ppermute | solution.py:38
  24.4 27.4 %collective-permute-start.15 = (bf16[192,1536]{1,0:T(8,128)(2,1)S(1)}, bf16[192,1536]{1,0:T(8,128)(2,1)S(1)}, u32[]{:S(2)}, u32[]{:S(2)}) collective-permute-start(bf16[192,1536]{1,0:T(8,128)(2,1)S(1)} %pad_maximum_fusion), channel_id=1, source_target_pairs={{0,2},{1,3},{2,0},{3,1},{4,6},{5,7},{6,4},{7,5},{8,10},{9,11},{10,... | collective-permute-start | bytes 1769480 | tf_op jit(solution)/shard_map/ppermute | solution.py:38
  38.3 17.5 %collective-permute-start.2 = (bf16[48,2048]{1,0:T(8,128)(2,1)S(1)}, bf16[48,2048]{1,0:T(8,128)(2,1)S(1)}, u32[]{:S(2)}, u32[]{:S(2)}) collective-permute-start(bf16[48,2048]{1,0:T(8,128)(2,1)S(1)} %get-tuple-element.136), channel_id=1, source_target_pairs={{0,24},{4,28},{8,16},{12,20},{16,8},{20,12},{24,0},{28,4},{1,25},{... | collective-permute-start | bytes 589832 | tf_op jit(solution)/shard_map/ppermute | solution.py:38
  45.2 10.6 %collective-permute-start.16 = (bf16[192,1536]{1,0:T(8,128)(2,1)S(1)}, bf16[192,1536]{1,0:T(8,128)(2,1)S(1)}, u32[]{:S(2)}, u32[]{:S(2)}) collective-permute-start(bf16[192,1536]{1,0:T(8,128)(2,1)S(1)} %pad_maximum_fusion.1), channel_id=1, source_target_pairs={{0,2},{1,3},{2,0},{3,1},{4,6},{5,7},{6,4},{7,5},{8,10},{9,11},{10,... | collective-permute-start | bytes 1769480 | tf_op jit(solution)/shard_map/ppermute | solution.py:38
  48.7 15.3 %collective-permute-start.10 = (bf16[384,1536]{1,0:T(8,128)(2,1)S(1)}, bf16[384,1536]{1,0:T(8,128)(2,1)S(1)}, u32[]{:S(2)}, u32[]{:S(2)}) collective-permute-start(bf16[384,1536]{1,0:T(8,128)(2,1)S(1)} %constant_dynamic-update-slice_fusion.refs_0_.refs_8_), channel_id=1, source_target_pairs={{0,1},{1,0},{2,3},{3,2},{4,5},{5,4},{6,7},{7,6},{8,9},{9,8},{10,11... | collective-permute-start | bytes 3538952 | tf_op jit(solution)/shard_map/ppermute | solution.py:38
  48.7 10.1 %collective-permute-start.12 = (bf16[48,2048]{1,0:T(8,128)(2,1)S(1)}, bf16[48,2048]{1,0:T(8,128)(2,1)S(1)}, u32[]{:S(2)}, u32[]{:S(2)}) collective-permute-start(bf16[48,2048]{1,0:T(8,128)(2,1)S(1)} %get-tuple-element.161), channel_id=1, source_target_pairs={{0,28},{4,24},{8,20},{12,16},{16,12},{20,8},{24,4},{28,0},{1,29},{... | collective-permute-start | bytes 589832 | tf_op jit(solution)/shard_map/ppermute | solution.py:38
  58.9 6.1 %collective-permute-start.17 = (bf16[384,1536]{1,0:T(8,128)(2,1)S(1)}, bf16[384,1536]{1,0:T(8,128)(2,1)S(1)}, u32[]{:S(2)}, u32[]{:S(2)}) collective-permute-start(bf16[384,1536]{1,0:T(8,128)(2,1)S(1)} %constant_dynamic-update-slice_fusion.5.refs_2_.refs_10_), channel_id=1, source_target_pairs={{0,1},{1,0},{2,3},{3,2},{4,5},{5,4},{6,7},{7,6},{8,9},{9,8},{10,11... | collective-permute-start | bytes 3538952 | tf_op jit(solution)/shard_map/ppermute | solution.py:38
  58.9 22.9 %collective-permute-start.14 = (bf16[48,2048]{1,0:T(8,128)(2,1)S(1)}, bf16[48,2048]{1,0:T(8,128)(2,1)S(1)}, u32[]{:S(2)}, u32[]{:S(2)}) collective-permute-start(bf16[48,2048]{1,0:T(8,128)(2,1)S(1)} %get-tuple-element.163), channel_id=1, source_target_pairs={{0,20},{4,16},{8,28},{12,24},{16,4},{20,0},{24,12},{28,8},{1,21},{... | collective-permute-start | bytes 589832 | tf_op jit(solution)/shard_map/ppermute | solution.py:38
  59.5 22.2 %collective-permute-start.3 = (bf16[48,2048]{1,0:T(8,128)(2,1)S(1)}, bf16[48,2048]{1,0:T(8,128)(2,1)S(1)}, u32[]{:S(2)}, u32[]{:S(2)}) collective-permute-start(bf16[48,2048]{1,0:T(8,128)(2,1)S(1)} %get-tuple-element.137), channel_id=1, source_target_pairs={{0,4},{4,0},{8,12},{12,8},{16,20},{20,16},{24,28},{28,24},{1,5},{5... | collective-permute-start | bytes 589832 | tf_op jit(solution)/shard_map/ppermute | solution.py:38
  61.0 20.7 %collective-permute-start.4 = (bf16[48,2048]{1,0:T(8,128)(2,1)S(1)}, bf16[48,2048]{1,0:T(8,128)(2,1)S(1)}, u32[]{:S(2)}, u32[]{:S(2)}) collective-permute-start(bf16[48,2048]{1,0:T(8,128)(2,1)S(1)} %get-tuple-element.139), channel_id=1, source_target_pairs={{0,8},{4,12},{8,0},{12,4},{16,24},{20,28},{24,16},{28,20},{1,9},{5... | collective-permute-start | bytes 589832 | tf_op jit(solution)/shard_map/ppermute | solution.py:38
  63.9 17.9 %collective-permute-start.13 = (bf16[48,2048]{1,0:T(8,128)(2,1)S(1)}, bf16[48,2048]{1,0:T(8,128)(2,1)S(1)}, u32[]{:S(2)}, u32[]{:S(2)}) collective-permute-start(bf16[48,2048]{1,0:T(8,128)(2,1)S(1)} %get-tuple-element.162), channel_id=1, source_target_pairs={{0,16},{4,20},{8,24},{12,28},{16,0},{20,4},{24,8},{28,12},{1,17},{... | collective-permute-start | bytes 589832 | tf_op jit(solution)/shard_map/ppermute | solution.py:38
  64.9 16.9 %collective-permute-start.11 = (bf16[48,2048]{1,0:T(8,128)(2,1)S(1)}, bf16[48,2048]{1,0:T(8,128)(2,1)S(1)}, u32[]{:S(2)}, u32[]{:S(2)}) collective-permute-start(bf16[48,2048]{1,0:T(8,128)(2,1)S(1)} %get-tuple-element.160), channel_id=1, source_target_pairs={{0,12},{4,8},{8,4},{12,0},{16,28},{20,24},{24,20},{28,16},{1,13},{... | collective-permute-start | bytes 589832 | tf_op jit(solution)/shard_map/ppermute | solution.py:38
  87.1 16.5 %collective-permute-start.26 = (bf16[384,1536]{1,0:T(8,128)(2,1)S(1)}, bf16[384,1536]{1,0:T(8,128)(2,1)S(1)}, u32[]{:S(2)}, u32[]{:S(2)}) collective-permute-start(bf16[384,1536]{1,0:T(8,128)(2,1)S(1)} %down.6), channel_id=1, source_target_pairs={{0,1},{1,0},{2,3},{3,2},{4,5},{5,4},{6,7},{7,6},{8,9},{9,8},{10,11... | collective-permute-start | bytes 3538952 | tf_op jit(solution)/shard_map/ppermute | solution.py:38
  92.5 35.9 %collective-permute-start.20 = (bf16[384,1536]{1,0:T(8,128)(2,1)S(1)}, bf16[384,1536]{1,0:T(8,128)(2,1)S(1)}, u32[]{:S(2)}, u32[]{:S(2)}) collective-permute-start(bf16[384,1536]{1,0:T(8,128)(2,1)S(1)} %down.4), channel_id=1, source_target_pairs={{0,1},{1,0},{2,3},{3,2},{4,5},{5,4},{6,7},{7,6},{8,9},{9,8},{10,11... | collective-permute-start | bytes 3538952 | tf_op jit(solution)/shard_map/ppermute | solution.py:38
  93.0 10.6 %collective-permute-start.18 = (bf16[48,2048]{1,0:T(8,128)(2,1)S(1)}, bf16[48,2048]{1,0:T(8,128)(2,1)S(1)}, u32[]{:S(2)}, u32[]{:S(2)}) collective-permute-start(bf16[48,2048]{1,0:T(8,128)(2,1)S(1)} %get-tuple-element.181), channel_id=1, source_target_pairs={{0,28},{4,24},{8,20},{12,16},{16,12},{20,8},{24,4},{28,0},{1,29},{... | collective-permute-start | bytes 589832 | tf_op jit(solution)/shard_map/ppermute | solution.py:38
  96.3 23.2 %collective-permute-start.19 = (bf16[48,2048]{1,0:T(8,128)(2,1)S(1)}, bf16[48,2048]{1,0:T(8,128)(2,1)S(1)}, u32[]{:S(2)}, u32[]{:S(2)}) collective-permute-start(bf16[48,2048]{1,0:T(8,128)(2,1)S(1)} %get-tuple-element.190), channel_id=1, source_target_pairs={{0,24},{4,28},{8,16},{12,20},{16,8},{20,12},{24,0},{28,4},{1,25},{... | collective-permute-start | bytes 589832 | tf_op jit(solution)/shard_map/ppermute | solution.py:38
  108.9 45.8 %collective-permute-start.27 = (bf16[192,1536]{1,0:T(8,128)(2,1)S(1)}, bf16[192,1536]{1,0:T(8,128)(2,1)S(1)}, u32[]{:S(2)}, u32[]{:S(2)}) collective-permute-start(bf16[192,1536]{1,0:T(8,128)(2,1)S(1)} %get-tuple-element.221), channel_id=1, source_target_pairs={{0,2},{1,3},{2,0},{3,1},{4,6},{5,7},{6,4},{7,5},{8,10},{9,11},{10,... | collective-permute-start | bytes 1769480 | tf_op jit(solution)/shard_map/ppermute | solution.py:38
  109.5 49.5 %collective-permute-start.31 = (bf16[192,1536]{1,0:T(8,128)(2,1)S(1)}, bf16[192,1536]{1,0:T(8,128)(2,1)S(1)}, u32[]{:S(2)}, u32[]{:S(2)}) collective-permute-start(bf16[192,1536]{1,0:T(8,128)(2,1)S(1)} %get-tuple-element.227), channel_id=1, source_target_pairs={{0,2},{1,3},{2,0},{3,1},{4,6},{5,7},{6,4},{7,5},{8,10},{9,11},{10,... | collective-permute-start | bytes 1769480 | tf_op jit(solution)/shard_map/ppermute | solution.py:38
  111.0 12.2 %collective-permute-start.23 = (bf16[48,2048]{1,0:T(8,128)(2,1)S(1)}, bf16[48,2048]{1,0:T(8,128)(2,1)S(1)}, u32[]{:S(2)}, u32[]{:S(2)}) collective-permute-start(bf16[48,2048]{1,0:T(8,128)(2,1)S(1)} %get-tuple-element.215), channel_id=1, source_target_pairs={{0,12},{4,8},{8,4},{12,0},{16,28},{20,24},{24,20},{28,16},{1,13},{... | collective-permute-start | bytes 589832 | tf_op jit(solution)/shard_map/ppermute | solution.py:38
  119.5 16.8 %copy-start.3 = (bf16[48,2048]{1,0:T(8,128)(2,1)}, bf16[48,2048]{1,0:T(8,128)(2,1)S(1)}, u32[]{:S(2)}) copy-start(bf16[48,2048]{1,0:T(8,128)(2,1)S(1)} %collective-permute-done.19.refs_6_) | copy-start | bytes 589828
  119.5 7.1 %collective-permute-start.21 = (bf16[48,2048]{1,0:T(8,128)(2,1)S(1)}, bf16[48,2048]{1,0:T(8,128)(2,1)S(1)}, u32[]{:S(2)}, u32[]{:S(2)}) collective-permute-start(bf16[48,2048]{1,0:T(8,128)(2,1)S(1)} %get-tuple-element.212), channel_id=1, source_target_pairs={{0,4},{4,0},{8,12},{12,8},{16,20},{20,16},{24,28},{28,24},{1,5},{5... | collective-permute-start | bytes 589832 | tf_op jit(solution)/shard_map/ppermute | solution.py:38
  123.2 13.0 %copy-start.5 = (bf16[48,2048]{1,0:T(8,128)(2,1)}, bf16[48,2048]{1,0:T(8,128)(2,1)S(1)}, u32[]{:S(2)}) copy-start(bf16[48,2048]{1,0:T(8,128)(2,1)S(1)} %collective-permute-done.23.refs_3_) | copy-start | bytes 589828
  123.2 31.5 %collective-permute-start.22 = (bf16[48,2048]{1,0:T(8,128)(2,1)S(1)}, bf16[48,2048]{1,0:T(8,128)(2,1)S(1)}, u32[]{:S(2)}, u32[]{:S(2)}) collective-permute-start(bf16[48,2048]{1,0:T(8,128)(2,1)S(1)} %get-tuple-element.214), channel_id=1, source_target_pairs={{0,8},{4,12},{8,0},{12,4},{16,24},{20,28},{24,16},{28,20},{1,9},{5... | collective-permute-start | bytes 589832 | tf_op jit(solution)/shard_map/ppermute | solution.py:38
  126.5 9.7 %copy-start.7 = (bf16[48,2048]{1,0:T(8,128)(2,1)}, bf16[48,2048]{1,0:T(8,128)(2,1)S(1)}, u32[]{:S(2)}) copy-start(bf16[48,2048]{1,0:T(8,128)(2,1)S(1)} %collective-permute-done.21.refs_1_) | copy-start | bytes 589828
  126.5 28.2 %collective-permute-start.24 = (bf16[48,2048]{1,0:T(8,128)(2,1)S(1)}, bf16[48,2048]{1,0:T(8,128)(2,1)S(1)}, u32[]{:S(2)}, u32[]{:S(2)}) collective-permute-start(bf16[48,2048]{1,0:T(8,128)(2,1)S(1)} %get-tuple-element.217), channel_id=1, source_target_pairs={{0,16},{4,20},{8,24},{12,28},{16,0},{20,4},{24,8},{28,12},{1,17},{... | collective-permute-start | bytes 589832 | tf_op jit(solution)/shard_map/ppermute | solution.py:38
  128.4 26.3 %collective-permute-start.25 = (bf16[48,2048]{1,0:T(8,128)(2,1)S(1)}, bf16[48,2048]{1,0:T(8,128)(2,1)S(1)}, u32[]{:S(2)}, u32[]{:S(2)}) collective-permute-start(bf16[48,2048]{1,0:T(8,128)(2,1)S(1)} %get-tuple-element.219), channel_id=1, source_target_pairs={{0,20},{4,16},{8,28},{12,24},{16,4},{20,0},{24,12},{28,8},{1,21},{... | collective-permute-start | bytes 589832 | tf_op jit(solution)/shard_map/ppermute | solution.py:38
  154.7 5.2 %copy-start.9 = (bf16[48,2048]{1,0:T(8,128)(2,1)}, bf16[48,2048]{1,0:T(8,128)(2,1)S(1)}, u32[]{:S(2)}) copy-start(bf16[48,2048]{1,0:T(8,128)(2,1)S(1)} %collective-permute-done.22.refs_2_) | copy-start | bytes 589828
  154.7 5.2 %copy-start.11 = (bf16[48,2048]{1,0:T(8,128)(2,1)}, bf16[48,2048]{1,0:T(8,128)(2,1)S(1)}, u32[]{:S(2)}) copy-start(bf16[48,2048]{1,0:T(8,128)(2,1)S(1)} %collective-permute-done.24.refs_4_) | copy-start | bytes 589828
  154.7 5.2 %copy-start.13 = (bf16[48,2048]{1,0:T(8,128)(2,1)}, bf16[48,2048]{1,0:T(8,128)(2,1)S(1)}, u32[]{:S(2)}) copy-start(bf16[48,2048]{1,0:T(8,128)(2,1)S(1)} %collective-permute-done.25.refs_5_) | copy-start | bytes 589828
  155.5 13.4 %copy-start.15 = (bf16[48,1536]{1,0:T(8,128)(2,1)}, bf16[48,1536]{1,0:T(8,128)(2,1)S(1)}, u32[]{:S(2)}) copy-start(bf16[48,1536]{1,0:T(8,128)(2,1)S(1)} %get-tuple-element.241.refs_0_) | copy-start | bytes 442372
  155.5 13.4 %copy-start.23 = (f32[128,2]{0,1:T(2,128)S(1)}, f32[128,2]{0,1:T(2,128)}, u32[]{:S(2)}) copy-start(f32[128,2]{0,1:T(2,128)} %param.9) | copy-start | bytes 3076
  155.5 7.9 %collective-permute-start.28 = (bf16[48,1536]{1,0:T(8,128)(2,1)S(1)}, bf16[48,1536]{1,0:T(8,128)(2,1)S(1)}, u32[]{:S(2)}, u32[]{:S(2)}) collective-permute-start(bf16[48,1536]{1,0:T(8,128)(2,1)S(1)} %get-tuple-element.223), channel_id=1, source_target_pairs={{0,4},{4,0},{8,12},{12,8},{16,20},{20,16},{24,28},{28,24},{1,5},{5... | collective-permute-start | bytes 442376 | tf_op jit(solution)/shard_map/ppermute | solution.py:38
  155.7 9.5 %collective-permute-start.30 = (bf16[48,1536]{1,0:T(8,128)(2,1)S(1)}, bf16[48,1536]{1,0:T(8,128)(2,1)S(1)}, u32[]{:S(2)}, u32[]{:S(2)}) collective-permute-start(bf16[48,1536]{1,0:T(8,128)(2,1)S(1)} %get-tuple-element.225), channel_id=1, source_target_pairs={{0,12},{4,8},{8,4},{12,0},{16,28},{20,24},{24,20},{28,16},{1,13},{... | collective-permute-start | bytes 442376 | tf_op jit(solution)/shard_map/ppermute | solution.py:38
  157.6 30.9 %collective-permute-start.29 = (bf16[48,1536]{1,0:T(8,128)(2,1)}, bf16[48,1536]{1,0:T(8,128)(2,1)}, u32[]{:S(2)}, u32[]{:S(2)}) collective-permute-start(bf16[48,1536]{1,0:T(8,128)(2,1)} %get-tuple-element.224), channel_id=1, source_target_pairs={{0,8},{4,12},{8,0},{12,4},{16,24},{20,28},{24,16},{28,20},{1,9},{5... | collective-permute-start | bytes 442376 | tf_op jit(solution)/shard_map/ppermute | solution.py:38
  159.9 28.6 %collective-permute-start.32 = (bf16[48,1536]{1,0:T(8,128)(2,1)}, bf16[48,1536]{1,0:T(8,128)(2,1)}, u32[]{:S(2)}, u32[]{:S(2)}) collective-permute-start(bf16[48,1536]{1,0:T(8,128)(2,1)} %get-tuple-element.228), channel_id=1, source_target_pairs={{0,16},{4,20},{8,24},{12,28},{16,0},{20,4},{24,8},{28,12},{1,17},{... | collective-permute-start | bytes 442376 | tf_op jit(solution)/shard_map/ppermute | solution.py:38
  160.4 28.1 %collective-permute-start.33 = (bf16[48,1536]{1,0:T(8,128)(2,1)}, bf16[48,1536]{1,0:T(8,128)(2,1)}, u32[]{:S(2)}, u32[]{:S(2)}) collective-permute-start(bf16[48,1536]{1,0:T(8,128)(2,1)} %get-tuple-element.229), channel_id=1, source_target_pairs={{0,20},{4,16},{8,28},{12,24},{16,4},{20,0},{24,12},{28,8},{1,21},{... | collective-permute-start | bytes 442376 | tf_op jit(solution)/shard_map/ppermute | solution.py:38
  164.1 24.5 %collective-permute-start.34 = (bf16[48,1536]{1,0:T(8,128)(2,1)}, bf16[48,1536]{1,0:T(8,128)(2,1)}, u32[]{:S(2)}, u32[]{:S(2)}) collective-permute-start(bf16[48,1536]{1,0:T(8,128)(2,1)} %get-tuple-element.230), channel_id=1, source_target_pairs={{0,24},{4,28},{8,16},{12,20},{16,8},{20,12},{24,0},{28,4},{1,25},{... | collective-permute-start | bytes 442376 | tf_op jit(solution)/shard_map/ppermute | solution.py:38
  165.9 22.7 %collective-permute-start.35 = (bf16[48,1536]{1,0:T(8,128)(2,1)}, bf16[48,1536]{1,0:T(8,128)(2,1)}, u32[]{:S(2)}, u32[]{:S(2)}) collective-permute-start(bf16[48,1536]{1,0:T(8,128)(2,1)} %get-tuple-element.231), channel_id=1, source_target_pairs={{0,28},{4,24},{8,20},{12,16},{16,12},{20,8},{24,4},{28,0},{1,29},{... | collective-permute-start | bytes 442376 | tf_op jit(solution)/shard_map/ppermute | solution.py:38
  180.6 8.6 %copy-start.2 = (bf16[256,2048]{1,0:T(8,128)(2,1)S(1)}, bf16[256,2048]{1,0:T(8,128)(2,1)}, u32[]{:S(2)}) copy-start(bf16[256,2048]{1,0:T(8,128)(2,1)} %copy-done.1) | copy-start | bytes 3145732
  (22 other events, 24.2 us)

commit v2 on v0

v2 whole, which is shorter than its diff:
```python
import functools

import jax
import jax.numpy as jnp
from jax import lax
from jax.experimental import pallas as pl
from jax.experimental.pallas import tpu as pltpu
from jax.sharding import PartitionSpec as P

E = 8
TOP = 2
CAP = 48
F32 = jnp.float32
BF16 = jnp.bfloat16
I32 = jnp.int32
PARAMS = pltpu.CompilerParams(vmem_limit_bytes=40 * 1024 * 1024)
ROWS = (((0,), (0,)), ((), ()))
COLUMNS = (((1,), (1,)), ((), ()))
WORK = 1 / 1000


def whole(a):
    return pl.BlockSpec(a.shape, lambda *_: (0,) * len(a.shape))


def cost(flops, *arrays):
    size = sum(a.size * jnp.dtype(a.dtype).itemsize for a in arrays)
    return pl.CostEstimate(
        flops=int(flops * WORK), bytes_accessed=int(size * WORK), transcendentals=0
    )


def swap(x, axis, bit, after=()):
    if len(after):
        x = lax.optimization_barrier((x, tuple(after)))[0]
    count = lax.axis_size(axis)
    return lax.ppermute(x, axis, [(i, i ^ bit) for i in range(count)])


def ones(table):
    return jnp.where(table, 1.0, 0.0).astype(BF16)


def block_table(d, slices, slot_key):
    key = lax.broadcasted_iota(I32, (CAP, slot_key.shape[1]), 0) + d // slices * CAP
    return key == slot_key


def table_of(slices, slot_key):
    count = E * slices
    return jnp.concatenate([block_table(d, slices, slot_key) for d in range(count)], axis=0)


def scale_kernel(slices, dp_ref, hid_ref, ids_ref, weight_ref, *refs):
    grads, o_refs, key_ref = refs[:slices], refs[slices:-1], refs[-1]
    tokens = ids_ref.shape[1]
    slots = tokens * TOP
    ids = jnp.concatenate([ids_ref[s : s + 1] for s in range(TOP)], axis=1)
    weight = jnp.concatenate([weight_ref[s : s + 1] for s in range(TOP)], axis=1)
    is_expert = lax.broadcasted_iota(I32, (E, slots), 0) == ids
    before = lax.broadcasted_iota(I32, (slots, slots), 0) < lax.broadcasted_iota(
        I32, (slots, slots), 1
    )
    earlier = jnp.dot(ones(is_expert), ones(before), preferred_element_type=F32)
    place = jnp.sum(jnp.where(is_expert, earlier, 0.0), axis=0, keepdims=True)
    slot_key = ids * CAP + place.astype(I32)
    for s in range(TOP):
        key_ref[s : s + 1, :] = slot_key[:, s * tokens : (s + 1) * tokens]
    to = [dp_ref[0] ^ k for k in range(E * slices)]
    table = jnp.concatenate([block_table(d, slices, slot_key) for d in to], axis=0)
    row_weight = jnp.sum(jnp.where(table, weight, 0.0), axis=1, keepdims=True)
    picks = ones(table[:, :tokens]) + ones(table[:, tokens:])
    picked = [jnp.dot(picks, g[...], preferred_element_type=F32) for g in grads]
    for k, o_ref in enumerate(o_refs):
        at = slice(k * CAP, (k + 1) * CAP)
        rows = picked[0][at]
        for j in range(1, slices):
            rows = jnp.where(to[k] % slices == j, picked[j][at], rows)
        o_ref[...] = (rows * row_weight[at]).astype(BF16)


def send_scaled(my_dp, my_hid, ids, weight, out_grad, slices, quarter):
    tokens = ids.shape[1]
    hid_count = out_grad.shape[1] // (slices * quarter)
    outs = [jax.ShapeDtypeStruct((CAP, quarter), BF16)] * (E * slices)
    key = jax.ShapeDtypeStruct(ids.shape, I32)

    def part(j):
        return pl.BlockSpec((tokens, quarter), lambda i, d, h: (0, j * hid_count + h[0]))

    return pl.pallas_call(
        functools.partial(scale_kernel, slices),
        grid_spec=pltpu.PrefetchScalarGridSpec(
            num_scalar_prefetch=2,
            grid=(1,),
            in_specs=[whole(ids), whole(weight)] + [part(j) for j in range(slices)],
            out_specs=[whole(o) for o in outs] + [whole(key)],
        ),
        out_shape=outs + [key],
        compiler_params=PARAMS,
        cost_estimate=cost(0, *outs),
        name="send_scaled",
    )(my_dp, my_hid, ids, weight, *[out_grad] * slices)


def hidden_of(gate, up):
    sig = 1.0 / (1.0 + jnp.exp(-gate))
    return sig, (gate * sig * up).astype(BF16)


def send_kernel(slices, key_ref, gate_ref, up_ref, o_ref):
    hidden = hidden_of(gate_ref[...].astype(F32), up_ref[...].astype(F32))[1]
    table = ones(table_of(slices, key_ref[...]))
    o_ref[...] = jnp.dot(table, hidden, preferred_element_type=F32).astype(BF16)


def send_hidden(slices, slot_key, gate, up):
    slots, depth = gate.shape
    rows = CAP * E * slices
    block = 512
    out = jax.ShapeDtypeStruct((rows, depth), BF16)
    part = pl.BlockSpec((slots, block), lambda i: (0, i))
    return pl.pallas_call(
        functools.partial(send_kernel, slices),
        grid=(depth // block,),
        in_specs=[whole(slot_key), part, part],
        out_specs=pl.BlockSpec((rows, block), lambda i: (0, i)),
        out_shape=out,
        compiler_params=PARAMS,
        cost_estimate=cost(0, gate, up, out),
        name="send_hidden",
    )(slot_key, gate, up)


def down_kernel(added, hid_ref, x_ref, w_ref, *refs):
    out = jnp.dot(x_ref[...], w_ref[...], preferred_element_type=F32)
    for a in refs[:added]:
        out = out + a[...].astype(F32)
    o_ref = refs[added]
    o_ref[...] = out.astype(o_ref.dtype)


def down(my_hid, x, weights, q, quarter, dtype, *add):
    rows, depth = x.shape
    block = min(512, quarter)
    per = quarter // block
    out = jax.ShapeDtypeStruct((rows, quarter), dtype)
    return pl.pallas_call(
        functools.partial(down_kernel, len(add)),
        grid_spec=pltpu.PrefetchScalarGridSpec(
            num_scalar_prefetch=1,
            grid=(per,),
            in_specs=[
                whole(x),
                pl.BlockSpec((depth, block), lambda j, h: (0, (h[0] ^ q) * per + j)),
            ]
            + [pl.BlockSpec((rows, block), lambda j, h: (0, j)) for _ in add],
            out_specs=pl.BlockSpec((rows, block), lambda j, h: (0, j)),
        ),
        out_shape=out,
        compiler_params=PARAMS,
        cost_estimate=cost(
            2 * rows * depth * quarter, x, out, jax.ShapeDtypeStruct((depth, quarter), BF16)
        ),
        name="down",
    )(my_hid, x, weights, *add)


def sum_kernel(a_ref, b_ref, o_ref):
    o_ref[...] = (a_ref[...] + b_ref[...].astype(F32)).astype(BF16)


def sum_of(a, b):
    rows, width = a.shape
    block = min(512, width)
    part = pl.BlockSpec((rows, block), lambda i: (0, i))
    out = jax.ShapeDtypeStruct((rows, width), BF16)
    return pl.pallas_call(
        sum_kernel,
        grid=(width // block,),
        in_specs=[part, part],
        out_specs=part,
        out_shape=out,
        compiler_params=PARAMS,
        cost_estimate=cost(0, a, b, out),
        name="sum_of",
    )(a, b)


def in_order(dp_ref, halves, y_ref):
    per = halves[0].shape[0] // CAP
    for n, half in enumerate(halves):
        for k in range(per):
            at = pl.multiple_of((dp_ref[0] ^ (n % 2 * per + k)) * CAP, CAP)
            y_ref[n // 2, pl.ds(at, CAP), :] = half[k * CAP : (k + 1) * CAP, :]


def quarter_at(hid_ref, q, quarter):
    return pl.ds(pl.multiple_of((hid_ref[0] ^ q) * quarter, 128), quarter)


def back_kernel(dp_ref, hid_ref, *refs):
    *halves, w_ref, o_ref, y_ref = refs

    @pl.when(pl.program_id(0) == 0)
    def _():
        in_order(dp_ref, halves, y_ref)

    count, _, quarter = y_ref.shape
    total = None
    for q in range(count):
        w = w_ref[:, quarter_at(hid_ref, q, quarter)]
        term = lax.dot_general(y_ref[q], w, COLUMNS, preferred_element_type=F32)
        total = term if total is None else total + term
    o_ref[...] = total.astype(BF16)


def back(my_dp, my_hid, halves, weights):
    rows, quarter = 2 * halves[0].shape[0], halves[0].shape[1]
    depth, width = weights.shape
    block = 256
    out = jax.ShapeDtypeStruct((rows, depth), BF16)
    return pl.pallas_call(
        back_kernel,
        grid_spec=pltpu.PrefetchScalarGridSpec(
            num_scalar_prefetch=2,
            grid=(depth // block,),
            in_specs=[whole(p) for p in halves]
            + [pl.BlockSpec((block, width), lambda i, d, h: (i, 0))],
            out_specs=pl.BlockSpec((rows, block), lambda i, d, h: (0, i)),
            scratch_shapes=[pltpu.VMEM((width // quarter, rows, quarter), BF16)],
        ),
        out_shape=out,
        compiler_params=PARAMS,
        cost_estimate=cost(2 * rows * depth * width, *halves, weights, out),
        name="back",
    )(my_dp, my_hid, *halves, weights)


def outer_kernel(dp_ref, hid_ref, x_ref, *refs):
    *halves, o_ref, y_ref = refs

    @pl.when(pl.program_id(0) == 0)
    def _():
        in_order(dp_ref, halves, y_ref)

    count, _, quarter = y_ref.shape
    x = x_ref[...]
    for q in range(count):
        o_ref[0, :, quarter_at(hid_ref, q, quarter)] = lax.dot_general(
            x, y_ref[q], ROWS, preferred_element_type=F32
        ).astype(BF16)


def outer(my_dp, my_hid, x, halves):
    rows, depth = x.shape
    quarter = halves[0].shape[1]
    width = quarter * len(halves) // 2
    block = 256
    out = jax.ShapeDtypeStruct((1, depth, width), BF16)
    return pl.pallas_call(
        outer_kernel,
        grid_spec=pltpu.PrefetchScalarGridSpec(
            num_scalar_prefetch=2,
            grid=(depth // block,),
            in_specs=[pl.BlockSpec((rows, block), lambda i, d, h: (0, i))]
            + [whole(p) for p in halves],
            out_specs=pl.BlockSpec((1, block, width), lambda i, d, h: (0, i, 0)),
            scratch_shapes=[pltpu.VMEM((width // quarter, rows, quarter), BF16)],
        ),
        out_shape=out,
        compiler_params=PARAMS,
        cost_estimate=cost(2 * rows * depth * width, x, *halves, out),
        name="outer",
    )(my_dp, my_hid, x, *halves)


def grads_kernel(slices, key_ref, gate_ref, up_ref, back_ref, dgate_ref, dup_ref, dot_ref):
    table = ones(table_of(slices, key_ref[...]))
    h = lax.dot_general(table, back_ref[...], ROWS, preferred_element_type=F32)
    g, u = gate_ref[...].astype(F32), up_ref[...].astype(F32)
    sig, hidden = hidden_of(g, u)
    dgate_ref[...] = (h * u * sig * (1.0 + g * (1.0 - sig))).astype(BF16)
    dup_ref[...] = (h * g * sig).astype(BF16)
    dots = jnp.sum(hidden.astype(F32) * h, axis=1, keepdims=True)

    @pl.when(pl.program_id(0) == 0)
    def _():
        dot_ref[...] = dots

    @pl.when(pl.program_id(0) > 0)
    def _():
        dot_ref[...] += dots


def grads(slices, slot_key, gate, up, got_back):
    slots, depth = gate.shape
    rows = got_back.shape[0]
    block = 512
    part = pl.BlockSpec((slots, block), lambda i: (0, i))
    out = jax.ShapeDtypeStruct(gate.shape, BF16)
    dots = jax.ShapeDtypeStruct((slots, 1), F32)
    return pl.pallas_call(
        functools.partial(grads_kernel, slices),
        grid=(depth // block,),
        in_specs=[
            whole(slot_key),
            part,
            part,
            pl.BlockSpec((rows, block), lambda i: (0, i)),
        ],
        out_specs=[part, part, whole(dots)],
        out_shape=[out, out, dots],
        compiler_params=PARAMS,
        cost_estimate=cost(0, gate, up, got_back, out, out),
        name="grads",
    )(slot_key, gate, up, got_back)


def mix_kernel(slices, key_ref, weight_ref, x_ref, *refs):
    o_ref = refs[-1]
    tokens = key_ref.shape[1]
    x = x_ref[...]
    for j in range(slices):
        rows = []
        for d in range(E * slices):
            row = jnp.zeros((CAP, tokens), F32)
            if d % slices == j:
                for s in range(TOP):
                    hit = block_table(d, slices, key_ref[s : s + 1, :])
                    row = jnp.where(hit, weight_ref[s : s + 1, :], row)
            rows.append(row)
        left = jnp.concatenate(rows, axis=0)
        total = None
        for _ in range(3):
            part = left.astype(BF16)
            left = left - part.astype(F32)
            term = lax.dot_general(part, x, ROWS, preferred_element_type=F32)
            total = term if total is None else total + term
        o_ref[j] = total.astype(BF16)


def mixed_of(slices, slot_key, weight, got_out, after):
    tokens = slot_key.shape[1]
    rows, quarter = got_out.shape
    out = jax.ShapeDtypeStruct((slices, tokens, quarter), BF16)
    return pl.pallas_call(
        functools.partial(mix_kernel, slices),
        grid=(1,),
        in_specs=[whole(slot_key), whole(weight), whole(got_out)]
        + [pl.BlockSpec(memory_space=pl.ANY) for _ in after],
        out_specs=whole(out),
        out_shape=out,
        compiler_params=PARAMS,
        cost_estimate=cost(0, got_out, out),
        name="mixed",
    )(slot_key, weight, got_out, *after)


def per_device(gate_pre, up_pre, out_grad, combine, expert_ids, down_weight):
    dp_count = lax.axis_size("dp")
    hid_count = lax.axis_size("hid")
    my_dp = lax.axis_index("dp").astype(I32).reshape(1)
    my_hid = lax.axis_index("hid").astype(I32).reshape(1)
    slices = dp_count // E
    tokens = gate_pre.shape[0]
    local_ff = gate_pre.shape[2]
    quarter = down_weight.shape[2] // hid_count
    slots = tokens * TOP
    weights = down_weight[0]
    ids, weight = expert_ids.T, combine.T

    def over_dp(x):
        return lax.all_to_all(x, "dp", split_axis=0, concat_axis=0, tiled=True)

    *scaled, slot_key = send_scaled(my_dp, my_hid, ids, weight, out_grad, slices, quarter)
    gate, up = gate_pre.reshape(slots, local_ff), up_pre.reshape(slots, local_ff)
    token_key = slot_key.T.reshape(1, slots)
    hidden = send_hidden(slices, token_key, gate, up)

    near, far = range(1, dp_count // 2), range(dp_count // 2, dp_count)
    got = {0: scaled[0]}
    for k in [*near, *far[:2]]:
        got[k] = swap(scaled[k], "dp", k)
    for i, k in enumerate(far[2:]):
        got[k] = swap(scaled[k], "dp", k, [got[near[i % len(near)]]])
    halves = []
    for part in ([0, *near], far):
        blocks = lax.optimization_barrier(tuple(got[k] for k in part))
        piece = {0: jnp.concatenate(blocks)}
        if not halves:
            piece[0], hidden = lax.optimization_barrier((piece[0], hidden))
        bit = hid_count // 2
        while bit:
            for q in sorted(piece):
                piece[q ^ bit] = swap(piece[q], "hid", bit)
            bit //= 2
        halves.append(piece)
    hidden = lax.optimization_barrier((hidden, [got[k] for k in far]))[0]
    got_hidden = over_dp(hidden)
    halves = [piece[q] for q in range(hid_count) for piece in halves]
    sent_back = back(my_dp, my_hid, halves, weights)
    got_hidden, sent_back = lax.optimization_barrier((got_hidden, sent_back))

    got_back = over_dp(sent_back)
    sums = {}
    for q in range(hid_count - 1, 0, -2):
        sums[q] = swap(down(my_hid, got_hidden, weights, q, quarter, BF16), "hid", 1)
    others = []
    for q in range(hid_count - 2, 0, -2):
        made = down(my_hid, got_hidden, weights, q, quarter, BF16, sums[q ^ 1])
        others.append(swap(made, "hid", q))
    x = lax.optimization_barrier((got_hidden, made))[0]
    total = down(my_hid, x, weights, 0, quarter, F32, sums[1])
    x = lax.optimization_barrier((x, total))[0]
    weight_grad = outer(my_dp, my_hid, x, halves)
    for other in others[1:]:
        total = total + other.astype(F32)
    total, got_back, weight_grad = lax.optimization_barrier((total, got_back, weight_grad))
    total, got_back = lax.optimization_barrier((sum_of(total, others[0]), got_back))
    got_out = over_dp(total)

    gate_grad, up_grad, dots = grads(slices, token_key, gate, up, got_back)
    shape = (tokens, TOP, local_ff)
    gate_grad, up_grad = gate_grad.reshape(shape), up_grad.reshape(shape)
    cg = dots.reshape(tokens, TOP) / combine
    bit = 1
    while bit < hid_count:
        cg = cg + swap(cg, "hid", bit)
        bit *= 2
    after = (weight_grad, gate_grad, up_grad, cg)
    mixed = mixed_of(slices, slot_key, weight, got_out, after)
    return jnp.swapaxes(mixed, 0, 1), cg, gate_grad, up_grad, weight_grad


def solution(mesh):
    return jax.shard_map(
        per_device,
        mesh=mesh,
        in_specs=(
            P("dp", None, "hid"),
            P("dp", None, "hid"),
            P("dp", None),
            P("dp", None),
            P("dp", None),
            P("dp", "hid", None),
        ),
        out_specs=(
            P("dp", None, "hid"),
            P("dp", None),
            P("dp", None, "hid"),
            P("dp", None, "hid"),
            P("dp", "hid", None),
        ),
        check_vma=False,
    )
```

time: 631 us -> 186 us (0.29); the launches traced: 623 us -> 185 us
  blocking collectives: 372 us -> 0 us
  Pallas kernels: 0 us -> 64.8 us
  matrix products: 52.5 us -> 0 us
  waiting for transfers between devices: 100 us -> 48.5 us
  starting transfers between devices: 4 us -> 41.7 us
  other arithmetic: 27.9 us -> 1.23 us
  local copies, waits for them, and re-layouts: 51.4 us -> 27.5 us
  between operations: 14.7 us -> 1.02 us
    all_to_all x3 -> x0, blocking collectives: 362 us -> none  [the longest x1 209 us: per_device(): lax.all_to_all(expert_out.reshape(dp_count, capacity, slice_width), 'dp',...]
    pallas_call x0 -> x11, Pallas kernels: none -> 64.8 us  [the longest x4 21.8 us: down(): pl.pallas_call(functools.partial(down_kernel, len(add)), grid_spec=pltpu....]
    all_to_all x1 -> x3, waiting for transfers between devices: 69.4 us -> 13.9 us  [over_dp(): return lax.all_to_all(x, 'dp', split_axis=0, concat_axis=0, tiled=True)]
    dot_general x3 -> x0, matrix products: 52.5 us -> none  [the longest x1 21.2 us: per_device(): lax.dot_general(hidden_rows, grad_rows, (((0,), (0,)), ((), ())), preferr...]
    ppermute x0 -> x18, waiting for transfers between devices: none -> 34.5 us  [swap(): return lax.ppermute(x, axis, [(i, i ^ bit) for i in range(count)])]
    reduce_scatter x1 -> x0, waiting for transfers between devices: 30.8 us -> none  [per_device(): lax.psum_scatter(slot_part, 'hid', scatter_dimension=2, tiled=True)]
    gather x5 -> x0, local copies, waits for them, and re-layouts: 24.8 us -> none  [the longest x1 11.6 us: per_device(): jnp.take(back_out.reshape(dp_count * capacity, slice_width), return_index...]
    ppermute x0 -> x18, starting transfers between devices: none -> 21.3 us  [swap(): return lax.ppermute(x, axis, [(i, i ^ bit) for i in range(count)])]
  transfers between devices with their start and end apart: 2 -> 21, of which waited for: 2 -> 9; matrix products, arithmetic and copies ran while one was open for 4% -> 6% of each run, Pallas kernels for 0% -> 33%
where the time goes in v2:
time: 186 us; the launch traced here: 185 us
  Pallas kernels  64.8 us (35%)
  waiting for transfers between devices  48.5 us (26%)
  starting transfers between devices  41.7 us (22%)
  local copies, waits for them, and re-layouts  27.5 us (15%)
    ppermute x18, waiting for transfers between devices, swap(): return lax.ppermute(x, axis, [(i, i ^ bit) for i in range(count)])  34.5 us
    pallas_call x4, Pallas kernels, down(): pl.pallas_call(functools.partial(down_kernel, len(add)), grid_spec=pltpu....  21.8 us
    ppermute x18, starting transfers between devices, swap(): return lax.ppermute(x, axis, [(i, i ^ bit) for i in range(count)])  21.3 us
    all_to_all x3, starting transfers between devices, over_dp(): return lax.all_to_all(x, 'dp', split_axis=0, concat_axis=0, tiled=True)  20.4 us
    unnamed x67, local copies, waits for them, and re-layouts  20.4 us
    pallas_call x1, Pallas kernels, outer(): pl.pallas_call(outer_kernel, grid_spec=pltpu.PrefetchScalarGridSpec(num_s...  17 us
    pallas_call x1, Pallas kernels, back(): pl.pallas_call(back_kernel, grid_spec=pltpu.PrefetchScalarGridSpec(num_sc...  15.4 us
    all_to_all x3, waiting for transfers between devices, over_dp(): return lax.all_to_all(x, 'dp', split_axis=0, concat_axis=0, tiled=True)  13.9 us
  transfers between devices with their start and end apart: 21, of which 9 were waited for; matrix products, arithmetic and copies ran while one was open for 6% of the time, Pallas kernels for 33%

profile of v2, /device:TPU:0, one launch (start us, length us, event | category | flops | bytes accessed | tf_op | source)
XLA Modules:
  0.0 184.6 jit_solution(553808939982614523)
XLA Ops:
  0.6 1.4 copy-done.23
  4.0 3.0 %collective-permute-start = (bf16[48,1536]{1,0:T(8,128)(2,1)S(1)}, bf16[48,1536]{1,0:T(8,128)(2,1)}, u32[]{:S(2)}, u32[]{:S(2)}) collective-permute-start(bf16[48,1536]{1,0:T(8,128)(2,1)S(1)} %get-tuple-element.41), channel_id=1, source_target_pairs={{0,4},{4,0},{8,12},{12,8},{16,20},{20,16},{24,28},{28,24},{1,5},{5... | collective-permute-start | bytes 442376 | tf_op jit(solution)/shard_map/ppermute | solution.py:37
  7.1 1.6 collective-permute-start.1
  8.6 3.0 %collective-permute-start.3 = (bf16[48,1536]{1,0:T(8,128)(2,1)S(1)}, bf16[48,1536]{1,0:T(8,128)(2,1)}, u32[]{:S(2)}, u32[]{:S(2)}) collective-permute-start(bf16[48,1536]{1,0:T(8,128)(2,1)S(1)} %get-tuple-element.49), channel_id=1, source_target_pairs={{0,16},{4,20},{8,24},{12,28},{16,0},{20,4},{24,8},{28,12},{1,17},{... | collective-permute-start | bytes 442376 | tf_op jit(solution)/shard_map/ppermute | solution.py:37
  11.6 1.3 collective-permute-start.4
  13.6 1.5 reshape.44.up_ref
  15.1 1.9 %send_hidden.1 = bf16[384,2048]{1,0:T(8,128)(2,1)S(1)} custom-call(s32[1,256]{1,0:T(1,128)S(1)} %reshape.42.key_ref, bf16[256,2048]{1,0:T(8,128)(2,1)S(1)} %reshape.43.gate_ref, bf16[256,2048]{1,0:T(8,128)(2,1)S(1)} %reshape.44.up_ref), custom_call_target="tpu_custom_call" | custom-call | bytes 3670 | tf_op jit(solution)/shard_map/send_hidden/pallas_call | solution.py:123
  17.1 1.1 copy-done.5
  18.2 1.6 collective-permute-done.1
  20.2 1.8 %collective-permute-start.5 = (bf16[48,1536]{1,0:T(8,128)(2,1)S(1)}, bf16[48,1536]{1,0:T(8,128)(2,1)S(1)}, u32[]{:S(2)}, u32[]{:S(2)}) collective-permute-start(bf16[48,1536]{1,0:T(8,128)(2,1)S(1)} %get-tuple-element.52), channel_id=1, source_target_pairs={{0,24},{4,28},{8,16},{12,20},{16,8},{20,12},{24,0},{28,4},{1,25},{... | collective-permute-start | bytes 442376 | tf_op jit(solution)/shard_map/ppermute | solution.py:37
  22.0 4.2 %collective-permute-start.6 = (bf16[48,1536]{1,0:T(8,128)(2,1)S(1)}, bf16[48,1536]{1,0:T(8,128)(2,1)S(1)}, u32[]{:S(2)}, u32[]{:S(2)}) collective-permute-start(bf16[48,1536]{1,0:T(8,128)(2,1)S(1)} %get-tuple-element.54), channel_id=1, source_target_pairs={{0,28},{4,24},{8,20},{12,16},{16,12},{20,8},{24,4},{28,0},{1,29},{... | collective-permute-start | bytes 442376 | tf_op jit(solution)/shard_map/ppermute | solution.py:37
  26.2 1.1 pad_maximum_fusion.refs_0_
  27.3 5.9 %collective-permute-done.4 = bf16[48,1536]{1,0:T(8,128)(2,1)} collective-permute-done((bf16[48,1536]{1,0:T(8,128)(2,1)S(1)}, bf16[48,1536]{1,0:T(8,128)(2,1)}, u32[]{:S(2)}, u32[]{:S(2)}) %collective-permute-start.4) | collective-permute-done | bytes 147488 | tf_op jit(solution)/shard_map/ppermute | solution.py:37
  33.9 8.5 %all-to-all-start = ((bf16[8,48,2048]{2,1,0:T(8,128)(2,1)}), bf16[8,48,2048]{2,1,0:T(8,128)(2,1)S(1)}, u32[]{:S(2)}, u32[]{:S(2)}) async-start(bf16[8,48,2048]{2,1,0:T(8,128)(2,1)} %bitcast.19), calls=%async_computation | async-start | bytes 3145728 | tf_op jit(solution)/shard_map/all_to_all | solution.py:374
  42.4 1.5 collective-permute-start.9
  43.9 0.9 constant_dynamic-update-slice_fusion.3
  44.9 0.9 constant_dynamic-update-slice_fusion.2
  45.8 0.9 constant_dynamic-update-slice_fusion.refs_1_
  47.8 10.9 %collective-permute-done.9.refs_4_ = bf16[192,1536]{1,0:T(8,128)(2,1)S(1)} collective-permute-done((bf16[192,1536]{1,0:T(8,128)(2,1)S(1)}, bf16[192,1536]{1,0:T(8,128)(2,1)S(1)}, u32[]{:S(2)}, u32[]{:S(2)}) %collective-permute-start.9) | collective-permute-done | bytes 589856 | tf_op jit(solution)/shard_map/ppermute | solution.py:37
  58.7 9.5 %collective-permute-done.10.refs_5_ = bf16[192,1536]{1,0:T(8,128)(2,1)S(1)} collective-permute-done((bf16[192,1536]{1,0:T(8,128)(2,1)S(1)}, bf16[192,1536]{1,0:T(8,128)(2,1)S(1)}, u32[]{:S(2)}, u32[]{:S(2)}) %collective-permute-start.10) | collective-permute-done | bytes 589856 | tf_op jit(solution)/shard_map/ppermute | solution.py:37
  68.2 2.0 %collective-permute-done.12.refs_7_ = bf16[192,1536]{1,0:T(8,128)(2,1)S(1)} collective-permute-done((bf16[192,1536]{1,0:T(8,128)(2,1)S(1)}, bf16[192,1536]{1,0:T(8,128)(2,1)S(1)}, u32[]{:S(2)}, u32[]{:S(2)}) %collective-permute-start.12) | collective-permute-done | bytes 589856 | tf_op jit(solution)/shard_map/ppermute | solution.py:37
  70.2 15.4 %back.1 = bf16[384,2048]{1,0:T(8,128)(2,1)S(1)} custom-call(s32[1]{0:T(128)} %bitcast.dp_ref, s32[1]{0:T(128)} %bitcast.1.hid_ref, bf16[192,1536]{1,0:T(8,128)(2,1)S(1)} %pad_maximum_fusion.refs_0_, bf16[192,1536]{1,0:T(8,128)(2,1)S(1)} %constant_dynamic-update-slice_fusion.refs_1_, bf16[192,1536]{1,0:T(8,128)(2,1)S(1)} %collective-permute-done.7.refs_2_, ...), custom_call_target="tpu_custom_call" | custom-call | flops 9663676 | bytes 31457 | tf_op jit(solution)/shard_map/back/pallas_call | solution.py:223
  85.6 1.1 copy-done.4
  88.3 0.8 copy-done.13
  89.2 0.9 copy-done.15
  90.9 0.8 copy-done.19
  92.5 5.7 %all-to-all-start.1 = ((bf16[8,48,2048]{2,1,0:T(8,128)(2,1)}), bf16[8,48,2048]{2,1,0:T(8,128)(2,1)}, u32[]{:S(2)}, u32[]{:S(2)}) async-start(bf16[8,48,2048]{2,1,0:T(8,128)(2,1)} %bitcast.18), calls=%async_computation.1 | async-start | bytes 3145728 | tf_op jit(solution)/shard_map/all_to_all | solution.py:374
  98.2 5.2 %down.4 = bf16[384,1536]{1,0:T(8,128)(2,1)S(1)} custom-call(s32[1]{0:T(128)} %bitcast.1.hid_ref, bf16[384,2048]{1,0:T(8,128)(2,1)S(1)} %bitcast.13, bf16[2048,6144]{1,0:T(8,128)(2,1)} %bitcast.27), custom_call_target="tpu_custom_call" | custom-call | flops 2415919 | bytes 9043 | tf_op jit(solution)/shard_map/down/pallas_call | solution.py:148
  103.5 5.2 %down.6 = bf16[384,1536]{1,0:T(8,128)(2,1)S(1)} custom-call(s32[1]{0:T(128)} %bitcast.1.hid_ref, bf16[384,2048]{1,0:T(8,128)(2,1)S(1)} %bitcast.14, bf16[2048,6144]{1,0:T(8,128)(2,1)} %bitcast.28), custom_call_target="tpu_custom_call" | custom-call | flops 2415919 | bytes 9043 | tf_op jit(solution)/shard_map/down/pallas_call | solution.py:148
  109.3 6.1 %down.5 = bf16[384,1536]{1,0:T(8,128)(2,1)} custom-call(s32[1]{0:T(128)} %bitcast.1.hid_ref, bf16[384,2048]{1,0:T(8,128)(2,1)S(1)} %bitcast.15, bf16[2048,6144]{1,0:T(8,128)(2,1)} %bitcast.29, bf16[384,1536]{1,0:T(8,128)(2,1)S(1)} %collective-permute-done.13.refs_0_), custom_call_target="tpu_custom_call" | custom-call | flops 2415919 | bytes 9043 | tf_op jit(solution)/shard_map/down/pallas_call | solution.py:148
  115.4 1.6 collective-permute-start.15
  117.0 5.3 %down.7.a_ref = f32[384,1536]{1,0:T(8,128)S(1)} custom-call(s32[1]{0:T(128)} %bitcast.1.hid_ref, bf16[384,2048]{1,0:T(8,128)(2,1)S(1)} %bitcast.16, bf16[2048,6144]{1,0:T(8,128)(2,1)} %bitcast.30, bf16[384,1536]{1,0:T(8,128)(2,1)S(1)} %collective-permute-done.14.refs_0_), custom_call_target="tpu_custom_call" | custom-call | flops 2415919 | bytes 10223 | tf_op jit(solution)/shard_map/down/pallas_call | solution.py:148
  122.3 1.4 copy-done.2
  123.7 17.0 %outer.1.refs_0_ = bf16[1,2048,6144]{2,1,0:T(8,128)(2,1)} custom-call(s32[1]{0:T(128)} %bitcast.dp_ref, s32[1]{0:T(128)} %bitcast.1.hid_ref, bf16[384,2048]{1,0:T(8,128)(2,1)S(1)} %bitcast.17, bf16[192,1536]{1,0:T(8,128)(2,1)S(1)} %pad_maximum_fusion.refs_0_, bf16[192,1536]{1,0:T(8,128)(2,1)S(1)} %copy-done.10, bf16[192,1536]{1,0:T(8,128)(2,1)S(1)} %copy-done.16, ...), custom_call_target="tpu_custom_call" | custom-call | flops 9663676 | bytes 31457 | tf_op jit(solution)/shard_map/outer/pallas_call | solution.py:261
  140.7 3.0 %collective-permute-done.15.b_ref = bf16[384,1536]{1,0:T(8,128)(2,1)} collective-permute-done((bf16[384,1536]{1,0:T(8,128)(2,1)}, bf16[384,1536]{1,0:T(8,128)(2,1)}, u32[]{:S(2)}, u32[]{:S(2)}) %collective-permute-start.15) | collective-permute-done | bytes 1179680 | tf_op jit(solution)/shard_map/ppermute | solution.py:37
  143.7 1.7 copy-done.3
  145.4 2.3 %sum_of.1 = bf16[384,1536]{1,0:T(8,128)(2,1)S(1)} custom-call(f32[384,1536]{1,0:T(8,128)S(1)} %copy-done.3, bf16[384,1536]{1,0:T(8,128)(2,1)} %collective-permute-done.15.b_ref), custom_call_target="tpu_custom_call" | custom-call | bytes 4718 | tf_op jit(solution)/shard_map/sum_of/pallas_call | solution.py:178
  147.7 1.1 copy-done.6
  148.8 6.1 %all-to-all-start.2 = ((bf16[8,48,1536]{2,1,0:T(8,128)(2,1)}), bf16[8,48,1536]{2,1,0:T(8,128)(2,1)S(1)}, u32[]{:S(2)}, u32[]{:S(2)}) async-start(bf16[8,48,1536]{2,1,0:T(8,128)(2,1)} %bitcast.21), calls=%async_computation.2 | async-start | bytes 2359296 | tf_op jit(solution)/shard_map/all_to_all | solution.py:374
  155.0 4.3 %grads.1 = (bf16[256,2048]{1,0:T(8,128)(2,1)S(1)}, bf16[256,2048]{1,0:T(8,128)(2,1)S(1)}, f32[256,1]{1,0:T(8,128)S(1)}) custom-call(s32[1,256]{1,0:T(1,128)S(1)} %reshape.42.key_ref, bf16[256,2048]{1,0:T(8,128)(2,1)S(1)} %reshape.43.gate_ref, bf16[256,2048]{1,0:T(8,128)(2,1)S(1)} %copy-done.1, bf16[384,2048]{1,0:T(8,128)(2,1)} %bitcast.9.back_ref), custom_call_target="tpu_custom_call" | custom-call | bytes 5767 | tf_op jit(solution)/shard_map/grads/pallas_call | solution.py:303
  159.3 1.0 copy-done.24
  160.3 1.0 copy-done.25
  161.6 1.2 collective-permute-done.16
  162.9 1.6 collective-permute-start.17
  164.5 1.7 reshape.45.refs_1_
  166.2 2.1 %reshape.46.refs_2_ = bf16[128,2,2048]{2,1,0:T(2,128)(2,1)S(1)} reshape(bf16[256,2048]{1,0:T(8,128)(2,1)} %copy-done.24) | data formatting | bytes 2097152 | tf_op jit(solution)/shard_map/reshape | solution.py:425
  169.2 13.9 %all-to-all-done.2 = bf16[8,48,1536]{2,1,0:T(8,128)(2,1)S(1)} async-done(((bf16[8,48,1536]{2,1,0:T(8,128)(2,1)}), bf16[8,48,1536]{2,1,0:T(8,128)(2,1)S(1)}, u32[]{:S(2)}, u32[]{:S(2)}) %all-to-all-start.2) | async-done | bytes 1179680 | tf_op jit(solution)/shard_map/all_to_all | solution.py:374
  183.1 1.6 mixed.1
  (85 shorter events, 10.0 us)
Async XLA Ops:
  0.6 1.4 copy-start.23
  3.4 9.8 %copy-start.29 = (bf16[128,2,2048]{2,1,0:T(2,128)(2,1)S(1)}, bf16[128,2,2048]{2,1,0:T(2,128)(2,1)}, u32[]{:S(2)}) copy-start(bf16[128,2,2048]{2,1,0:T(2,128)(2,1)} %param.6) | copy-start | bytes 3145732
  4.0 14.2 %collective-permute-start = (bf16[48,1536]{1,0:T(8,128)(2,1)S(1)}, bf16[48,1536]{1,0:T(8,128)(2,1)}, u32[]{:S(2)}, u32[]{:S(2)}) collective-permute-start(bf16[48,1536]{1,0:T(8,128)(2,1)S(1)} %get-tuple-element.41), channel_id=1, source_target_pairs={{0,4},{4,0},{8,12},{12,8},{16,20},{20,16},{24,28},{28,24},{1,5},{5... | collective-permute-start | bytes 442376 | tf_op jit(solution)/shard_map/ppermute | solution.py:37
  7.1 12.7 %collective-permute-start.1 = (bf16[48,1536]{1,0:T(8,128)(2,1)S(1)}, bf16[48,1536]{1,0:T(8,128)(2,1)}, u32[]{:S(2)}, u32[]{:S(2)}) collective-permute-start(bf16[48,1536]{1,0:T(8,128)(2,1)S(1)} %get-tuple-element.42), channel_id=1, source_target_pairs={{0,8},{4,12},{8,0},{12,4},{16,24},{20,28},{24,16},{28,20},{1,9},{5... | collective-permute-start | bytes 442376 | tf_op jit(solution)/shard_map/ppermute | solution.py:37
  8.6 11.5 %collective-permute-start.2 = (bf16[48,1536]{1,0:T(8,128)(2,1)S(1)}, bf16[48,1536]{1,0:T(8,128)(2,1)}, u32[]{:S(2)}, u32[]{:S(2)}) collective-permute-start(bf16[48,1536]{1,0:T(8,128)(2,1)S(1)} %get-tuple-element.43), channel_id=1, source_target_pairs={{0,12},{4,8},{8,4},{12,0},{16,28},{20,24},{24,20},{28,16},{1,13},{... | collective-permute-start | bytes 442376 | tf_op jit(solution)/shard_map/ppermute | solution.py:37
  8.6 18.6 %collective-permute-start.3 = (bf16[48,1536]{1,0:T(8,128)(2,1)S(1)}, bf16[48,1536]{1,0:T(8,128)(2,1)}, u32[]{:S(2)}, u32[]{:S(2)}) collective-permute-start(bf16[48,1536]{1,0:T(8,128)(2,1)S(1)} %get-tuple-element.49), channel_id=1, source_target_pairs={{0,16},{4,20},{8,24},{12,28},{16,0},{20,4},{24,8},{28,12},{1,17},{... | collective-permute-start | bytes 442376 | tf_op jit(solution)/shard_map/ppermute | solution.py:37
  11.6 21.6 %collective-permute-start.4 = (bf16[48,1536]{1,0:T(8,128)(2,1)S(1)}, bf16[48,1536]{1,0:T(8,128)(2,1)}, u32[]{:S(2)}, u32[]{:S(2)}) collective-permute-start(bf16[48,1536]{1,0:T(8,128)(2,1)S(1)} %get-tuple-element.50), channel_id=1, source_target_pairs={{0,20},{4,16},{8,28},{12,24},{16,4},{20,0},{24,12},{28,8},{1,21},{... | collective-permute-start | bytes 442376 | tf_op jit(solution)/shard_map/ppermute | solution.py:37
  15.1 1.9 %copy-start = (bf16[256,2048]{1,0:T(8,128)(2,1)}, bf16[256,2048]{1,0:T(8,128)(2,1)S(1)}, u32[]{:S(2)}) copy-start(bf16[256,2048]{1,0:T(8,128)(2,1)S(1)} %reshape.44.up_ref) | copy-start | bytes 3145732
  17.0 1.1 copy-start.5
  20.2 13.1 %collective-permute-start.5 = (bf16[48,1536]{1,0:T(8,128)(2,1)S(1)}, bf16[48,1536]{1,0:T(8,128)(2,1)S(1)}, u32[]{:S(2)}, u32[]{:S(2)}) collective-permute-start(bf16[48,1536]{1,0:T(8,128)(2,1)S(1)} %get-tuple-element.52), channel_id=1, source_target_pairs={{0,24},{4,28},{8,16},{12,20},{16,8},{20,12},{24,0},{28,4},{1,25},{... | collective-permute-start | bytes 442376 | tf_op jit(solution)/shard_map/ppermute | solution.py:37
  22.0 11.2 %collective-permute-start.6 = (bf16[48,1536]{1,0:T(8,128)(2,1)S(1)}, bf16[48,1536]{1,0:T(8,128)(2,1)S(1)}, u32[]{:S(2)}, u32[]{:S(2)}) collective-permute-start(bf16[48,1536]{1,0:T(8,128)(2,1)S(1)} %get-tuple-element.54), channel_id=1, source_target_pairs={{0,28},{4,24},{8,20},{12,16},{16,12},{20,8},{24,4},{28,0},{1,29},{... | collective-permute-start | bytes 442376 | tf_op jit(solution)/shard_map/ppermute | solution.py:37
  33.9 58.6 %all-to-all-start = ((bf16[8,48,2048]{2,1,0:T(8,128)(2,1)}), bf16[8,48,2048]{2,1,0:T(8,128)(2,1)S(1)}, u32[]{:S(2)}, u32[]{:S(2)}) async-start(bf16[8,48,2048]{2,1,0:T(8,128)(2,1)} %bitcast.19), calls=%async_computation | async-start | bytes 3145728 | tf_op jit(solution)/shard_map/all_to_all | solution.py:374
  42.4 16.3 %collective-permute-start.9 = (bf16[192,1536]{1,0:T(8,128)(2,1)S(1)}, bf16[192,1536]{1,0:T(8,128)(2,1)S(1)}, u32[]{:S(2)}, u32[]{:S(2)}) collective-permute-start(bf16[192,1536]{1,0:T(8,128)(2,1)S(1)} %pad_maximum_fusion.refs_0_), channel_id=1, source_target_pairs={{0,2},{1,3},{2,0},{3,1},{4,6},{5,7},{6,4},{7,5},{8,10},{9,11},{10,... | collective-permute-start | bytes 1769480 | tf_op jit(solution)/shard_map/ppermute | solution.py:37
  46.7 21.5 %collective-permute-start.10 = (bf16[192,1536]{1,0:T(8,128)(2,1)S(1)}, bf16[192,1536]{1,0:T(8,128)(2,1)S(1)}, u32[]{:S(2)}, u32[]{:S(2)}) collective-permute-start(bf16[192,1536]{1,0:T(8,128)(2,1)S(1)} %constant_dynamic-update-slice_fusion.refs_1_), channel_id=1, source_target_pairs={{0,2},{1,3},{2,0},{3,1},{4,6},{5,7},{6,4},{7,5},{8,10},{9,11},{10,... | collective-permute-start | bytes 1769480 | tf_op jit(solution)/shard_map/ppermute | solution.py:37
  47.3 20.9 %collective-permute-start.7 = (bf16[192,1536]{1,0:T(8,128)(2,1)S(1)}, bf16[192,1536]{1,0:T(8,128)(2,1)S(1)}, u32[]{:S(2)}, u32[]{:S(2)}) collective-permute-start(bf16[192,1536]{1,0:T(8,128)(2,1)S(1)} %pad_maximum_fusion.refs_0_), channel_id=1, source_target_pairs={{0,1},{1,0},{2,3},{3,2},{4,5},{5,4},{6,7},{7,6},{8,9},{9,8},{10,11... | collective-permute-start | bytes 1769480 | tf_op jit(solution)/shard_map/ppermute | solution.py:37
  47.3 20.9 %collective-permute-start.8 = (bf16[192,1536]{1,0:T(8,128)(2,1)S(1)}, bf16[192,1536]{1,0:T(8,128)(2,1)S(1)}, u32[]{:S(2)}, u32[]{:S(2)}) collective-permute-start(bf16[192,1536]{1,0:T(8,128)(2,1)S(1)} %constant_dynamic-update-slice_fusion.refs_1_), channel_id=1, source_target_pairs={{0,1},{1,0},{2,3},{3,2},{4,5},{5,4},{6,7},{7,6},{8,9},{9,8},{10,11... | collective-permute-start | bytes 1769480 | tf_op jit(solution)/shard_map/ppermute | solution.py:37
  58.7 9.5 %collective-permute-start.11 = (bf16[192,1536]{1,0:T(8,128)(2,1)S(1)}, bf16[192,1536]{1,0:T(8,128)(2,1)S(1)}, u32[]{:S(2)}, u32[]{:S(2)}) collective-permute-start(bf16[192,1536]{1,0:T(8,128)(2,1)S(1)} %collective-permute-done.9.refs_4_), channel_id=1, source_target_pairs={{0,1},{1,0},{2,3},{3,2},{4,5},{5,4},{6,7},{7,6},{8,9},{9,8},{10,11... | collective-permute-start | bytes 1769480 | tf_op jit(solution)/shard_map/ppermute | solution.py:37
  68.2 2.0 %collective-permute-start.12 = (bf16[192,1536]{1,0:T(8,128)(2,1)S(1)}, bf16[192,1536]{1,0:T(8,128)(2,1)S(1)}, u32[]{:S(2)}, u32[]{:S(2)}) collective-permute-start(bf16[192,1536]{1,0:T(8,128)(2,1)S(1)} %collective-permute-done.10.refs_5_), channel_id=1, source_target_pairs={{0,1},{1,0},{2,3},{3,2},{4,5},{5,4},{6,7},{7,6},{8,9},{9,8},{10,11... | collective-permute-start | bytes 1769480 | tf_op jit(solution)/shard_map/ppermute | solution.py:37
  85.6 1.2 copy-start.4
  86.7 0.8 copy-start.9
  88.3 0.8 copy-start.13
  89.2 0.9 copy-start.15
  90.1 0.8 copy-start.17
  90.9 0.8 copy-start.19
  91.7 0.8 copy-start.21
  92.5 48.2 %all-to-all-start.1 = ((bf16[8,48,2048]{2,1,0:T(8,128)(2,1)}), bf16[8,48,2048]{2,1,0:T(8,128)(2,1)}, u32[]{:S(2)}, u32[]{:S(2)}) async-start(bf16[8,48,2048]{2,1,0:T(8,128)(2,1)} %bitcast.18), calls=%async_computation.1 | async-start | bytes 3145728 | tf_op jit(solution)/shard_map/all_to_all | solution.py:374
  103.4 5.8 %collective-permute-start.13 = (bf16[384,1536]{1,0:T(8,128)(2,1)S(1)}, bf16[384,1536]{1,0:T(8,128)(2,1)S(1)}, u32[]{:S(2)}, u32[]{:S(2)}) collective-permute-start(bf16[384,1536]{1,0:T(8,128)(2,1)S(1)} %down.4), channel_id=1, source_target_pairs={{0,1},{1,0},{2,3},{3,2},{4,5},{5,4},{6,7},{7,6},{8,9},{9,8},{10,11... | collective-permute-start | bytes 3538952 | tf_op jit(solution)/shard_map/ppermute | solution.py:37
  108.7 8.3 %collective-permute-start.14 = (bf16[384,1536]{1,0:T(8,128)(2,1)S(1)}, bf16[384,1536]{1,0:T(8,128)(2,1)S(1)}, u32[]{:S(2)}, u32[]{:S(2)}) collective-permute-start(bf16[384,1536]{1,0:T(8,128)(2,1)S(1)} %down.6), channel_id=1, source_target_pairs={{0,1},{1,0},{2,3},{3,2},{4,5},{5,4},{6,7},{7,6},{8,9},{9,8},{10,11... | collective-permute-start | bytes 3538952 | tf_op jit(solution)/shard_map/ppermute | solution.py:37
  115.4 8.3 %copy-start.10 = (bf16[192,1536]{1,0:T(8,128)(2,1)S(1)}, bf16[192,1536]{1,0:T(8,128)(2,1)}, u32[]{:S(2)}) copy-start(bf16[192,1536]{1,0:T(8,128)(2,1)} %copy-done.9) | copy-start | bytes 1769476
  115.4 8.3 %copy-start.12 = (bf16[192,1536]{1,0:T(8,128)(2,1)S(1)}, bf16[192,1536]{1,0:T(8,128)(2,1)}, u32[]{:S(2)}) copy-start(bf16[192,1536]{1,0:T(8,128)(2,1)} %copy-done.11) | copy-start | bytes 1769476
  115.4 8.3 %copy-start.14 = (bf16[192,1536]{1,0:T(8,128)(2,1)S(1)}, bf16[192,1536]{1,0:T(8,128)(2,1)}, u32[]{:S(2)}) copy-start(bf16[192,1536]{1,0:T(8,128)(2,1)} %copy-done.13) | copy-start | bytes 1769476
  115.4 8.3 %copy-start.16 = (bf16[192,1536]{1,0:T(8,128)(2,1)S(1)}, bf16[192,1536]{1,0:T(8,128)(2,1)}, u32[]{:S(2)}) copy-start(bf16[192,1536]{1,0:T(8,128)(2,1)} %copy-done.15) | copy-start | bytes 1769476
  115.4 8.3 %copy-start.18 = (bf16[192,1536]{1,0:T(8,128)(2,1)S(1)}, bf16[192,1536]{1,0:T(8,128)(2,1)}, u32[]{:S(2)}) copy-start(bf16[192,1536]{1,0:T(8,128)(2,1)} %copy-done.17) | copy-start | bytes 1769476
  115.4 8.3 %copy-start.20 = (bf16[192,1536]{1,0:T(8,128)(2,1)S(1)}, bf16[192,1536]{1,0:T(8,128)(2,1)}, u32[]{:S(2)}) copy-start(bf16[192,1536]{1,0:T(8,128)(2,1)} %copy-done.19) | copy-start | bytes 1769476
  115.4 8.3 %copy-start.22 = (bf16[192,1536]{1,0:T(8,128)(2,1)S(1)}, bf16[192,1536]{1,0:T(8,128)(2,1)}, u32[]{:S(2)}) copy-start(bf16[192,1536]{1,0:T(8,128)(2,1)} %copy-done.21) | copy-start | bytes 1769476
  115.4 28.3 %collective-permute-start.15 = (bf16[384,1536]{1,0:T(8,128)(2,1)}, bf16[384,1536]{1,0:T(8,128)(2,1)}, u32[]{:S(2)}, u32[]{:S(2)}) collective-permute-start(bf16[384,1536]{1,0:T(8,128)(2,1)} %down.5), channel_id=1, source_target_pairs={{0,2},{1,3},{2,0},{3,1},{4,6},{5,7},{6,4},{7,5},{8,10},{9,11},{10,... | collective-permute-start | bytes 3538952 | tf_op jit(solution)/shard_map/ppermute | solution.py:37
  122.3 1.4 copy-start.2
  143.7 1.7 copy-start.3
  147.7 1.1 copy-start.6
  148.8 6.1 %copy-start.27 = (f32[128,2]{0,1:T(2,128)S(1)}, f32[128,2]{0,1:T(2,128)}, u32[]{:S(2)}) copy-start(f32[128,2]{0,1:T(2,128)} %param.9) | copy-start | bytes 3076
  148.8 6.2 %copy-start.1 = (bf16[256,2048]{1,0:T(8,128)(2,1)S(1)}, bf16[256,2048]{1,0:T(8,128)(2,1)}, u32[]{:S(2)}) copy-start(bf16[256,2048]{1,0:T(8,128)(2,1)} %copy-done) | copy-start | bytes 3145732
  148.8 34.3 %all-to-all-start.2 = ((bf16[8,48,1536]{2,1,0:T(8,128)(2,1)}), bf16[8,48,1536]{2,1,0:T(8,128)(2,1)S(1)}, u32[]{:S(2)}, u32[]{:S(2)}) async-start(bf16[8,48,1536]{2,1,0:T(8,128)(2,1)} %bitcast.21), calls=%async_computation.2 | async-start | bytes 2359296 | tf_op jit(solution)/shard_map/all_to_all | solution.py:374
  159.3 1.0 copy-start.24
  160.3 1.0 copy-start.25
  161.6 1.3 collective-permute-start.16
  162.9 5.5 %collective-permute-start.17 = (f32[128,2]{1,0:T(8,128)S(1)}, f32[128,2]{1,0:T(8,128)S(1)}, u32[]{:S(2)}, u32[]{:S(2)}) collective-permute-start(f32[128,2]{1,0:T(8,128)S(1)} %add.6), channel_id=1, source_target_pairs={{0,2},{1,3},{2,0},{3,1},{4,6},{5,7},{6,4},{7,5},{8,10},{9,11},{10,... | collective-permute-start | bytes 3080 | tf_op jit(solution)/shard_map/ppermute | solution.py:37
  166.2 16.9 %copy-start.7 = (bf16[128,2,2048]{2,1,0:T(2,128)(2,1)}, bf16[128,2,2048]{2,1,0:T(2,128)(2,1)S(1)}, u32[]{:S(2)}) copy-start(bf16[128,2,2048]{2,1,0:T(2,128)(2,1)S(1)} %reshape.45.refs_1_) | copy-start | bytes 3145732
  168.4 16.3 %copy-start.8 = (bf16[128,2,2048]{2,1,0:T(2,128)(2,1)}, bf16[128,2,2048]{2,1,0:T(2,128)(2,1)S(1)}, u32[]{:S(2)}) copy-start(bf16[128,2,2048]{2,1,0:T(2,128)(2,1)S(1)} %reshape.46.refs_2_) | copy-start | bytes 3145732
  (4 other events, 2.8 us)

commit v3 on v2

--- a/solution.py
+++ b/solution.py
@@ -13,6 +13,7 @@
 F32 = jnp.float32
 BF16 = jnp.bfloat16
 I32 = jnp.int32
+WIDE = pltpu.CompilerParams(vmem_limit_bytes=63 * 1024 * 1024)
 PARAMS = pltpu.CompilerParams(vmem_limit_bytes=40 * 1024 * 1024)
 ROWS = (((0,), (0,)), ((), ()))
 COLUMNS = (((1,), (1,)), ((), ()))
@@ -97,7 +98,7 @@
             out_specs=[whole(o) for o in outs] + [whole(key)],
         ),
         out_shape=outs + [key],
-        compiler_params=PARAMS,
+        compiler_params=WIDE,
         cost_estimate=cost(0, *outs),
         name="send_scaled",
     )(my_dp, my_hid, ids, weight, *[out_grad] * slices)
@@ -108,28 +109,33 @@
     return sig, (gate * sig * up).astype(BF16)
 
 
-def send_kernel(slices, key_ref, gate_ref, up_ref, o_ref):
+def send_kernel(slices, dp_ref, key_ref, gate_ref, up_ref, *o_refs):
     hidden = hidden_of(gate_ref[...].astype(F32), up_ref[...].astype(F32))[1]
-    table = ones(table_of(slices, key_ref[...]))
-    o_ref[...] = jnp.dot(table, hidden, preferred_element_type=F32).astype(BF16)
-
-
-def send_hidden(slices, slot_key, gate, up):
+    blocks = [block_table(dp_ref[0] ^ k, slices, key_ref[...]) for k in range(len(o_refs))]
+    table = ones(jnp.concatenate(blocks, axis=0))
+    rows = jnp.dot(table, hidden, preferred_element_type=F32).astype(BF16)
+    for k, o_ref in enumerate(o_refs):
+        o_ref[...] = rows[k * CAP : (k + 1) * CAP]
+
+
+def send_hidden(my_dp, slices, slot_key, gate, up):
     slots, depth = gate.shape
-    rows = CAP * E * slices
     block = 512
-    out = jax.ShapeDtypeStruct((rows, depth), BF16)
-    part = pl.BlockSpec((slots, block), lambda i: (0, i))
+    outs = [jax.ShapeDtypeStruct((CAP, depth), BF16)] * (E * slices)
+    part = pl.BlockSpec((slots, block), lambda i, d: (0, i))
     return pl.pallas_call(
         functools.partial(send_kernel, slices),
-        grid=(depth // block,),
-        in_specs=[whole(slot_key), part, part],
-        out_specs=pl.BlockSpec((rows, block), lambda i: (0, i)),
-        out_shape=out,
+        grid_spec=pltpu.PrefetchScalarGridSpec(
+            num_scalar_prefetch=1,
+            grid=(depth // block,),
+            in_specs=[whole(slot_key), part, part],
+            out_specs=[pl.BlockSpec((CAP, block), lambda i, d: (0, i)) for _ in outs],
+        ),
+        out_shape=outs,
         compiler_params=PARAMS,
-        cost_estimate=cost(0, gate, up, out),
+        cost_estimate=cost(0, gate, up, *outs),
         name="send_hidden",
-    )(slot_key, gate, up)
+    )(my_dp, slot_key, gate, up)
 
 
 def down_kernel(added, hid_ref, x_ref, w_ref, *refs):
@@ -140,7 +146,7 @@
     o_ref[...] = out.astype(o_ref.dtype)
 
 
-def down(my_hid, x, weights, q, quarter, dtype, *add):
+def down(my_hid, x, weights, q, quarter, dtype, params, *add):
     rows, depth = x.shape
     block = min(512, quarter)
     per = quarter // block
@@ -158,12 +164,46 @@
             out_specs=pl.BlockSpec((rows, block), lambda j, h: (0, j)),
         ),
         out_shape=out,
+        compiler_params=params,
+        cost_estimate=cost(
+            2 * rows * depth * quarter, x, out, jax.ShapeDtypeStruct((depth, quarter), BF16)
+        ),
+        name="down",
+    )(my_hid, x, weights, *add)
+
+
+def first_down_kernel(count, dp_ref, hid_ref, *refs):
+    blocks, w_ref, o_ref, x_ref = refs[:count], *refs[count:]
+
+    @pl.when(pl.program_id(0) == 0)
+    def _():
+        for k, b in enumerate(blocks):
+            x_ref[rows_of(dp_ref, k), :] = b[...]
+
+    o_ref[...] = jnp.dot(x_ref[...], w_ref[...], preferred_element_type=F32).astype(BF16)
+
+
+def first_down(my_dp, my_hid, blocks, weights, q, quarter):
+    rows, depth = CAP * len(blocks), blocks[0].shape[1]
+    block = min(512, quarter)
+    per = quarter // block
+    outs = [jax.ShapeDtypeStruct((rows, quarter), BF16), jax.ShapeDtypeStruct((rows, depth), BF16)]
+    return pl.pallas_call(
+        functools.partial(first_down_kernel, len(blocks)),
+        grid_spec=pltpu.PrefetchScalarGridSpec(
+            num_scalar_prefetch=2,
+            grid=(per,),
+            in_specs=[whole(b) for b in blocks]
+            + [pl.BlockSpec((depth, block), lambda j, d, h: (0, (h[0] ^ q) * per + j))],
+            out_specs=[pl.BlockSpec((rows, block), lambda j, d, h: (0, j)), whole(outs[1])],
+        ),
+        out_shape=outs,
         compiler_params=PARAMS,
         cost_estimate=cost(
-            2 * rows * depth * quarter, x, out, jax.ShapeDtypeStruct((depth, quarter), BF16)
-        ),
-        name="down",
-    )(my_hid, x, weights, *add)
+            2 * rows * depth * quarter, *outs, jax.ShapeDtypeStruct((depth, quarter), BF16)
+        ),
+        name="first_down",
+    )(my_dp, my_hid, *blocks, weights)
 
 
 def sum_kernel(a_ref, b_ref, o_ref):
@@ -181,18 +221,41 @@
         in_specs=[part, part],
         out_specs=part,
         out_shape=out,
-        compiler_params=PARAMS,
+        compiler_params=WIDE,
         cost_estimate=cost(0, a, b, out),
         name="sum_of",
     )(a, b)
+
+
+def stack_kernel(*refs):
+    *blocks, o_ref = refs
+    for k, b in enumerate(blocks):
+        o_ref[k * CAP : (k + 1) * CAP, :] = b[...]
+
+
+def stack(blocks):
+    out = jax.ShapeDtypeStruct((CAP * len(blocks), blocks[0].shape[1]), BF16)
+    return pl.pallas_call(
+        stack_kernel,
+        grid=(1,),
+        in_specs=[whole(b) for b in blocks],
+        out_specs=whole(out),
+        out_shape=out,
+        compiler_params=PARAMS,
+        cost_estimate=cost(0, out, out),
+        name="stack",
+    )(*blocks)
+
+
+def rows_of(dp_ref, k):
+    return pl.ds(pl.multiple_of((dp_ref[0] ^ k) * CAP, CAP), CAP)
 
 
 def in_order(dp_ref, halves, y_ref):
     per = halves[0].shape[0] // CAP
     for n, half in enumerate(halves):
         for k in range(per):
-            at = pl.multiple_of((dp_ref[0] ^ (n % 2 * per + k)) * CAP, CAP)
-            y_ref[n // 2, pl.ds(at, CAP), :] = half[k * CAP : (k + 1) * CAP, :]
+            y_ref[n // 2, rows_of(dp_ref, n % 2 * per + k), :] = half[k * CAP : (k + 1) * CAP, :]
 
 
 def quarter_at(hid_ref, q, quarter):
@@ -220,6 +283,7 @@
     depth, width = weights.shape
     block = 256
     out = jax.ShapeDtypeStruct((rows, depth), BF16)
+    y = jax.ShapeDtypeStruct((width // quarter, rows, quarter), BF16)
     return pl.pallas_call(
         back_kernel,
         grid_spec=pltpu.PrefetchScalarGridSpec(
@@ -227,23 +291,16 @@
             grid=(depth // block,),
             in_specs=[whole(p) for p in halves]
             + [pl.BlockSpec((block, width), lambda i, d, h: (i, 0))],
-            out_specs=pl.BlockSpec((rows, block), lambda i, d, h: (0, i)),
-            scratch_shapes=[pltpu.VMEM((width // quarter, rows, quarter), BF16)],
-        ),
-        out_shape=out,
+            out_specs=[pl.BlockSpec((rows, block), lambda i, d, h: (0, i)), whole(y)],
+        ),
+        out_shape=[out, y],
         compiler_params=PARAMS,
         cost_estimate=cost(2 * rows * depth * width, *halves, weights, out),
         name="back",
     )(my_dp, my_hid, *halves, weights)
 
 
-def outer_kernel(dp_ref, hid_ref, x_ref, *refs):
-    *halves, o_ref, y_ref = refs
-
-    @pl.when(pl.program_id(0) == 0)
-    def _():
-        in_order(dp_ref, halves, y_ref)
-
+def outer_kernel(hid_ref, x_ref, y_ref, o_ref):
     count, _, quarter = y_ref.shape
     x = x_ref[...]
     for q in range(count):
@@ -252,27 +309,24 @@
         ).astype(BF16)
 
 
-def outer(my_dp, my_hid, x, halves):
+def outer(my_hid, x, y):
     rows, depth = x.shape
-    quarter = halves[0].shape[1]
-    width = quarter * len(halves) // 2
+    width = y.shape[0] * y.shape[2]
     block = 256
     out = jax.ShapeDtypeStruct((1, depth, width), BF16)
     return pl.pallas_call(
         outer_kernel,
         grid_spec=pltpu.PrefetchScalarGridSpec(
-            num_scalar_prefetch=2,
+            num_scalar_prefetch=1,
             grid=(depth // block,),
-            in_specs=[pl.BlockSpec((rows, block), lambda i, d, h: (0, i))]
-            + [whole(p) for p in halves],
-            out_specs=pl.BlockSpec((1, block, width), lambda i, d, h: (0, i, 0)),
-            scratch_shapes=[pltpu.VMEM((width // quarter, rows, quarter), BF16)],
+            in_specs=[pl.BlockSpec((rows, block), lambda i, h: (0, i)), whole(y)],
+            out_specs=pl.BlockSpec((1, block, width), lambda i, h: (0, i, 0)),
         ),
         out_shape=out,
-        compiler_params=PARAMS,
-        cost_estimate=cost(2 * rows * depth * width, x, *halves, out),
+        compiler_params=WIDE,
+        cost_estimate=cost(2 * rows * depth * width, x, y, out),
         name="outer",
-    )(my_dp, my_hid, x, *halves)
+    )(my_hid, x, y)
 
 
 def grads_kernel(slices, key_ref, gate_ref, up_ref, back_ref, dgate_ref, dup_ref, dot_ref):
@@ -311,7 +365,7 @@
         ],
         out_specs=[part, part, whole(dots)],
         out_shape=[out, out, dots],
-        compiler_params=PARAMS,
+        compiler_params=WIDE,
         cost_estimate=cost(0, gate, up, got_back, out, out),
         name="grads",
     )(slot_key, gate, up, got_back)
@@ -376,44 +430,55 @@
     *scaled, slot_key = send_scaled(my_dp, my_hid, ids, weight, out_grad, slices, quarter)
     gate, up = gate_pre.reshape(slots, local_ff), up_pre.reshape(slots, local_ff)
     token_key = slot_key.T.reshape(1, slots)
-    hidden = send_hidden(slices, token_key, gate, up)
-
-    near, far = range(1, dp_count // 2), range(dp_count // 2, dp_count)
+    hidden = send_hidden(my_dp, slices, token_key, gate, up)
+
+    near, far = list(range(dp_count // 2 - 1, 0, -1)), list(range(dp_count - 1, dp_count // 2 - 1, -1))
     got = {0: scaled[0]}
-    for k in [*near, *far[:2]]:
+    for k in far[:2] + near:
         got[k] = swap(scaled[k], "dp", k)
-    for i, k in enumerate(far[2:]):
-        got[k] = swap(scaled[k], "dp", k, [got[near[i % len(near)]]])
-    halves = []
-    for part in ([0, *near], far):
-        blocks = lax.optimization_barrier(tuple(got[k] for k in part))
-        piece = {0: jnp.concatenate(blocks)}
-        if not halves:
-            piece[0], hidden = lax.optimization_barrier((piece[0], hidden))
-        bit = hid_count // 2
-        while bit:
+    for k, ahead in zip(far[2:], near * len(far)):
+        got[k] = swap(scaled[k], "dp", k, [got[ahead]])
+    own = [stack([got[k] for k in part]) for part in ([0, *near[::-1]], far[::-1])]
+    own[0] = lax.optimization_barrier((own[0], hidden))[0]
+    got_hidden = {0: hidden[0]}
+    for k, ahead in zip(far[:3], far[2:4] + far[3:4]):
+        got_hidden[k] = swap(hidden[k], "dp", k, [got[ahead]])
+    halves = [{0: x} for x in own]
+    bit = hid_count // 2
+    for piece in halves:
+        piece[bit] = swap(piece[0], "hid", bit)
+    while bit > 1:
+        bit //= 2
+        for piece in halves:
             for q in sorted(piece):
-                piece[q ^ bit] = swap(piece[q], "hid", bit)
-            bit //= 2
-        halves.append(piece)
-    hidden = lax.optimization_barrier((hidden, [got[k] for k in far]))[0]
-    got_hidden = over_dp(hidden)
+                if q ^ bit not in piece:
+                    ahead = [got_hidden[k] for k in far[:2]] if q and piece is halves[1] else []
+                    piece[q ^ bit] = swap(piece[q], "hid", bit, ahead)
+    got_hidden[near[0]] = swap(hidden[near[0]], "dp", near[0], [halves[1][1]])
+    for i, k in enumerate(far[3:] + near[1:]):
+        got_hidden[k] = swap(hidden[k], "dp", k, [got_hidden[far[min(i, 1)]]])
     halves = [piece[q] for q in range(hid_count) for piece in halves]
-    sent_back = back(my_dp, my_hid, halves, weights)
+    sent_back, y = back(my_dp, my_hid, halves, weights)
+    got_hidden = [got_hidden[k] for k in range(dp_count)]
     got_hidden, sent_back = lax.optimization_barrier((got_hidden, sent_back))
 
-    got_back = over_dp(sent_back)
-    sums = {}
+    sums, others = {}, []
     for q in range(hid_count - 1, 0, -2):
-        sums[q] = swap(down(my_hid, got_hidden, weights, q, quarter, BF16), "hid", 1)
-    others = []
-    for q in range(hid_count - 2, 0, -2):
-        made = down(my_hid, got_hidden, weights, q, quarter, BF16, sums[q ^ 1])
-        others.append(swap(made, "hid", q))
-    x = lax.optimization_barrier((got_hidden, made))[0]
-    total = down(my_hid, x, weights, 0, quarter, F32, sums[1])
+        if q == hid_count - 1:
+            made, x = first_down(my_dp, my_hid, got_hidden, weights, q, quarter)
+        else:
+            made = down(my_hid, x, weights, q, quarter, BF16, PARAMS)
+        sums[q] = swap(made, "hid", 1)
+        if q == hid_count - 1:
+            sent_back = lax.optimization_barrier((sent_back, made))[0]
+            got_back = over_dp(sent_back)
+        if q > 1:
+            made = down(my_hid, x, weights, q - 1, quarter, BF16, PARAMS, sums[q])
+            others.append(swap(made, "hid", q - 1))
+            x = lax.optimization_barrier((x, made))[0]
+    total = down(my_hid, x, weights, 0, quarter, F32, WIDE, sums[1])
     x = lax.optimization_barrier((x, total))[0]
-    weight_grad = outer(my_dp, my_hid, x, halves)
+    weight_grad = outer(my_hid, x, y)
     for other in others[1:]:
         total = total + other.astype(F32)
     total, got_back, weight_grad = lax.optimization_barrier((total, got_back, weight_grad))

time: 186 us -> 174 us (0.935)
  local copies, waits for them, and re-layouts: 27.5 us -> 9.17 us
  Pallas kernels: 64.8 us -> 77.2 us
  waiting for transfers between devices: 48.5 us -> 39.8 us
  starting transfers between devices: 41.7 us -> 44.7 us
    unnamed x67 -> x22, local copies, waits for them, and re-layouts: 20.4 us -> 0.93 us
    ppermute x18 -> x25, starting transfers between devices: 21.3 us -> 34.4 us  [swap(): return lax.ppermute(x, axis, [(i, i ^ bit) for i in range(count)])]
    all_to_all x3 -> x2, starting transfers between devices: 20.4 us -> 10.3 us  [over_dp(): return lax.all_to_all(x, 'dp', split_axis=0, concat_axis=0, tiled=True)]
    ppermute x18 -> x25, waiting for transfers between devices: 34.5 us -> 24.9 us  [swap(): return lax.ppermute(x, axis, [(i, i ^ bit) for i in range(count)])]
    pallas_call x1 -> x4, Pallas kernels: 1.9 us -> 8.98 us  [the longest x1 6.93 us: first_down(): pl.pallas_call(functools.partial(first_down_kernel, len(blocks)), grid_sp...]
    pallas_call x4 -> x3, Pallas kernels: 21.8 us -> 18.4 us  [down(): pl.pallas_call(functools.partial(down_kernel, len(add)), grid_spec=pltpu....]
    pallas_call x1, Pallas kernels: 0.62 us -> 2.56 us  [send_scaled(): pl.pallas_call(functools.partial(scale_kernel, slices), grid_spec=pltpu.P...]
    all_to_all x3 -> x2, waiting for transfers between devices: 13.9 us -> 14.9 us  [over_dp(): return lax.all_to_all(x, 'dp', split_axis=0, concat_axis=0, tiled=True)]
  transfers between devices with their start and end apart: 21 -> 27, of which waited for: 9 -> 10; matrix products, arithmetic and copies ran while one was open for 6% -> 6% of each run, Pallas kernels for 33% -> 35%
where the time goes in v3:
time: 174 us; the launch traced here: 173 us
  Pallas kernels  77.2 us (44%)
  starting transfers between devices  44.7 us (26%)
  waiting for transfers between devices  39.8 us (23%)
  local copies, waits for them, and re-layouts  9.17 us (5%)
    ppermute x25, starting transfers between devices, swap(): return lax.ppermute(x, axis, [(i, i ^ bit) for i in range(count)])  34.4 us
    ppermute x25, waiting for transfers between devices, swap(): return lax.ppermute(x, axis, [(i, i ^ bit) for i in range(count)])  24.9 us
    pallas_call x1, Pallas kernels, outer(): pl.pallas_call(outer_kernel, grid_spec=pltpu.PrefetchScalarGridSpec(num_s...  18.8 us
    pallas_call x3, Pallas kernels, down(): pl.pallas_call(functools.partial(down_kernel, len(add)), grid_spec=pltpu....  18.4 us
    pallas_call x1, Pallas kernels, back(): pl.pallas_call(back_kernel, grid_spec=pltpu.PrefetchScalarGridSpec(num_sc...  16.3 us
    all_to_all x2, waiting for transfers between devices, over_dp(): return lax.all_to_all(x, 'dp', split_axis=0, concat_axis=0, tiled=True)  14.9 us
    all_to_all x2, starting transfers between devices, over_dp(): return lax.all_to_all(x, 'dp', split_axis=0, concat_axis=0, tiled=True)  10.3 us
    pallas_call x1, Pallas kernels, first_down(): pl.pallas_call(functools.partial(first_down_kernel, len(blocks)), grid_sp...  6.93 us
  transfers between devices with their start and end apart: 27, of which 10 were waited for; matrix products, arithmetic and copies ran while one was open for 6% of the time, Pallas kernels for 35%

profile of v3, /device:TPU:0, one launch (start us, length us, event | category | flops | bytes accessed | tf_op | source)
XLA Modules:
  0.0 172.8 jit_solution(17191807415601279968)
XLA Ops:
  0.6 2.6 %send_scaled.1 = (bf16[48,1536]{1,0:T(8,128)(2,1)}, bf16[48,1536]{1,0:T(8,128)(2,1)}, bf16[48,1536]{1,0:T(8,128)(2,1)}, bf16[48,1536]{1,0:T(8,128)(2,1)}, bf16[4...) custom-call(s32[1]{0:T(128)} %bitcast.dp_ref, ...), custom_call_target="tpu_custom_call" | custom-call | bytes 1179 | tf_op jit(solution)/shard_map/send_scaled/pallas_call | solution.py:92
  3.2 3.0 %collective-permute-start = (bf16[48,1536]{1,0:T(8,128)(2,1)}, bf16[48,1536]{1,0:T(8,128)(2,1)S(1)}, u32[]{:S(2)}, u32[]{:S(2)}) collective-permute-start(bf16[48,1536]{1,0:T(8,128)(2,1)} %get-tuple-element.62), channel_id=1, source_target_pairs={{0,8},{4,12},{8,0},{12,4},{16,24},{20,28},{24,16},{28,20},{1,9},{5... | collective-permute-start | bytes 442376 | tf_op jit(solution)/shard_map/ppermute | solution.py:38
  6.2 1.4 collective-permute-start.5
  7.7 4.0 %collective-permute-start.7 = (bf16[48,1536]{1,0:T(8,128)(2,1)}, bf16[48,1536]{1,0:T(8,128)(2,1)S(1)}, u32[]{:S(2)}, u32[]{:S(2)}) collective-permute-start(bf16[48,1536]{1,0:T(8,128)(2,1)} %get-tuple-element.72), channel_id=1, source_target_pairs={{0,24},{4,28},{8,16},{12,20},{16,8},{20,12},{24,0},{28,4},{1,25},{... | collective-permute-start | bytes 442376 | tf_op jit(solution)/shard_map/ppermute | solution.py:38
  11.7 1.2 collective-permute-start.8
  12.9 1.0 collective-permute-start.1
  13.9 0.7 collective-permute-done.5.refs_3_
  14.7 3.8 %collective-permute-start.6 = (bf16[48,1536]{1,0:T(8,128)(2,1)}, bf16[48,1536]{1,0:T(8,128)(2,1)S(1)}, u32[]{:S(2)}, u32[]{:S(2)}) collective-permute-start(bf16[48,1536]{1,0:T(8,128)(2,1)} %get-tuple-element.71), channel_id=1, source_target_pairs={{0,20},{4,16},{8,28},{12,24},{16,4},{20,0},{24,12},{28,8},{1,21},{... | collective-permute-start | bytes 442376 | tf_op jit(solution)/shard_map/ppermute | solution.py:38
  18.5 0.8 copy.14
  19.4 1.5 reshape.41.gate_ref
  20.9 1.8 %reshape.42.up_ref = bf16[256,2048]{1,0:T(8,128)(2,1)S(1)} reshape(bf16[128,2,2048]{2,1,0:T(2,128)(2,1)} %param.7) | data formatting | bytes 2097152 | tf_op jit(solution)/shard_map/reshape | solution.py:431
  22.8 2.0 %send_hidden.1 = (bf16[48,2048]{1,0:T(8,128)(2,1)S(1)}, bf16[48,2048]{1,0:T(8,128)(2,1)S(1)}, bf16[48,2048]{1,0:T(8,128)(2,1)S(1)}, bf16[48,2048]{1,0:T(8,128)(2...) custom-call(s32[1]{0:T(128)} %bitcast.dp_ref, ...), custom_call_target="tpu_custom_call" | custom-call | bytes 3670 | tf_op jit(solution)/shard_map/send_hidden/pallas_call | solution.py:126
  24.9 1.6 collective-permute-start.16
  26.4 8.4 %collective-permute-done.1.refs_0_ = bf16[48,1536]{1,0:T(8,128)(2,1)S(1)} collective-permute-done((bf16[48,1536]{1,0:T(8,128)(2,1)}, bf16[48,1536]{1,0:T(8,128)(2,1)S(1)}, u32[]{:S(2)}, u32[]{:S(2)}) %collective-permute-start.1) | collective-permute-done | bytes 147488 | tf_op jit(solution)/shard_map/ppermute | solution.py:38
  34.8 2.4 %collective-permute-done.6.refs_1_ = bf16[48,1536]{1,0:T(8,128)(2,1)S(1)} collective-permute-done((bf16[48,1536]{1,0:T(8,128)(2,1)}, bf16[48,1536]{1,0:T(8,128)(2,1)S(1)}, u32[]{:S(2)}, u32[]{:S(2)}) %collective-permute-start.6) | collective-permute-done | bytes 147488 | tf_op jit(solution)/shard_map/ppermute | solution.py:38
  37.2 1.5 collective-permute-start.17
  38.8 3.3 %collective-permute-start.2 = (bf16[48,2048]{1,0:T(8,128)(2,1)S(1)}, bf16[48,2048]{1,0:T(8,128)(2,1)S(1)}, u32[]{:S(2)}, u32[]{:S(2)}) collective-permute-start(bf16[48,2048]{1,0:T(8,128)(2,1)S(1)} %get-tuple-element.64), channel_id=1, source_target_pairs={{0,24},{4,28},{8,16},{12,20},{16,8},{20,12},{24,0},{28,4},{1,25},{... | collective-permute-start | bytes 589832 | tf_op jit(solution)/shard_map/ppermute | solution.py:38
  42.1 0.9 collective-permute-start.11
  43.0 4.1 %collective-permute-done.2.refs_6_ = bf16[48,2048]{1,0:T(8,128)(2,1)S(1)} collective-permute-done((bf16[48,2048]{1,0:T(8,128)(2,1)S(1)}, bf16[48,2048]{1,0:T(8,128)(2,1)S(1)}, u32[]{:S(2)}, u32[]{:S(2)}) %collective-permute-start.2) | collective-permute-done | bytes 196640 | tf_op jit(solution)/shard_map/ppermute | solution.py:38
  47.1 0.5 collective-permute-start.18
  47.6 3.0 %collective-permute-done.11.refs_7_ = bf16[48,2048]{1,0:T(8,128)(2,1)S(1)} collective-permute-done((bf16[48,2048]{1,0:T(8,128)(2,1)S(1)}, bf16[48,2048]{1,0:T(8,128)(2,1)S(1)}, u32[]{:S(2)}, u32[]{:S(2)}) %collective-permute-start.11) | collective-permute-done | bytes 196640 | tf_op jit(solution)/shard_map/ppermute | solution.py:38
  50.6 0.4 collective-permute-done.17.refs_5_
  51.0 5.8 %collective-permute-start.13 = (bf16[48,2048]{1,0:T(8,128)(2,1)S(1)}, bf16[48,2048]{1,0:T(8,128)(2,1)S(1)}, u32[]{:S(2)}, u32[]{:S(2)}) collective-permute-start(bf16[48,2048]{1,0:T(8,128)(2,1)S(1)} %get-tuple-element.80), channel_id=1, source_target_pairs={{0,20},{4,16},{8,28},{12,24},{16,4},{20,0},{24,12},{28,8},{1,21},{... | collective-permute-start | bytes 589832 | tf_op jit(solution)/shard_map/ppermute | solution.py:38
  56.8 0.4 collective-permute-start.3
  57.2 3.1 %collective-permute-start.12 = (bf16[48,2048]{1,0:T(8,128)(2,1)S(1)}, bf16[48,2048]{1,0:T(8,128)(2,1)S(1)}, u32[]{:S(2)}, u32[]{:S(2)}) collective-permute-start(bf16[48,2048]{1,0:T(8,128)(2,1)S(1)} %get-tuple-element.78), channel_id=1, source_target_pairs={{0,16},{4,20},{8,24},{12,28},{16,0},{20,4},{24,8},{28,12},{1,17},{... | collective-permute-start | bytes 589832 | tf_op jit(solution)/shard_map/ppermute | solution.py:38
  60.3 16.3 %back.1 = (bf16[384,2048]{1,0:T(8,128)(2,1)}, bf16[4,384,1536]{2,1,0:T(8,128)(2,1)S(1)}) custom-call(s32[1]{0:T(128)} %bitcast.dp_ref, s32[1]{0:T(128)} %bitcast.1.hid_ref, bf16[192,1536]{1,0:T(8,128)(2,1)S(1)} %stack.3.refs_0_, bf16[192,1536]{1,0:T(8,128)(2,1)S(1)} %stack.2.refs_1_, bf16[192,1536]{1,0:T(8,128)(2,1)S(1)} %collective-permute-done.15.refs_2_, ...), custom_call_target="tpu_custom_call" | custom-call | flops 9663676 | bytes 31457 | tf_op jit(solution)/shard_map/back/pallas_call | solution.py:287
  76.7 6.9 %first_down.1 = (bf16[384,1536]{1,0:T(8,128)(2,1)S(1)}, bf16[384,2048]{1,0:T(8,128)(2,1)S(1)}) custom-call(s32[1]{0:T(128)} %bitcast.dp_ref, s32[1]{0:T(128)} %bitcast.1.hid_ref, bf16[48,2048]{1,0:T(8,128)(2,1)S(1)} %get-tuple-element.86.refs_0_, bf16[48,2048]{1,0:T(8,128)(2,1)S(1)} %collective-permute-done.3.refs_1_, ...), custom_call_target="tpu_custom_call" | custom-call | flops 2415919 | bytes 9043 | tf_op jit(solution)/shard_map/first_down/pallas_call | solution.py:191
  83.6 4.3 %all-to-all-start = ((bf16[8,48,2048]{2,1,0:T(8,128)(2,1)}), bf16[8,48,2048]{2,1,0:T(8,128)(2,1)}, u32[]{:S(2)}, u32[]{:S(2)}) async-start(bf16[8,48,2048]{2,1,0:T(8,128)(2,1)} %bitcast.6), calls=%async_computation | async-start | bytes 3145728 | tf_op jit(solution)/shard_map/all_to_all | solution.py:428
  88.0 2.8 %collective-permute-done.20.refs_0_ = bf16[384,1536]{1,0:T(8,128)(2,1)S(1)} collective-permute-done((bf16[384,1536]{1,0:T(8,128)(2,1)S(1)}, bf16[384,1536]{1,0:T(8,128)(2,1)S(1)}, u32[]{:S(2)}, u32[]{:S(2)}) %collective-permute-start.20) | collective-permute-done | bytes 1179680 | tf_op jit(solution)/shard_map/ppermute | solution.py:38
  90.9 6.1 %down.3 = bf16[384,1536]{1,0:T(8,128)(2,1)} custom-call(s32[1]{0:T(128)} %bitcast.1.hid_ref, bf16[384,2048]{1,0:T(8,128)(2,1)S(1)} %get-tuple-element.99.x_ref, bf16[2048,6144]{1,0:T(8,128)(2,1)} %bitcast.16, bf16[384,1536]{1,0:T(8,128)(2,1)S(1)} %collective-permute-done.20.refs_0_), custom_call_target="tpu_custom_call" | custom-call | flops 2415919 | bytes 9043 | tf_op jit(solution)/shard_map/down/pallas_call | solution.py:154
  97.0 5.2 %down.4 = bf16[384,1536]{1,0:T(8,128)(2,1)S(1)} custom-call(s32[1]{0:T(128)} %bitcast.1.hid_ref, bf16[384,2048]{1,0:T(8,128)(2,1)S(1)} %get-tuple-element.99.x_ref, bf16[2048,6144]{1,0:T(8,128)(2,1)} %bitcast.17), custom_call_target="tpu_custom_call" | custom-call | flops 2415919 | bytes 9043 | tf_op jit(solution)/shard_map/down/pallas_call | solution.py:154
  102.2 0.2 collective-permute-start.21
  102.4 1.1 collective-permute-start.22
  103.4 1.8 %collective-permute-done.21.refs_0_ = bf16[384,1536]{1,0:T(8,128)(2,1)} collective-permute-done((bf16[384,1536]{1,0:T(8,128)(2,1)S(1)}, bf16[384,1536]{1,0:T(8,128)(2,1)}, u32[]{:S(2)}, u32[]{:S(2)}) %collective-permute-start.21) | collective-permute-done | bytes 1179680 | tf_op jit(solution)/shard_map/ppermute | solution.py:38
  105.2 7.1 %down.5.a_ref = f32[384,1536]{1,0:T(8,128)} custom-call(s32[1]{0:T(128)} %bitcast.1.hid_ref, bf16[384,2048]{1,0:T(8,128)(2,1)} %copy-done, bf16[2048,6144]{1,0:T(8,128)(2,1)} %bitcast.18, bf16[384,1536]{1,0:T(8,128)(2,1)} %collective-permute-done.21.refs_0_), custom_call_target="tpu_custom_call" | custom-call | flops 2415919 | bytes 10223 | tf_op jit(solution)/shard_map/down/pallas_call | solution.py:154
  112.4 18.8 %outer.1.refs_0_ = bf16[1,2048,6144]{2,1,0:T(8,128)(2,1)} custom-call(s32[1]{0:T(128)} %bitcast.1.hid_ref, bf16[384,2048]{1,0:T(8,128)(2,1)} %copy-done, bf16[4,384,1536]{2,1,0:T(8,128)(2,1)} %copy-done.3), custom_call_target="tpu_custom_call" | custom-call | flops 9663676 | bytes 31457 | tf_op jit(solution)/shard_map/outer/pallas_call | solution.py:317
  131.2 3.8 %sum_of.1 = bf16[384,1536]{1,0:T(8,128)(2,1)} custom-call(f32[384,1536]{1,0:T(8,128)} %down.5.a_ref, bf16[384,1536]{1,0:T(8,128)(2,1)} %collective-permute-done.22.b_ref), custom_call_target="tpu_custom_call" | custom-call | bytes 4718 | tf_op jit(solution)/shard_map/sum_of/pallas_call | solution.py:218
  135.0 6.0 %all-to-all-start.1 = ((bf16[8,48,1536]{2,1,0:T(8,128)(2,1)}), bf16[8,48,1536]{2,1,0:T(8,128)(2,1)}, u32[]{:S(2)}, u32[]{:S(2)}) async-start(bf16[8,48,1536]{2,1,0:T(8,128)(2,1)} %bitcast.19), calls=%async_computation.1 | async-start | bytes 2359296 | tf_op jit(solution)/shard_map/all_to_all | solution.py:428
  141.1 5.4 %grads.1 = (bf16[256,2048]{1,0:T(8,128)(2,1)}, bf16[256,2048]{1,0:T(8,128)(2,1)}, f32[256,1]{1,0:T(8,128)}) custom-call(s32[1,256]{1,0:T(1,128)} %copy-done.8, bf16[256,2048]{1,0:T(8,128)(2,1)} %copy-done.1, bf16[256,2048]{1,0:T(8,128)(2,1)} %copy-done.2, bf16[384,2048]{1,0:T(8,128)(2,1)} %bitcast.7.back_ref), custom_call_target="tpu_custom_call" | custom-call | bytes 5767 | tf_op jit(solution)/shard_map/grads/pallas_call | solution.py:357
  146.5 1.0 reduce
  147.5 0.1 reshape.45
  147.8 1.2 collective-permute-done.23
  149.0 1.3 collective-permute-start.24
  150.3 1.7 %reshape.43.refs_1_ = bf16[128,2,2048]{2,1,0:T(2,128)(2,1)S(1)} reshape(bf16[256,2048]{1,0:T(8,128)(2,1)} %get-tuple-element.106) | data formatting | bytes 2097152 | tf_op jit(solution)/shard_map/reshape | solution.py:490
  152.1 2.1 %reshape.44.refs_2_ = bf16[128,2,2048]{2,1,0:T(2,128)(2,1)S(1)} reshape(bf16[256,2048]{1,0:T(8,128)(2,1)} %get-tuple-element.107) | data formatting | bytes 2097152 | tf_op jit(solution)/shard_map/reshape | solution.py:490
  154.2 0.8 copy.16
  155.0 14.9 %all-to-all-done.1 = bf16[8,48,1536]{2,1,0:T(8,128)(2,1)} async-done(((bf16[8,48,1536]{2,1,0:T(8,128)(2,1)}), bf16[8,48,1536]{2,1,0:T(8,128)(2,1)}, u32[]{:S(2)}, u32[]{:S(2)}) %all-to-all-start.1) | async-done | bytes 1179680 | tf_op jit(solution)/shard_map/all_to_all | solution.py:428
  169.9 2.8 %mixed.1 = bf16[1,128,1536]{2,1,0:T(8,128)(2,1)} custom-call(s32[2,128]{1,0:T(2,128)S(1)} %copy-done.9, f32[2,128]{1,0:T(2,128)S(1)} %bitcast.12, bf16[384,1536]{1,0:T(8,128)(2,1)} %bitcast.9.x_ref, bf16[1,2048,6144]{2,1,0:T(8,128)(2,1)} %outer.1.refs_0_, bf16[128,2,2048]{2,1,0:T(2,128)(2,1)S(1)} %reshape.43.refs_1_, ...), custom_call_target="tpu_custom_call" | custom-call | bytes 1572 | tf_op jit(solution)/shard_map/mixed/pallas_call | solution.py:401
  (52 shorter events, 0.9 us)
Async XLA Ops:
  3.2 9.7 %collective-permute-start = (bf16[48,1536]{1,0:T(8,128)(2,1)}, bf16[48,1536]{1,0:T(8,128)(2,1)S(1)}, u32[]{:S(2)}, u32[]{:S(2)}) collective-permute-start(bf16[48,1536]{1,0:T(8,128)(2,1)} %get-tuple-element.62), channel_id=1, source_target_pairs={{0,8},{4,12},{8,0},{12,4},{16,24},{20,28},{24,16},{28,20},{1,9},{5... | collective-permute-start | bytes 442376 | tf_op jit(solution)/shard_map/ppermute | solution.py:38
  6.2 8.4 %collective-permute-start.5 = (bf16[48,1536]{1,0:T(8,128)(2,1)}, bf16[48,1536]{1,0:T(8,128)(2,1)S(1)}, u32[]{:S(2)}, u32[]{:S(2)}) collective-permute-start(bf16[48,1536]{1,0:T(8,128)(2,1)} %get-tuple-element.70), channel_id=1, source_target_pairs={{0,12},{4,8},{8,4},{12,0},{16,28},{20,24},{24,20},{28,16},{1,13},{... | collective-permute-start | bytes 442376 | tf_op jit(solution)/shard_map/ppermute | solution.py:38
  7.6 17.1 %collective-permute-start.14 = (bf16[48,1536]{1,0:T(8,128)(2,1)}, bf16[48,1536]{1,0:T(8,128)(2,1)S(1)}, u32[]{:S(2)}, u32[]{:S(2)}) collective-permute-start(bf16[48,1536]{1,0:T(8,128)(2,1)} %get-tuple-element.82), channel_id=1, source_target_pairs={{0,4},{4,0},{8,12},{12,8},{16,20},{20,16},{24,28},{28,24},{1,5},{5... | collective-permute-start | bytes 442376 | tf_op jit(solution)/shard_map/ppermute | solution.py:38
  7.7 18.7 %collective-permute-start.7 = (bf16[48,1536]{1,0:T(8,128)(2,1)}, bf16[48,1536]{1,0:T(8,128)(2,1)S(1)}, u32[]{:S(2)}, u32[]{:S(2)}) collective-permute-start(bf16[48,1536]{1,0:T(8,128)(2,1)} %get-tuple-element.72), channel_id=1, source_target_pairs={{0,24},{4,28},{8,16},{12,20},{16,8},{20,12},{24,0},{28,4},{1,25},{... | collective-permute-start | bytes 442376 | tf_op jit(solution)/shard_map/ppermute | solution.py:38
  11.7 14.7 %collective-permute-start.8 = (bf16[48,1536]{1,0:T(8,128)(2,1)}, bf16[48,1536]{1,0:T(8,128)(2,1)S(1)}, u32[]{:S(2)}, u32[]{:S(2)}) collective-permute-start(bf16[48,1536]{1,0:T(8,128)(2,1)} %get-tuple-element.73), channel_id=1, source_target_pairs={{0,28},{4,24},{8,20},{12,16},{16,12},{20,8},{24,4},{28,0},{1,29},{... | collective-permute-start | bytes 442376 | tf_op jit(solution)/shard_map/ppermute | solution.py:38
  12.9 21.9 %collective-permute-start.1 = (bf16[48,1536]{1,0:T(8,128)(2,1)}, bf16[48,1536]{1,0:T(8,128)(2,1)S(1)}, u32[]{:S(2)}, u32[]{:S(2)}) collective-permute-start(bf16[48,1536]{1,0:T(8,128)(2,1)} %get-tuple-element.63), channel_id=1, source_target_pairs={{0,16},{4,20},{8,24},{12,28},{16,0},{20,4},{24,8},{28,12},{1,17},{... | collective-permute-start | bytes 442376 | tf_op jit(solution)/shard_map/ppermute | solution.py:38
  14.7 22.5 %collective-permute-start.6 = (bf16[48,1536]{1,0:T(8,128)(2,1)}, bf16[48,1536]{1,0:T(8,128)(2,1)S(1)}, u32[]{:S(2)}, u32[]{:S(2)}) collective-permute-start(bf16[48,1536]{1,0:T(8,128)(2,1)} %get-tuple-element.71), channel_id=1, source_target_pairs={{0,20},{4,16},{8,28},{12,24},{16,4},{20,0},{24,12},{28,8},{1,21},{... | collective-permute-start | bytes 442376 | tf_op jit(solution)/shard_map/ppermute | solution.py:38
  19.4 3.4 %copy-start.8 = (s32[1,256]{1,0:T(1,128)}, s32[1,256]{1,0:T(1,128)S(1)}, u32[]{:S(2)}) copy-start(s32[1,256]{1,0:T(1,128)S(1)} %reshape.40.key_ref) | copy-start | bytes 3076
  20.9 3.9 %copy-start.1 = (bf16[256,2048]{1,0:T(8,128)(2,1)}, bf16[256,2048]{1,0:T(8,128)(2,1)S(1)}, u32[]{:S(2)}) copy-start(bf16[256,2048]{1,0:T(8,128)(2,1)S(1)} %reshape.41.gate_ref) | copy-start | bytes 3145732
  22.8 2.1 %copy-start.2 = (bf16[256,2048]{1,0:T(8,128)(2,1)}, bf16[256,2048]{1,0:T(8,128)(2,1)S(1)}, u32[]{:S(2)}) copy-start(bf16[256,2048]{1,0:T(8,128)(2,1)S(1)} %reshape.42.up_ref) | copy-start | bytes 3145732
  22.8 2.0 %copy-start.6 = (bf16[48,1536]{1,0:T(8,128)(2,1)S(1)}, bf16[48,1536]{1,0:T(8,128)(2,1)}, u32[]{:S(2)}) copy-start(bf16[48,1536]{1,0:T(8,128)(2,1)} %get-tuple-element.81.refs_0_) | copy-start | bytes 442372
  24.9 22.2 %collective-permute-start.16 = (bf16[192,1536]{1,0:T(8,128)(2,1)S(1)}, bf16[192,1536]{1,0:T(8,128)(2,1)S(1)}, u32[]{:S(2)}, u32[]{:S(2)}) collective-permute-start(bf16[192,1536]{1,0:T(8,128)(2,1)S(1)} %stack.3.refs_0_), channel_id=1, source_target_pairs={{0,2},{1,3},{2,0},{3,1},{4,6},{5,7},{6,4},{7,5},{8,10},{9,11},{10,... | collective-permute-start | bytes 1769480 | tf_op jit(solution)/shard_map/ppermute | solution.py:38
  37.2 13.7 %collective-permute-start.17 = (bf16[192,1536]{1,0:T(8,128)(2,1)S(1)}, bf16[192,1536]{1,0:T(8,128)(2,1)S(1)}, u32[]{:S(2)}, u32[]{:S(2)}) collective-permute-start(bf16[192,1536]{1,0:T(8,128)(2,1)S(1)} %stack.2.refs_1_), channel_id=1, source_target_pairs={{0,2},{1,3},{2,0},{3,1},{4,6},{5,7},{6,4},{7,5},{8,10},{9,11},{10,... | collective-permute-start | bytes 1769480 | tf_op jit(solution)/shard_map/ppermute | solution.py:38
  38.8 8.3 %collective-permute-start.2 = (bf16[48,2048]{1,0:T(8,128)(2,1)S(1)}, bf16[48,2048]{1,0:T(8,128)(2,1)S(1)}, u32[]{:S(2)}, u32[]{:S(2)}) collective-permute-start(bf16[48,2048]{1,0:T(8,128)(2,1)S(1)} %get-tuple-element.64), channel_id=1, source_target_pairs={{0,24},{4,28},{8,16},{12,20},{16,8},{20,12},{24,0},{28,4},{1,25},{... | collective-permute-start | bytes 589832 | tf_op jit(solution)/shard_map/ppermute | solution.py:38
  42.1 8.5 %collective-permute-start.11 = (bf16[48,2048]{1,0:T(8,128)(2,1)S(1)}, bf16[48,2048]{1,0:T(8,128)(2,1)S(1)}, u32[]{:S(2)}, u32[]{:S(2)}) collective-permute-start(bf16[48,2048]{1,0:T(8,128)(2,1)S(1)} %get-tuple-element.77), channel_id=1, source_target_pairs={{0,28},{4,24},{8,20},{12,16},{16,12},{20,8},{24,4},{28,0},{1,29},{... | collective-permute-start | bytes 589832 | tf_op jit(solution)/shard_map/ppermute | solution.py:38
  43.0 13.7 %collective-permute-start.9 = (bf16[192,1536]{1,0:T(8,128)(2,1)S(1)}, bf16[192,1536]{1,0:T(8,128)(2,1)S(1)}, u32[]{:S(2)}, u32[]{:S(2)}) collective-permute-start(bf16[192,1536]{1,0:T(8,128)(2,1)S(1)} %stack.2.refs_1_), channel_id=1, source_target_pairs={{0,1},{1,0},{2,3},{3,2},{4,5},{5,4},{6,7},{7,6},{8,9},{9,8},{10,11... | collective-permute-start | bytes 1769480 | tf_op jit(solution)/shard_map/ppermute | solution.py:38
  47.1 10.1 %collective-permute-start.15 = (bf16[192,1536]{1,0:T(8,128)(2,1)S(1)}, bf16[192,1536]{1,0:T(8,128)(2,1)S(1)}, u32[]{:S(2)}, u32[]{:S(2)}) collective-permute-start(bf16[192,1536]{1,0:T(8,128)(2,1)S(1)} %stack.3.refs_0_), channel_id=1, source_target_pairs={{0,1},{1,0},{2,3},{3,2},{4,5},{5,4},{6,7},{7,6},{8,9},{9,8},{10,11... | collective-permute-start | bytes 1769480 | tf_op jit(solution)/shard_map/ppermute | solution.py:38
  47.1 10.1 %collective-permute-start.18 = (bf16[192,1536]{1,0:T(8,128)(2,1)S(1)}, bf16[192,1536]{1,0:T(8,128)(2,1)S(1)}, u32[]{:S(2)}, u32[]{:S(2)}) collective-permute-start(bf16[192,1536]{1,0:T(8,128)(2,1)S(1)} %collective-permute-done.16.refs_4_), channel_id=1, source_target_pairs={{0,1},{1,0},{2,3},{3,2},{4,5},{5,4},{6,7},{7,6},{8,9},{9,8},{10,11... | collective-permute-start | bytes 1769480 | tf_op jit(solution)/shard_map/ppermute | solution.py:38
  51.0 9.2 %collective-permute-start.19 = (bf16[192,1536]{1,0:T(8,128)(2,1)S(1)}, bf16[192,1536]{1,0:T(8,128)(2,1)S(1)}, u32[]{:S(2)}, u32[]{:S(2)}) collective-permute-start(bf16[192,1536]{1,0:T(8,128)(2,1)S(1)} %collective-permute-done.17.refs_5_), channel_id=1, source_target_pairs={{0,1},{1,0},{2,3},{3,2},{4,5},{5,4},{6,7},{7,6},{8,9},{9,8},{10,11... | collective-permute-start | bytes 1769480 | tf_op jit(solution)/shard_map/ppermute | solution.py:38
  51.0 25.7 %collective-permute-start.13 = (bf16[48,2048]{1,0:T(8,128)(2,1)S(1)}, bf16[48,2048]{1,0:T(8,128)(2,1)S(1)}, u32[]{:S(2)}, u32[]{:S(2)}) collective-permute-start(bf16[48,2048]{1,0:T(8,128)(2,1)S(1)} %get-tuple-element.80), channel_id=1, source_target_pairs={{0,20},{4,16},{8,28},{12,24},{16,4},{20,0},{24,12},{28,8},{1,21},{... | collective-permute-start | bytes 589832 | tf_op jit(solution)/shard_map/ppermute | solution.py:38
  56.8 19.9 %collective-permute-start.3 = (bf16[48,2048]{1,0:T(8,128)(2,1)S(1)}, bf16[48,2048]{1,0:T(8,128)(2,1)S(1)}, u32[]{:S(2)}, u32[]{:S(2)}) collective-permute-start(bf16[48,2048]{1,0:T(8,128)(2,1)S(1)} %get-tuple-element.65), channel_id=1, source_target_pairs={{0,4},{4,0},{8,12},{12,8},{16,20},{20,16},{24,28},{28,24},{1,5},{5... | collective-permute-start | bytes 589832 | tf_op jit(solution)/shard_map/ppermute | solution.py:38
  57.1 19.5 %collective-permute-start.4 = (bf16[48,2048]{1,0:T(8,128)(2,1)S(1)}, bf16[48,2048]{1,0:T(8,128)(2,1)S(1)}, u32[]{:S(2)}, u32[]{:S(2)}) collective-permute-start(bf16[48,2048]{1,0:T(8,128)(2,1)S(1)} %get-tuple-element.67), channel_id=1, source_target_pairs={{0,8},{4,12},{8,0},{12,4},{16,24},{20,28},{24,16},{28,20},{1,9},{5... | collective-permute-start | bytes 589832 | tf_op jit(solution)/shard_map/ppermute | solution.py:38
  57.2 19.5 %collective-permute-start.12 = (bf16[48,2048]{1,0:T(8,128)(2,1)S(1)}, bf16[48,2048]{1,0:T(8,128)(2,1)S(1)}, u32[]{:S(2)}, u32[]{:S(2)}) collective-permute-start(bf16[48,2048]{1,0:T(8,128)(2,1)S(1)} %get-tuple-element.78), channel_id=1, source_target_pairs={{0,16},{4,20},{8,24},{12,28},{16,0},{20,4},{24,8},{28,12},{1,17},{... | collective-permute-start | bytes 589832 | tf_op jit(solution)/shard_map/ppermute | solution.py:38
  60.2 16.5 %collective-permute-start.10 = (bf16[48,2048]{1,0:T(8,128)(2,1)S(1)}, bf16[48,2048]{1,0:T(8,128)(2,1)S(1)}, u32[]{:S(2)}, u32[]{:S(2)}) collective-permute-start(bf16[48,2048]{1,0:T(8,128)(2,1)S(1)} %get-tuple-element.74), channel_id=1, source_target_pairs={{0,12},{4,8},{8,4},{12,0},{16,28},{20,24},{24,20},{28,16},{1,13},{... | collective-permute-start | bytes 589832 | tf_op jit(solution)/shard_map/ppermute | solution.py:38
  76.6 7.0 %copy-start.3 = (bf16[4,384,1536]{2,1,0:T(8,128)(2,1)}, bf16[4,384,1536]{2,1,0:T(8,128)(2,1)S(1)}, u32[]{:S(2)}) copy-start(bf16[4,384,1536]{2,1,0:T(8,128)(2,1)S(1)} %get-tuple-element.100.y_ref) | copy-start | bytes 14155780
  83.6 13.3 %copy-start = (bf16[384,2048]{1,0:T(8,128)(2,1)}, bf16[384,2048]{1,0:T(8,128)(2,1)S(1)}, u32[]{:S(2)}) copy-start(bf16[384,2048]{1,0:T(8,128)(2,1)S(1)} %get-tuple-element.99.x_ref) | copy-start | bytes 4718596
  83.6 47.5 %all-to-all-start = ((bf16[8,48,2048]{2,1,0:T(8,128)(2,1)}), bf16[8,48,2048]{2,1,0:T(8,128)(2,1)}, u32[]{:S(2)}, u32[]{:S(2)}) async-start(bf16[8,48,2048]{2,1,0:T(8,128)(2,1)} %bitcast.6), calls=%async_computation | async-start | bytes 3145728 | tf_op jit(solution)/shard_map/all_to_all | solution.py:428
  87.9 2.9 %collective-permute-start.20 = (bf16[384,1536]{1,0:T(8,128)(2,1)S(1)}, bf16[384,1536]{1,0:T(8,128)(2,1)S(1)}, u32[]{:S(2)}, u32[]{:S(2)}) collective-permute-start(bf16[384,1536]{1,0:T(8,128)(2,1)S(1)} %get-tuple-element.95), channel_id=1, source_target_pairs={{0,1},{1,0},{2,3},{3,2},{4,5},{5,4},{6,7},{7,6},{8,9},{9,8},{10,11... | collective-permute-start | bytes 3538952 | tf_op jit(solution)/shard_map/ppermute | solution.py:38
  102.2 3.0 %collective-permute-start.21 = (bf16[384,1536]{1,0:T(8,128)(2,1)S(1)}, bf16[384,1536]{1,0:T(8,128)(2,1)}, u32[]{:S(2)}, u32[]{:S(2)}) collective-permute-start(bf16[384,1536]{1,0:T(8,128)(2,1)S(1)} %down.4), channel_id=1, source_target_pairs={{0,1},{1,0},{2,3},{3,2},{4,5},{5,4},{6,7},{7,6},{8,9},{9,8},{10,11... | collective-permute-start | bytes 3538952 | tf_op jit(solution)/shard_map/ppermute | solution.py:38
  102.4 28.8 %collective-permute-start.22 = (bf16[384,1536]{1,0:T(8,128)(2,1)}, bf16[384,1536]{1,0:T(8,128)(2,1)}, u32[]{:S(2)}, u32[]{:S(2)}) collective-permute-start(bf16[384,1536]{1,0:T(8,128)(2,1)} %down.3), channel_id=1, source_target_pairs={{0,2},{1,3},{2,0},{3,1},{4,6},{5,7},{6,4},{7,5},{8,10},{9,11},{10,... | collective-permute-start | bytes 3538952 | tf_op jit(solution)/shard_map/ppermute | solution.py:38
  135.0 6.0 %copy-start.7 = (f32[128,2]{0,1:T(2,128)S(1)}, f32[128,2]{0,1:T(2,128)}, u32[]{:S(2)}) copy-start(f32[128,2]{0,1:T(2,128)} %param.9) | copy-start | bytes 3076
  135.0 35.0 %all-to-all-start.1 = ((bf16[8,48,1536]{2,1,0:T(8,128)(2,1)}), bf16[8,48,1536]{2,1,0:T(8,128)(2,1)}, u32[]{:S(2)}, u32[]{:S(2)}) async-start(bf16[8,48,1536]{2,1,0:T(8,128)(2,1)} %bitcast.19), calls=%async_computation.1 | async-start | bytes 2359296 | tf_op jit(solution)/shard_map/all_to_all | solution.py:428
  147.7 1.3 collective-permute-start.23
  149.0 5.2 %collective-permute-start.24 = (f32[128,2]{1,0:T(8,128)S(1)}, f32[128,2]{1,0:T(8,128)S(1)}, u32[]{:S(2)}, u32[]{:S(2)}) collective-permute-start(f32[128,2]{1,0:T(8,128)S(1)} %add.6), channel_id=1, source_target_pairs={{0,2},{1,3},{2,0},{3,1},{4,6},{5,7},{6,4},{7,5},{8,10},{9,11},{10,... | collective-permute-start | bytes 3080 | tf_op jit(solution)/shard_map/ppermute | solution.py:38
  152.1 20.7 %copy-start.4 = (bf16[128,2,2048]{2,1,0:T(2,128)(2,1)}, bf16[128,2,2048]{2,1,0:T(2,128)(2,1)S(1)}, u32[]{:S(2)}) copy-start(bf16[128,2,2048]{2,1,0:T(2,128)(2,1)S(1)} %reshape.43.refs_1_) | copy-start | bytes 3145732
  152.1 17.9 %copy-start.9 = (s32[2,128]{1,0:T(2,128)S(1)}, s32[2,128]{1,0:T(2,128)}, u32[]{:S(2)}) copy-start(s32[2,128]{1,0:T(2,128)} %get-tuple-element.57.key_ref) | copy-start | bytes 3076
  154.2 18.6 %copy-start.5 = (bf16[128,2,2048]{2,1,0:T(2,128)(2,1)}, bf16[128,2,2048]{2,1,0:T(2,128)(2,1)S(1)}, u32[]{:S(2)}) copy-start(bf16[128,2,2048]{2,1,0:T(2,128)(2,1)S(1)} %reshape.44.refs_2_) | copy-start | bytes 3145732

commit v4 on v3

--- a/solution.py
+++ b/solution.py
@@ -212,12 +212,12 @@
 
 def sum_of(a, b):
     rows, width = a.shape
-    block = min(512, width)
-    part = pl.BlockSpec((rows, block), lambda i: (0, i))
+    block = 2 * CAP
+    part = pl.BlockSpec((block, width), lambda i: (i, 0))
     out = jax.ShapeDtypeStruct((rows, width), BF16)
     return pl.pallas_call(
         sum_kernel,
-        grid=(width // block,),
+        grid=(rows // block,),
         in_specs=[part, part],
         out_specs=part,
         out_shape=out,
@@ -440,13 +440,13 @@
         got[k] = swap(scaled[k], "dp", k, [got[ahead]])
     own = [stack([got[k] for k in part]) for part in ([0, *near[::-1]], far[::-1])]
     own[0] = lax.optimization_barrier((own[0], hidden))[0]
-    got_hidden = {0: hidden[0]}
-    for k, ahead in zip(far[:3], far[2:4] + far[3:4]):
-        got_hidden[k] = swap(hidden[k], "dp", k, [got[ahead]])
     halves = [{0: x} for x in own]
     bit = hid_count // 2
     for piece in halves:
         piece[bit] = swap(piece[0], "hid", bit)
+    got_hidden = {0: hidden[0]}
+    for k, ahead in zip(far[:3], (got[far[2]], got[far[3]], got[far[3]])):
+        got_hidden[k] = swap(hidden[k], "dp", k, [ahead])
     while bit > 1:
         bit //= 2
         for piece in halves:
@@ -462,20 +462,19 @@
     got_hidden = [got_hidden[k] for k in range(dp_count)]
     got_hidden, sent_back = lax.optimization_barrier((got_hidden, sent_back))
 
+    got_back = over_dp(sent_back)
     sums, others = {}, []
     for q in range(hid_count - 1, 0, -2):
-        if q == hid_count - 1:
+        if not sums:
             made, x = first_down(my_dp, my_hid, got_hidden, weights, q, quarter)
         else:
             made = down(my_hid, x, weights, q, quarter, BF16, PARAMS)
         sums[q] = swap(made, "hid", 1)
-        if q == hid_count - 1:
-            sent_back = lax.optimization_barrier((sent_back, made))[0]
-            got_back = over_dp(sent_back)
-        if q > 1:
-            made = down(my_hid, x, weights, q - 1, quarter, BF16, PARAMS, sums[q])
-            others.append(swap(made, "hid", q - 1))
-            x = lax.optimization_barrier((x, made))[0]
+    x = lax.optimization_barrier((x, made))[0]
+    for q in range(hid_count - 2, 0, -2):
+        made = down(my_hid, x, weights, q, quarter, BF16, PARAMS, sums[q + 1])
+        others.append(swap(made, "hid", q))
+    x = lax.optimization_barrier((x, made))[0]
     total = down(my_hid, x, weights, 0, quarter, F32, WIDE, sums[1])
     x = lax.optimization_barrier((x, total))[0]
     weight_grad = outer(my_hid, x, y)

time: 174 us -> 171 us (0.983)
  waiting for transfers between devices: 39.8 us -> 36.3 us
  local copies, waits for them, and re-layouts: 9.17 us -> 11.3 us
    ppermute x25, waiting for transfers between devices: 24.9 us -> 21.8 us  [swap(): return lax.ppermute(x, axis, [(i, i ^ bit) for i in range(count)])]
    unnamed x22, local copies, waits for them, and re-layouts: 0.93 us -> 3.06 us
  transfers between devices with their start and end apart: 27 -> 27, of which waited for: 10 -> 9; matrix products, arithmetic and copies ran while one was open for 6% -> 6% of each run, Pallas kernels for 35% -> 39%
where the time goes in v4:
time: 171 us; the launch traced here: 170 us
  Pallas kernels  76.2 us (45%)
  starting transfers between devices  44.6 us (26%)
  waiting for transfers between devices  36.3 us (21%)
  local copies, waits for them, and re-layouts  11.3 us (7%)
    ppermute x25, starting transfers between devices, swap(): return lax.ppermute(x, axis, [(i, i ^ bit) for i in range(count)])  34.3 us
    ppermute x25, waiting for transfers between devices, swap(): return lax.ppermute(x, axis, [(i, i ^ bit) for i in range(count)])  21.8 us
    pallas_call x3, Pallas kernels, down(): pl.pallas_call(functools.partial(down_kernel, len(add)), grid_spec=pltpu....  19 us
    pallas_call x1, Pallas kernels, outer(): pl.pallas_call(outer_kernel, grid_spec=pltpu.PrefetchScalarGridSpec(num_s...  18.8 us
    pallas_call x1, Pallas kernels, back(): pl.pallas_call(back_kernel, grid_spec=pltpu.PrefetchScalarGridSpec(num_sc...  16.3 us
    all_to_all x2, waiting for transfers between devices, over_dp(): return lax.all_to_all(x, 'dp', split_axis=0, concat_axis=0, tiled=True)  14.5 us
    all_to_all x2, starting transfers between devices, over_dp(): return lax.all_to_all(x, 'dp', split_axis=0, concat_axis=0, tiled=True)  10.3 us
    pallas_call x1, Pallas kernels, grads(): pl.pallas_call(functools.partial(grads_kernel, slices), grid=(depth // bl...  5.45 us
  transfers between devices with their start and end apart: 27, of which 9 were waited for; matrix products, arithmetic and copies ran while one was open for 6% of the time, Pallas kernels for 39%

profile of v4, /device:TPU:0, one launch (start us, length us, event | category | flops | bytes accessed | tf_op | source)
XLA Modules:
  0.0 170.4 jit_solution(15804176384643964135)
XLA Ops:
  0.6 2.6 %send_scaled.1 = (bf16[48,1536]{1,0:T(8,128)(2,1)}, bf16[48,1536]{1,0:T(8,128)(2,1)}, bf16[48,1536]{1,0:T(8,128)(2,1)}, bf16[48,1536]{1,0:T(8,128)(2,1)}, bf16[4...) custom-call(s32[1]{0:T(128)} %bitcast.dp_ref, ...), custom_call_target="tpu_custom_call" | custom-call | bytes 1179 | tf_op jit(solution)/shard_map/send_scaled/pallas_call | solution.py:92
  3.2 3.0 %collective-permute-start = (bf16[48,1536]{1,0:T(8,128)(2,1)}, bf16[48,1536]{1,0:T(8,128)(2,1)S(1)}, u32[]{:S(2)}, u32[]{:S(2)}) collective-permute-start(bf16[48,1536]{1,0:T(8,128)(2,1)} %get-tuple-element.62), channel_id=1, source_target_pairs={{0,8},{4,12},{8,0},{12,4},{16,24},{20,28},{24,16},{28,20},{1,9},{5... | collective-permute-start | bytes 442376 | tf_op jit(solution)/shard_map/ppermute | solution.py:38
  6.2 1.4 collective-permute-start.5
  7.7 4.0 %collective-permute-start.7 = (bf16[48,1536]{1,0:T(8,128)(2,1)}, bf16[48,1536]{1,0:T(8,128)(2,1)S(1)}, u32[]{:S(2)}, u32[]{:S(2)}) collective-permute-start(bf16[48,1536]{1,0:T(8,128)(2,1)} %get-tuple-element.72), channel_id=1, source_target_pairs={{0,24},{4,28},{8,16},{12,20},{16,8},{20,12},{24,0},{28,4},{1,25},{... | collective-permute-start | bytes 442376 | tf_op jit(solution)/shard_map/ppermute | solution.py:38
  11.7 1.2 collective-permute-start.8
  12.9 1.0 collective-permute-start.1
  13.9 0.7 collective-permute-done.5.refs_3_
  14.7 3.8 %collective-permute-start.6 = (bf16[48,1536]{1,0:T(8,128)(2,1)}, bf16[48,1536]{1,0:T(8,128)(2,1)S(1)}, u32[]{:S(2)}, u32[]{:S(2)}) collective-permute-start(bf16[48,1536]{1,0:T(8,128)(2,1)} %get-tuple-element.71), channel_id=1, source_target_pairs={{0,20},{4,16},{8,28},{12,24},{16,4},{20,0},{24,12},{28,8},{1,21},{... | collective-permute-start | bytes 442376 | tf_op jit(solution)/shard_map/ppermute | solution.py:38
  18.5 0.8 copy.14
  19.2 0.1 reshape.40.key_ref
  19.4 1.5 reshape.41.gate_ref
  20.9 1.8 %reshape.42.up_ref = bf16[256,2048]{1,0:T(8,128)(2,1)S(1)} reshape(bf16[128,2,2048]{2,1,0:T(2,128)(2,1)} %param.7) | data formatting | bytes 2097152 | tf_op jit(solution)/shard_map/reshape | solution.py:431
  22.8 2.0 %send_hidden.1 = (bf16[48,2048]{1,0:T(8,128)(2,1)S(1)}, bf16[48,2048]{1,0:T(8,128)(2,1)S(1)}, bf16[48,2048]{1,0:T(8,128)(2,1)S(1)}, bf16[48,2048]{1,0:T(8,128)(2...) custom-call(s32[1]{0:T(128)} %bitcast.dp_ref, ...), custom_call_target="tpu_custom_call" | custom-call | bytes 3670 | tf_op jit(solution)/shard_map/send_hidden/pallas_call | solution.py:126
  24.9 1.6 collective-permute-start.16
  26.4 8.4 %collective-permute-done.1.refs_0_ = bf16[48,1536]{1,0:T(8,128)(2,1)S(1)} collective-permute-done((bf16[48,1536]{1,0:T(8,128)(2,1)}, bf16[48,1536]{1,0:T(8,128)(2,1)S(1)}, u32[]{:S(2)}, u32[]{:S(2)}) %collective-permute-start.1) | collective-permute-done | bytes 147488 | tf_op jit(solution)/shard_map/ppermute | solution.py:38
  34.8 2.4 %collective-permute-done.6.refs_1_ = bf16[48,1536]{1,0:T(8,128)(2,1)S(1)} collective-permute-done((bf16[48,1536]{1,0:T(8,128)(2,1)}, bf16[48,1536]{1,0:T(8,128)(2,1)S(1)}, u32[]{:S(2)}, u32[]{:S(2)}) %collective-permute-start.6) | collective-permute-done | bytes 147488 | tf_op jit(solution)/shard_map/ppermute | solution.py:38
  37.2 1.5 collective-permute-start.17
  38.8 3.3 %collective-permute-start.2 = (bf16[48,2048]{1,0:T(8,128)(2,1)S(1)}, bf16[48,2048]{1,0:T(8,128)(2,1)S(1)}, u32[]{:S(2)}, u32[]{:S(2)}) collective-permute-start(bf16[48,2048]{1,0:T(8,128)(2,1)S(1)} %get-tuple-element.64), channel_id=1, source_target_pairs={{0,24},{4,28},{8,16},{12,20},{16,8},{20,12},{24,0},{28,4},{1,25},{... | collective-permute-start | bytes 589832 | tf_op jit(solution)/shard_map/ppermute | solution.py:38
  42.1 0.9 collective-permute-start.11
  43.0 4.1 %collective-permute-done.2.refs_6_ = bf16[48,2048]{1,0:T(8,128)(2,1)S(1)} collective-permute-done((bf16[48,2048]{1,0:T(8,128)(2,1)S(1)}, bf16[48,2048]{1,0:T(8,128)(2,1)S(1)}, u32[]{:S(2)}, u32[]{:S(2)}) %collective-permute-start.2) | collective-permute-done | bytes 196640 | tf_op jit(solution)/shard_map/ppermute | solution.py:38
  47.1 0.5 collective-permute-start.18
  47.6 3.0 %collective-permute-done.11.refs_7_ = bf16[48,2048]{1,0:T(8,128)(2,1)S(1)} collective-permute-done((bf16[48,2048]{1,0:T(8,128)(2,1)S(1)}, bf16[48,2048]{1,0:T(8,128)(2,1)S(1)}, u32[]{:S(2)}, u32[]{:S(2)}) %collective-permute-start.11) | collective-permute-done | bytes 196640 | tf_op jit(solution)/shard_map/ppermute | solution.py:38
  50.6 0.4 collective-permute-done.17.refs_5_
  51.0 5.8 %collective-permute-start.13 = (bf16[48,2048]{1,0:T(8,128)(2,1)S(1)}, bf16[48,2048]{1,0:T(8,128)(2,1)S(1)}, u32[]{:S(2)}, u32[]{:S(2)}) collective-permute-start(bf16[48,2048]{1,0:T(8,128)(2,1)S(1)} %get-tuple-element.80), channel_id=1, source_target_pairs={{0,20},{4,16},{8,28},{12,24},{16,4},{20,0},{24,12},{28,8},{1,21},{... | collective-permute-start | bytes 589832 | tf_op jit(solution)/shard_map/ppermute | solution.py:38
  56.8 0.4 collective-permute-start.3
  57.2 3.1 %collective-permute-start.12 = (bf16[48,2048]{1,0:T(8,128)(2,1)S(1)}, bf16[48,2048]{1,0:T(8,128)(2,1)S(1)}, u32[]{:S(2)}, u32[]{:S(2)}) collective-permute-start(bf16[48,2048]{1,0:T(8,128)(2,1)S(1)} %get-tuple-element.78), channel_id=1, source_target_pairs={{0,16},{4,20},{8,24},{12,28},{16,0},{20,4},{24,8},{28,12},{1,17},{... | collective-permute-start | bytes 589832 | tf_op jit(solution)/shard_map/ppermute | solution.py:38
  60.3 16.3 %back.1 = (bf16[384,2048]{1,0:T(8,128)(2,1)}, bf16[4,384,1536]{2,1,0:T(8,128)(2,1)S(1)}) custom-call(s32[1]{0:T(128)} %bitcast.dp_ref, s32[1]{0:T(128)} %bitcast.1.hid_ref, bf16[192,1536]{1,0:T(8,128)(2,1)S(1)} %stack.3.refs_0_, bf16[192,1536]{1,0:T(8,128)(2,1)S(1)} %stack.2.refs_1_, bf16[192,1536]{1,0:T(8,128)(2,1)S(1)} %collective-permute-done.15.refs_2_, ...), custom_call_target="tpu_custom_call" | custom-call | flops 9663676 | bytes 31457 | tf_op jit(solution)/shard_map/back/pallas_call | solution.py:287
  76.6 2.1 %copy-done.3 = bf16[4,384,1536]{2,1,0:T(8,128)(2,1)} copy-done((bf16[4,384,1536]{2,1,0:T(8,128)(2,1)}, bf16[4,384,1536]{2,1,0:T(8,128)(2,1)S(1)}, u32[]{:S(2)}) %copy-start.3) | copy-done | bytes 4718616
  78.8 4.3 %all-to-all-start = ((bf16[8,48,2048]{2,1,0:T(8,128)(2,1)}), bf16[8,48,2048]{2,1,0:T(8,128)(2,1)}, u32[]{:S(2)}, u32[]{:S(2)}) async-start(bf16[8,48,2048]{2,1,0:T(8,128)(2,1)} %bitcast.6), calls=%async_computation | async-start | bytes 3145728 | tf_op jit(solution)/shard_map/all_to_all | solution.py:428
  83.1 5.3 %first_down.1 = (bf16[384,1536]{1,0:T(8,128)(2,1)S(1)}, bf16[384,2048]{1,0:T(8,128)(2,1)S(1)}) custom-call(s32[1]{0:T(128)} %bitcast.dp_ref, s32[1]{0:T(128)} %bitcast.1.hid_ref, bf16[48,2048]{1,0:T(8,128)(2,1)S(1)} %get-tuple-element.86.refs_0_, bf16[48,2048]{1,0:T(8,128)(2,1)S(1)} %collective-permute-done.3.refs_1_, ...), custom_call_target="tpu_custom_call" | custom-call | flops 2415919 | bytes 9043 | tf_op jit(solution)/shard_map/first_down/pallas_call | solution.py:191
  88.5 5.7 %down.3 = bf16[384,1536]{1,0:T(8,128)(2,1)S(1)} custom-call(s32[1]{0:T(128)} %bitcast.1.hid_ref, bf16[384,2048]{1,0:T(8,128)(2,1)S(1)} %get-tuple-element.99.x_ref, bf16[2048,6144]{1,0:T(8,128)(2,1)} %bitcast.16), custom_call_target="tpu_custom_call" | custom-call | flops 2415919 | bytes 9043 | tf_op jit(solution)/shard_map/down/pallas_call | solution.py:154
  94.3 6.1 %down.4 = bf16[384,1536]{1,0:T(8,128)(2,1)} custom-call(s32[1]{0:T(128)} %bitcast.1.hid_ref, bf16[384,2048]{1,0:T(8,128)(2,1)S(1)} %get-tuple-element.99.x_ref, bf16[2048,6144]{1,0:T(8,128)(2,1)} %bitcast.17, bf16[384,1536]{1,0:T(8,128)(2,1)S(1)} %collective-permute-done.20.refs_0_), custom_call_target="tpu_custom_call" | custom-call | flops 2415919 | bytes 9043 | tf_op jit(solution)/shard_map/down/pallas_call | solution.py:154
  100.5 1.1 collective-permute-start.22
  101.5 7.2 %down.5.a_ref = f32[384,1536]{1,0:T(8,128)} custom-call(s32[1]{0:T(128)} %bitcast.1.hid_ref, bf16[384,2048]{1,0:T(8,128)(2,1)} %copy-done, bf16[2048,6144]{1,0:T(8,128)(2,1)} %bitcast.18, bf16[384,1536]{1,0:T(8,128)(2,1)} %collective-permute-done.21.refs_0_), custom_call_target="tpu_custom_call" | custom-call | flops 2415919 | bytes 10223 | tf_op jit(solution)/shard_map/down/pallas_call | solution.py:154
  108.7 18.8 %outer.1.refs_0_ = bf16[1,2048,6144]{2,1,0:T(8,128)(2,1)} custom-call(s32[1]{0:T(128)} %bitcast.1.hid_ref, bf16[384,2048]{1,0:T(8,128)(2,1)} %copy-done, bf16[4,384,1536]{2,1,0:T(8,128)(2,1)} %copy-done.3), custom_call_target="tpu_custom_call" | custom-call | flops 9663676 | bytes 31457 | tf_op jit(solution)/shard_map/outer/pallas_call | solution.py:317
  127.5 1.6 collective-permute-done.22.b_ref
  129.1 3.9 %sum_of.1 = bf16[384,1536]{1,0:T(8,128)(2,1)} custom-call(f32[384,1536]{1,0:T(8,128)} %down.5.a_ref, bf16[384,1536]{1,0:T(8,128)(2,1)} %collective-permute-done.22.b_ref), custom_call_target="tpu_custom_call" | custom-call | bytes 4718 | tf_op jit(solution)/shard_map/sum_of/pallas_call | solution.py:218
  133.0 6.0 %all-to-all-start.1 = ((bf16[8,48,1536]{2,1,0:T(8,128)(2,1)}), bf16[8,48,1536]{2,1,0:T(8,128)(2,1)}, u32[]{:S(2)}, u32[]{:S(2)}) async-start(bf16[8,48,1536]{2,1,0:T(8,128)(2,1)} %bitcast.19), calls=%async_computation.1 | async-start | bytes 2359296 | tf_op jit(solution)/shard_map/all_to_all | solution.py:428
  139.1 5.4 %grads.1 = (bf16[256,2048]{1,0:T(8,128)(2,1)}, bf16[256,2048]{1,0:T(8,128)(2,1)}, f32[256,1]{1,0:T(8,128)}) custom-call(s32[1,256]{1,0:T(1,128)} %copy-done.8, bf16[256,2048]{1,0:T(8,128)(2,1)} %copy-done.1, bf16[256,2048]{1,0:T(8,128)(2,1)} %copy-done.2, bf16[384,2048]{1,0:T(8,128)(2,1)} %bitcast.7.back_ref), custom_call_target="tpu_custom_call" | custom-call | bytes 5767 | tf_op jit(solution)/shard_map/grads/pallas_call | solution.py:357
  144.6 1.0 reduce
  145.6 0.1 reshape.45
  145.9 1.2 collective-permute-done.23
  147.1 1.3 collective-permute-start.24
  148.4 1.7 %reshape.43.refs_1_ = bf16[128,2,2048]{2,1,0:T(2,128)(2,1)S(1)} reshape(bf16[256,2048]{1,0:T(8,128)(2,1)} %get-tuple-element.106) | data formatting | bytes 2097152 | tf_op jit(solution)/shard_map/reshape | solution.py:489
  150.1 2.1 %reshape.44.refs_2_ = bf16[128,2,2048]{2,1,0:T(2,128)(2,1)S(1)} reshape(bf16[256,2048]{1,0:T(8,128)(2,1)} %get-tuple-element.107) | data formatting | bytes 2097152 | tf_op jit(solution)/shard_map/reshape | solution.py:489
  152.3 0.8 copy.16
  153.1 14.5 %all-to-all-done.1 = bf16[8,48,1536]{2,1,0:T(8,128)(2,1)} async-done(((bf16[8,48,1536]{2,1,0:T(8,128)(2,1)}), bf16[8,48,1536]{2,1,0:T(8,128)(2,1)}, u32[]{:S(2)}, u32[]{:S(2)}) %all-to-all-start.1) | async-done | bytes 1179680 | tf_op jit(solution)/shard_map/all_to_all | solution.py:428
  167.6 2.9 %mixed.1 = bf16[1,128,1536]{2,1,0:T(8,128)(2,1)} custom-call(s32[2,128]{1,0:T(2,128)S(1)} %copy-done.9, f32[2,128]{1,0:T(2,128)S(1)} %bitcast.12, bf16[384,1536]{1,0:T(8,128)(2,1)} %bitcast.9.x_ref, bf16[1,2048,6144]{2,1,0:T(8,128)(2,1)} %outer.1.refs_0_, bf16[128,2,2048]{2,1,0:T(2,128)(2,1)S(1)} %reshape.43.refs_1_, ...), custom_call_target="tpu_custom_call" | custom-call | bytes 1572 | tf_op jit(solution)/shard_map/mixed/pallas_call | solution.py:401
  (52 shorter events, 0.8 us)
Async XLA Ops:
  3.2 9.7 %collective-permute-start = (bf16[48,1536]{1,0:T(8,128)(2,1)}, bf16[48,1536]{1,0:T(8,128)(2,1)S(1)}, u32[]{:S(2)}, u32[]{:S(2)}) collective-permute-start(bf16[48,1536]{1,0:T(8,128)(2,1)} %get-tuple-element.62), channel_id=1, source_target_pairs={{0,8},{4,12},{8,0},{12,4},{16,24},{20,28},{24,16},{28,20},{1,9},{5... | collective-permute-start | bytes 442376 | tf_op jit(solution)/shard_map/ppermute | solution.py:38
  6.2 8.4 %collective-permute-start.5 = (bf16[48,1536]{1,0:T(8,128)(2,1)}, bf16[48,1536]{1,0:T(8,128)(2,1)S(1)}, u32[]{:S(2)}, u32[]{:S(2)}) collective-permute-start(bf16[48,1536]{1,0:T(8,128)(2,1)} %get-tuple-element.70), channel_id=1, source_target_pairs={{0,12},{4,8},{8,4},{12,0},{16,28},{20,24},{24,20},{28,16},{1,13},{... | collective-permute-start | bytes 442376 | tf_op jit(solution)/shard_map/ppermute | solution.py:38
  7.6 17.1 %collective-permute-start.14 = (bf16[48,1536]{1,0:T(8,128)(2,1)}, bf16[48,1536]{1,0:T(8,128)(2,1)S(1)}, u32[]{:S(2)}, u32[]{:S(2)}) collective-permute-start(bf16[48,1536]{1,0:T(8,128)(2,1)} %get-tuple-element.82), channel_id=1, source_target_pairs={{0,4},{4,0},{8,12},{12,8},{16,20},{20,16},{24,28},{28,24},{1,5},{5... | collective-permute-start | bytes 442376 | tf_op jit(solution)/shard_map/ppermute | solution.py:38
  7.7 18.7 %collective-permute-start.7 = (bf16[48,1536]{1,0:T(8,128)(2,1)}, bf16[48,1536]{1,0:T(8,128)(2,1)S(1)}, u32[]{:S(2)}, u32[]{:S(2)}) collective-permute-start(bf16[48,1536]{1,0:T(8,128)(2,1)} %get-tuple-element.72), channel_id=1, source_target_pairs={{0,24},{4,28},{8,16},{12,20},{16,8},{20,12},{24,0},{28,4},{1,25},{... | collective-permute-start | bytes 442376 | tf_op jit(solution)/shard_map/ppermute | solution.py:38
  11.7 14.7 %collective-permute-start.8 = (bf16[48,1536]{1,0:T(8,128)(2,1)}, bf16[48,1536]{1,0:T(8,128)(2,1)S(1)}, u32[]{:S(2)}, u32[]{:S(2)}) collective-permute-start(bf16[48,1536]{1,0:T(8,128)(2,1)} %get-tuple-element.73), channel_id=1, source_target_pairs={{0,28},{4,24},{8,20},{12,16},{16,12},{20,8},{24,4},{28,0},{1,29},{... | collective-permute-start | bytes 442376 | tf_op jit(solution)/shard_map/ppermute | solution.py:38
  12.9 21.9 %collective-permute-start.1 = (bf16[48,1536]{1,0:T(8,128)(2,1)}, bf16[48,1536]{1,0:T(8,128)(2,1)S(1)}, u32[]{:S(2)}, u32[]{:S(2)}) collective-permute-start(bf16[48,1536]{1,0:T(8,128)(2,1)} %get-tuple-element.63), channel_id=1, source_target_pairs={{0,16},{4,20},{8,24},{12,28},{16,0},{20,4},{24,8},{28,12},{1,17},{... | collective-permute-start | bytes 442376 | tf_op jit(solution)/shard_map/ppermute | solution.py:38
  14.7 22.5 %collective-permute-start.6 = (bf16[48,1536]{1,0:T(8,128)(2,1)}, bf16[48,1536]{1,0:T(8,128)(2,1)S(1)}, u32[]{:S(2)}, u32[]{:S(2)}) collective-permute-start(bf16[48,1536]{1,0:T(8,128)(2,1)} %get-tuple-element.71), channel_id=1, source_target_pairs={{0,20},{4,16},{8,28},{12,24},{16,4},{20,0},{24,12},{28,8},{1,21},{... | collective-permute-start | bytes 442376 | tf_op jit(solution)/shard_map/ppermute | solution.py:38
  19.4 3.4 %copy-start.8 = (s32[1,256]{1,0:T(1,128)}, s32[1,256]{1,0:T(1,128)S(1)}, u32[]{:S(2)}) copy-start(s32[1,256]{1,0:T(1,128)S(1)} %reshape.40.key_ref) | copy-start | bytes 3076
  20.9 3.9 %copy-start.1 = (bf16[256,2048]{1,0:T(8,128)(2,1)}, bf16[256,2048]{1,0:T(8,128)(2,1)S(1)}, u32[]{:S(2)}) copy-start(bf16[256,2048]{1,0:T(8,128)(2,1)S(1)} %reshape.41.gate_ref) | copy-start | bytes 3145732
  22.8 2.1 %copy-start.2 = (bf16[256,2048]{1,0:T(8,128)(2,1)}, bf16[256,2048]{1,0:T(8,128)(2,1)S(1)}, u32[]{:S(2)}) copy-start(bf16[256,2048]{1,0:T(8,128)(2,1)S(1)} %reshape.42.up_ref) | copy-start | bytes 3145732
  22.8 2.0 %copy-start.6 = (bf16[48,1536]{1,0:T(8,128)(2,1)S(1)}, bf16[48,1536]{1,0:T(8,128)(2,1)}, u32[]{:S(2)}) copy-start(bf16[48,1536]{1,0:T(8,128)(2,1)} %get-tuple-element.81.refs_0_) | copy-start | bytes 442372
  24.9 22.2 %collective-permute-start.16 = (bf16[192,1536]{1,0:T(8,128)(2,1)S(1)}, bf16[192,1536]{1,0:T(8,128)(2,1)S(1)}, u32[]{:S(2)}, u32[]{:S(2)}) collective-permute-start(bf16[192,1536]{1,0:T(8,128)(2,1)S(1)} %stack.3.refs_0_), channel_id=1, source_target_pairs={{0,2},{1,3},{2,0},{3,1},{4,6},{5,7},{6,4},{7,5},{8,10},{9,11},{10,... | collective-permute-start | bytes 1769480 | tf_op jit(solution)/shard_map/ppermute | solution.py:38
  37.2 13.7 %collective-permute-start.17 = (bf16[192,1536]{1,0:T(8,128)(2,1)S(1)}, bf16[192,1536]{1,0:T(8,128)(2,1)S(1)}, u32[]{:S(2)}, u32[]{:S(2)}) collective-permute-start(bf16[192,1536]{1,0:T(8,128)(2,1)S(1)} %stack.2.refs_1_), channel_id=1, source_target_pairs={{0,2},{1,3},{2,0},{3,1},{4,6},{5,7},{6,4},{7,5},{8,10},{9,11},{10,... | collective-permute-start | bytes 1769480 | tf_op jit(solution)/shard_map/ppermute | solution.py:38
  38.8 8.3 %collective-permute-start.2 = (bf16[48,2048]{1,0:T(8,128)(2,1)S(1)}, bf16[48,2048]{1,0:T(8,128)(2,1)S(1)}, u32[]{:S(2)}, u32[]{:S(2)}) collective-permute-start(bf16[48,2048]{1,0:T(8,128)(2,1)S(1)} %get-tuple-element.64), channel_id=1, source_target_pairs={{0,24},{4,28},{8,16},{12,20},{16,8},{20,12},{24,0},{28,4},{1,25},{... | collective-permute-start | bytes 589832 | tf_op jit(solution)/shard_map/ppermute | solution.py:38
  42.1 8.5 %collective-permute-start.11 = (bf16[48,2048]{1,0:T(8,128)(2,1)S(1)}, bf16[48,2048]{1,0:T(8,128)(2,1)S(1)}, u32[]{:S(2)}, u32[]{:S(2)}) collective-permute-start(bf16[48,2048]{1,0:T(8,128)(2,1)S(1)} %get-tuple-element.77), channel_id=1, source_target_pairs={{0,28},{4,24},{8,20},{12,16},{16,12},{20,8},{24,4},{28,0},{1,29},{... | collective-permute-start | bytes 589832 | tf_op jit(solution)/shard_map/ppermute | solution.py:38
  43.0 13.7 %collective-permute-start.9 = (bf16[192,1536]{1,0:T(8,128)(2,1)S(1)}, bf16[192,1536]{1,0:T(8,128)(2,1)S(1)}, u32[]{:S(2)}, u32[]{:S(2)}) collective-permute-start(bf16[192,1536]{1,0:T(8,128)(2,1)S(1)} %stack.2.refs_1_), channel_id=1, source_target_pairs={{0,1},{1,0},{2,3},{3,2},{4,5},{5,4},{6,7},{7,6},{8,9},{9,8},{10,11... | collective-permute-start | bytes 1769480 | tf_op jit(solution)/shard_map/ppermute | solution.py:38
  47.1 10.1 %collective-permute-start.15 = (bf16[192,1536]{1,0:T(8,128)(2,1)S(1)}, bf16[192,1536]{1,0:T(8,128)(2,1)S(1)}, u32[]{:S(2)}, u32[]{:S(2)}) collective-permute-start(bf16[192,1536]{1,0:T(8,128)(2,1)S(1)} %stack.3.refs_0_), channel_id=1, source_target_pairs={{0,1},{1,0},{2,3},{3,2},{4,5},{5,4},{6,7},{7,6},{8,9},{9,8},{10,11... | collective-permute-start | bytes 1769480 | tf_op jit(solution)/shard_map/ppermute | solution.py:38
  47.1 10.1 %collective-permute-start.18 = (bf16[192,1536]{1,0:T(8,128)(2,1)S(1)}, bf16[192,1536]{1,0:T(8,128)(2,1)S(1)}, u32[]{:S(2)}, u32[]{:S(2)}) collective-permute-start(bf16[192,1536]{1,0:T(8,128)(2,1)S(1)} %collective-permute-done.16.refs_4_), channel_id=1, source_target_pairs={{0,1},{1,0},{2,3},{3,2},{4,5},{5,4},{6,7},{7,6},{8,9},{9,8},{10,11... | collective-permute-start | bytes 1769480 | tf_op jit(solution)/shard_map/ppermute | solution.py:38
  51.0 9.2 %collective-permute-start.19 = (bf16[192,1536]{1,0:T(8,128)(2,1)S(1)}, bf16[192,1536]{1,0:T(8,128)(2,1)S(1)}, u32[]{:S(2)}, u32[]{:S(2)}) collective-permute-start(bf16[192,1536]{1,0:T(8,128)(2,1)S(1)} %collective-permute-done.17.refs_5_), channel_id=1, source_target_pairs={{0,1},{1,0},{2,3},{3,2},{4,5},{5,4},{6,7},{7,6},{8,9},{9,8},{10,11... | collective-permute-start | bytes 1769480 | tf_op jit(solution)/shard_map/ppermute | solution.py:38
  51.0 27.8 %collective-permute-start.13 = (bf16[48,2048]{1,0:T(8,128)(2,1)S(1)}, bf16[48,2048]{1,0:T(8,128)(2,1)S(1)}, u32[]{:S(2)}, u32[]{:S(2)}) collective-permute-start(bf16[48,2048]{1,0:T(8,128)(2,1)S(1)} %get-tuple-element.80), channel_id=1, source_target_pairs={{0,20},{4,16},{8,28},{12,24},{16,4},{20,0},{24,12},{28,8},{1,21},{... | collective-permute-start | bytes 589832 | tf_op jit(solution)/shard_map/ppermute | solution.py:38
  56.8 22.0 %collective-permute-start.3 = (bf16[48,2048]{1,0:T(8,128)(2,1)S(1)}, bf16[48,2048]{1,0:T(8,128)(2,1)S(1)}, u32[]{:S(2)}, u32[]{:S(2)}) collective-permute-start(bf16[48,2048]{1,0:T(8,128)(2,1)S(1)} %get-tuple-element.65), channel_id=1, source_target_pairs={{0,4},{4,0},{8,12},{12,8},{16,20},{20,16},{24,28},{28,24},{1,5},{5... | collective-permute-start | bytes 589832 | tf_op jit(solution)/shard_map/ppermute | solution.py:38
  57.1 21.6 %collective-permute-start.4 = (bf16[48,2048]{1,0:T(8,128)(2,1)S(1)}, bf16[48,2048]{1,0:T(8,128)(2,1)S(1)}, u32[]{:S(2)}, u32[]{:S(2)}) collective-permute-start(bf16[48,2048]{1,0:T(8,128)(2,1)S(1)} %get-tuple-element.67), channel_id=1, source_target_pairs={{0,8},{4,12},{8,0},{12,4},{16,24},{20,28},{24,16},{28,20},{1,9},{5... | collective-permute-start | bytes 589832 | tf_op jit(solution)/shard_map/ppermute | solution.py:38
  57.2 21.6 %collective-permute-start.12 = (bf16[48,2048]{1,0:T(8,128)(2,1)S(1)}, bf16[48,2048]{1,0:T(8,128)(2,1)S(1)}, u32[]{:S(2)}, u32[]{:S(2)}) collective-permute-start(bf16[48,2048]{1,0:T(8,128)(2,1)S(1)} %get-tuple-element.78), channel_id=1, source_target_pairs={{0,16},{4,20},{8,24},{12,28},{16,0},{20,4},{24,8},{28,12},{1,17},{... | collective-permute-start | bytes 589832 | tf_op jit(solution)/shard_map/ppermute | solution.py:38
  60.2 18.6 %collective-permute-start.10 = (bf16[48,2048]{1,0:T(8,128)(2,1)S(1)}, bf16[48,2048]{1,0:T(8,128)(2,1)S(1)}, u32[]{:S(2)}, u32[]{:S(2)}) collective-permute-start(bf16[48,2048]{1,0:T(8,128)(2,1)S(1)} %get-tuple-element.74), channel_id=1, source_target_pairs={{0,12},{4,8},{8,4},{12,0},{16,28},{20,24},{24,20},{28,16},{1,13},{... | collective-permute-start | bytes 589832 | tf_op jit(solution)/shard_map/ppermute | solution.py:38
  76.6 2.1 %copy-start.3 = (bf16[4,384,1536]{2,1,0:T(8,128)(2,1)}, bf16[4,384,1536]{2,1,0:T(8,128)(2,1)S(1)}, u32[]{:S(2)}) copy-start(bf16[4,384,1536]{2,1,0:T(8,128)(2,1)S(1)} %get-tuple-element.100.y_ref) | copy-start | bytes 14155780
  78.8 48.7 %all-to-all-start = ((bf16[8,48,2048]{2,1,0:T(8,128)(2,1)}), bf16[8,48,2048]{2,1,0:T(8,128)(2,1)}, u32[]{:S(2)}, u32[]{:S(2)}) async-start(bf16[8,48,2048]{2,1,0:T(8,128)(2,1)} %bitcast.6), calls=%async_computation | async-start | bytes 3145728 | tf_op jit(solution)/shard_map/all_to_all | solution.py:428
  88.4 5.9 %copy-start = (bf16[384,2048]{1,0:T(8,128)(2,1)}, bf16[384,2048]{1,0:T(8,128)(2,1)S(1)}, u32[]{:S(2)}) copy-start(bf16[384,2048]{1,0:T(8,128)(2,1)S(1)} %get-tuple-element.99.x_ref) | copy-start | bytes 4718596
  88.4 5.8 %collective-permute-start.20 = (bf16[384,1536]{1,0:T(8,128)(2,1)S(1)}, bf16[384,1536]{1,0:T(8,128)(2,1)S(1)}, u32[]{:S(2)}, u32[]{:S(2)}) collective-permute-start(bf16[384,1536]{1,0:T(8,128)(2,1)S(1)} %get-tuple-element.96), channel_id=1, source_target_pairs={{0,1},{1,0},{2,3},{3,2},{4,5},{5,4},{6,7},{7,6},{8,9},{9,8},{10,11... | collective-permute-start | bytes 3538952 | tf_op jit(solution)/shard_map/ppermute | solution.py:38
  94.2 7.3 %collective-permute-start.21 = (bf16[384,1536]{1,0:T(8,128)(2,1)S(1)}, bf16[384,1536]{1,0:T(8,128)(2,1)}, u32[]{:S(2)}, u32[]{:S(2)}) collective-permute-start(bf16[384,1536]{1,0:T(8,128)(2,1)S(1)} %down.3), channel_id=1, source_target_pairs={{0,1},{1,0},{2,3},{3,2},{4,5},{5,4},{6,7},{7,6},{8,9},{9,8},{10,11... | collective-permute-start | bytes 3538952 | tf_op jit(solution)/shard_map/ppermute | solution.py:38
  100.5 28.7 %collective-permute-start.22 = (bf16[384,1536]{1,0:T(8,128)(2,1)}, bf16[384,1536]{1,0:T(8,128)(2,1)}, u32[]{:S(2)}, u32[]{:S(2)}) collective-permute-start(bf16[384,1536]{1,0:T(8,128)(2,1)} %down.4), channel_id=1, source_target_pairs={{0,2},{1,3},{2,0},{3,1},{4,6},{5,7},{6,4},{7,5},{8,10},{9,11},{10,... | collective-permute-start | bytes 3538952 | tf_op jit(solution)/shard_map/ppermute | solution.py:38
  133.0 6.0 %copy-start.7 = (f32[128,2]{0,1:T(2,128)S(1)}, f32[128,2]{0,1:T(2,128)}, u32[]{:S(2)}) copy-start(f32[128,2]{0,1:T(2,128)} %param.9) | copy-start | bytes 3076
  133.0 34.6 %all-to-all-start.1 = ((bf16[8,48,1536]{2,1,0:T(8,128)(2,1)}), bf16[8,48,1536]{2,1,0:T(8,128)(2,1)}, u32[]{:S(2)}, u32[]{:S(2)}) async-start(bf16[8,48,1536]{2,1,0:T(8,128)(2,1)} %bitcast.19), calls=%async_computation.1 | async-start | bytes 2359296 | tf_op jit(solution)/shard_map/all_to_all | solution.py:428
  145.8 1.3 collective-permute-start.23
  147.1 5.2 %collective-permute-start.24 = (f32[128,2]{1,0:T(8,128)S(1)}, f32[128,2]{1,0:T(8,128)S(1)}, u32[]{:S(2)}, u32[]{:S(2)}) collective-permute-start(f32[128,2]{1,0:T(8,128)S(1)} %add.6), channel_id=1, source_target_pairs={{0,2},{1,3},{2,0},{3,1},{4,6},{5,7},{6,4},{7,5},{8,10},{9,11},{10,... | collective-permute-start | bytes 3080 | tf_op jit(solution)/shard_map/ppermute | solution.py:38
  150.1 20.3 %copy-start.4 = (bf16[128,2,2048]{2,1,0:T(2,128)(2,1)}, bf16[128,2,2048]{2,1,0:T(2,128)(2,1)S(1)}, u32[]{:S(2)}) copy-start(bf16[128,2,2048]{2,1,0:T(2,128)(2,1)S(1)} %reshape.43.refs_1_) | copy-start | bytes 3145732
  150.1 17.4 %copy-start.9 = (s32[2,128]{1,0:T(2,128)S(1)}, s32[2,128]{1,0:T(2,128)}, u32[]{:S(2)}) copy-start(s32[2,128]{1,0:T(2,128)} %get-tuple-element.57.key_ref) | copy-start | bytes 3076
  152.3 18.1 %copy-start.5 = (bf16[128,2,2048]{2,1,0:T(2,128)(2,1)}, bf16[128,2,2048]{2,1,0:T(2,128)(2,1)S(1)}, u32[]{:S(2)}) copy-start(bf16[128,2,2048]{2,1,0:T(2,128)(2,1)S(1)} %reshape.44.refs_2_) | copy-start | bytes 3145732

commit v5 on v4

--- a/solution.py
+++ b/solution.py
@@ -172,30 +172,47 @@
     )(my_hid, x, weights, *add)
 
 
-def first_down_kernel(count, dp_ref, hid_ref, *refs):
-    blocks, w_ref, o_ref, x_ref = refs[:count], *refs[count:]
+def first_down_kernel(count, per, dp_ref, hid_ref, *refs):
+    blocks, w_ref, o_refs, x_ref = refs[:count], refs[count], refs[count + 1 : -1], refs[-1]
 
     @pl.when(pl.program_id(0) == 0)
     def _():
         for k, b in enumerate(blocks):
             x_ref[rows_of(dp_ref, k), :] = b[...]
 
-    o_ref[...] = jnp.dot(x_ref[...], w_ref[...], preferred_element_type=F32).astype(BF16)
-
-
-def first_down(my_dp, my_hid, blocks, weights, q, quarter):
+    made = jnp.dot(x_ref[...], w_ref[...], preferred_element_type=F32).astype(BF16)
+    for i, o_ref in enumerate(o_refs):
+
+        @pl.when(pl.program_id(0) // per == i)
+        def _(o_ref=o_ref):
+            o_ref[...] = made
+
+
+def first_down(my_dp, my_hid, blocks, weights, quarters, quarter):
     rows, depth = CAP * len(blocks), blocks[0].shape[1]
     block = min(512, quarter)
     per = quarter // block
-    outs = [jax.ShapeDtypeStruct((rows, quarter), BF16), jax.ShapeDtypeStruct((rows, depth), BF16)]
-    return pl.pallas_call(
-        functools.partial(first_down_kernel, len(blocks)),
+    top = quarters[0]
+    outs = [jax.ShapeDtypeStruct((rows, quarter), BF16)] * len(quarters)
+    outs.append(jax.ShapeDtypeStruct((rows, depth), BF16))
+
+    def place(i):
+        return lambda j, d, h: (0, jnp.clip(j - i * per, 0, per - 1))
+
+    return pl.pallas_call(
+        functools.partial(first_down_kernel, len(blocks), per),
         grid_spec=pltpu.PrefetchScalarGridSpec(
             num_scalar_prefetch=2,
-            grid=(per,),
+            grid=(per * len(quarters),),
             in_specs=[whole(b) for b in blocks]
-            + [pl.BlockSpec((depth, block), lambda j, d, h: (0, (h[0] ^ q) * per + j))],
-            out_specs=[pl.BlockSpec((rows, block), lambda j, d, h: (0, j)), whole(outs[1])],
+            + [
+                pl.BlockSpec(
+                    (depth, block),
+                    lambda j, d, h: (0, (h[0] ^ (top - 2 * (j // per))) * per + j % per),
+                )
+            ],
+            out_specs=[pl.BlockSpec((rows, block), place(i)) for i in range(len(quarters))]
+            + [whole(outs[-1])],
         ),
         out_shape=outs,
         compiler_params=PARAMS,
@@ -212,7 +229,7 @@
 
 def sum_of(a, b):
     rows, width = a.shape
-    block = 2 * CAP
+    block = rows // 2
     part = pl.BlockSpec((block, width), lambda i: (i, 0))
     out = jax.ShapeDtypeStruct((rows, width), BF16)
     return pl.pallas_call(
@@ -323,7 +340,7 @@
             out_specs=pl.BlockSpec((1, block, width), lambda i, h: (0, i, 0)),
         ),
         out_shape=out,
-        compiler_params=WIDE,
+        compiler_params=PARAMS,
         cost_estimate=cost(2 * rows * depth * width, x, y, out),
         name="outer",
     )(my_hid, x, y)
@@ -385,12 +402,14 @@
                     row = jnp.where(hit, weight_ref[s : s + 1, :], row)
             rows.append(row)
         left = jnp.concatenate(rows, axis=0)
-        total = None
+        terms = []
         for _ in range(3):
-            part = left.astype(BF16)
-            left = left - part.astype(F32)
-            term = lax.dot_general(part, x, ROWS, preferred_element_type=F32)
-            total = term if total is None else total + term
+            terms.append(left.astype(BF16))
+            left = left - terms[-1].astype(F32)
+        sums = lax.dot_general(
+            jnp.concatenate(terms, axis=1), x, ROWS, preferred_element_type=F32
+        )
+        total = sums[:tokens] + sums[tokens : 2 * tokens] + sums[2 * tokens :]
         o_ref[j] = total.astype(BF16)
 
 
@@ -444,6 +463,7 @@
     bit = hid_count // 2
     for piece in halves:
         piece[bit] = swap(piece[0], "hid", bit)
+    halves[0][bit // 2] = swap(own[0], "hid", bit // 2)
     got_hidden = {0: hidden[0]}
     for k, ahead in zip(far[:3], (got[far[2]], got[far[3]], got[far[3]])):
         got_hidden[k] = swap(hidden[k], "dp", k, [ahead])
@@ -463,19 +483,15 @@
     got_hidden, sent_back = lax.optimization_barrier((got_hidden, sent_back))
 
     got_back = over_dp(sent_back)
-    sums, others = {}, []
-    for q in range(hid_count - 1, 0, -2):
-        if not sums:
-            made, x = first_down(my_dp, my_hid, got_hidden, weights, q, quarter)
-        else:
-            made = down(my_hid, x, weights, q, quarter, BF16, PARAMS)
-        sums[q] = swap(made, "hid", 1)
-    x = lax.optimization_barrier((x, made))[0]
+    others = []
+    odd = list(range(hid_count - 1, 0, -2))
+    *away, x = first_down(my_dp, my_hid, got_hidden, weights, odd, quarter)
+    sums = {q: swap(made, "hid", 1) for q, made in zip(odd, away)}
     for q in range(hid_count - 2, 0, -2):
         made = down(my_hid, x, weights, q, quarter, BF16, PARAMS, sums[q + 1])
         others.append(swap(made, "hid", q))
     x = lax.optimization_barrier((x, made))[0]
-    total = down(my_hid, x, weights, 0, quarter, F32, WIDE, sums[1])
+    total = down(my_hid, x, weights, 0, quarter, F32, PARAMS, sums[1])
     x = lax.optimization_barrier((x, total))[0]
     weight_grad = outer(my_hid, x, y)
     for other in others[1:]:

time: 171 us -> 170 us (level)
  Pallas kernels: 76.2 us -> 68.7 us
  waiting for transfers between devices: 36.3 us -> 40.6 us
    pallas_call x3 -> x2, Pallas kernels: 19 us -> 10.6 us  [down(): pl.pallas_call(functools.partial(down_kernel, len(add)), grid_spec=pltpu....]
    ppermute x25, waiting for transfers between devices: 21.8 us -> 26.3 us  [swap(): return lax.ppermute(x, axis, [(i, i ^ bit) for i in range(count)])]
    pallas_call x1, Pallas kernels: 5.31 us -> 9.51 us  [first_down(): pl.pallas_call(functools.partial(first_down_kernel, len(blocks), per), gr...]
    pallas_call x1, Pallas kernels: 18.8 us -> 16.6 us  [outer(): pl.pallas_call(outer_kernel, grid_spec=pltpu.PrefetchScalarGridSpec(num_s...]
    unnamed x22 -> x26, local copies, waits for them, and re-layouts: 3.06 us -> 4.55 us
  transfers between devices with their start and end apart: 27 -> 27, of which waited for: 9 -> 10; matrix products, arithmetic and copies ran while one was open for 6% -> 6% of each run, Pallas kernels for 39% -> 36%
where the time goes in v5:
time: 170 us; the launch traced here: 169 us
  Pallas kernels  68.7 us (40%)
  starting transfers between devices  45.1 us (27%)
  waiting for transfers between devices  40.6 us (24%)
  local copies, waits for them, and re-layouts  12.8 us (8%)
    ppermute x25, starting transfers between devices, swap(): return lax.ppermute(x, axis, [(i, i ^ bit) for i in range(count)])  34.7 us
    ppermute x25, waiting for transfers between devices, swap(): return lax.ppermute(x, axis, [(i, i ^ bit) for i in range(count)])  26.3 us
    pallas_call x1, Pallas kernels, outer(): pl.pallas_call(outer_kernel, grid_spec=pltpu.PrefetchScalarGridSpec(num_s...  16.6 us
    pallas_call x1, Pallas kernels, back(): pl.pallas_call(back_kernel, grid_spec=pltpu.PrefetchScalarGridSpec(num_sc...  16.3 us
    all_to_all x2, waiting for transfers between devices, over_dp(): return lax.all_to_all(x, 'dp', split_axis=0, concat_axis=0, tiled=True)  14.3 us
    pallas_call x2, Pallas kernels, down(): pl.pallas_call(functools.partial(down_kernel, len(add)), grid_spec=pltpu....  10.6 us
    all_to_all x2, starting transfers between devices, over_dp(): return lax.all_to_all(x, 'dp', split_axis=0, concat_axis=0, tiled=True)  10.3 us
    pallas_call x1, Pallas kernels, first_down(): pl.pallas_call(functools.partial(first_down_kernel, len(blocks), per), gr...  9.51 us
  transfers between devices with their start and end apart: 27, of which 10 were waited for; matrix products, arithmetic and copies ran while one was open for 6% of the time, Pallas kernels for 36%

profile of v5, /device:TPU:0, one launch (start us, length us, event | category | flops | bytes accessed | tf_op | source)
XLA Modules:
  0.0 169.2 jit_solution(7690468510807081030)
XLA Ops:
  0.6 2.6 %send_scaled.1 = (bf16[48,1536]{1,0:T(8,128)(2,1)}, bf16[48,1536]{1,0:T(8,128)(2,1)}, bf16[48,1536]{1,0:T(8,128)(2,1)}, bf16[48,1536]{1,0:T(8,128)(2,1)}, bf16[4...) custom-call(s32[1]{0:T(128)} %bitcast.dp_ref, ...), custom_call_target="tpu_custom_call" | custom-call | bytes 1179 | tf_op jit(solution)/shard_map/send_scaled/pallas_call | solution.py:92
  3.2 3.0 %collective-permute-start = (bf16[48,1536]{1,0:T(8,128)(2,1)}, bf16[48,1536]{1,0:T(8,128)(2,1)S(1)}, u32[]{:S(2)}, u32[]{:S(2)}) collective-permute-start(bf16[48,1536]{1,0:T(8,128)(2,1)} %get-tuple-element.62), channel_id=1, source_target_pairs={{0,8},{4,12},{8,0},{12,4},{16,24},{20,28},{24,16},{28,20},{1,9},{5... | collective-permute-start | bytes 442376 | tf_op jit(solution)/shard_map/ppermute | solution.py:38
  6.2 1.4 collective-permute-start.5
  7.8 4.0 %collective-permute-start.7 = (bf16[48,1536]{1,0:T(8,128)(2,1)}, bf16[48,1536]{1,0:T(8,128)(2,1)S(1)}, u32[]{:S(2)}, u32[]{:S(2)}) collective-permute-start(bf16[48,1536]{1,0:T(8,128)(2,1)} %get-tuple-element.72), channel_id=1, source_target_pairs={{0,24},{4,28},{8,16},{12,20},{16,8},{20,12},{24,0},{28,4},{1,25},{... | collective-permute-start | bytes 442376 | tf_op jit(solution)/shard_map/ppermute | solution.py:38
  11.8 1.2 collective-permute-start.8
  12.9 1.0 collective-permute-start.1
  13.9 0.7 collective-permute-done.5.refs_3_
  14.7 3.8 %collective-permute-start.6 = (bf16[48,1536]{1,0:T(8,128)(2,1)}, bf16[48,1536]{1,0:T(8,128)(2,1)S(1)}, u32[]{:S(2)}, u32[]{:S(2)}) collective-permute-start(bf16[48,1536]{1,0:T(8,128)(2,1)} %get-tuple-element.71), channel_id=1, source_target_pairs={{0,20},{4,16},{8,28},{12,24},{16,4},{20,0},{24,12},{28,8},{1,21},{... | collective-permute-start | bytes 442376 | tf_op jit(solution)/shard_map/ppermute | solution.py:38
  18.5 0.8 copy.14
  19.4 1.5 reshape.41.gate_ref
  20.9 1.8 %reshape.42.up_ref = bf16[256,2048]{1,0:T(8,128)(2,1)S(1)} reshape(bf16[128,2,2048]{2,1,0:T(2,128)(2,1)} %param.7) | data formatting | bytes 2097152 | tf_op jit(solution)/shard_map/reshape | solution.py:450
  22.8 2.0 %send_hidden.1 = (bf16[48,2048]{1,0:T(8,128)(2,1)S(1)}, bf16[48,2048]{1,0:T(8,128)(2,1)S(1)}, bf16[48,2048]{1,0:T(8,128)(2,1)S(1)}, bf16[48,2048]{1,0:T(8,128)(2...) custom-call(s32[1]{0:T(128)} %bitcast.dp_ref, ...), custom_call_target="tpu_custom_call" | custom-call | bytes 3670 | tf_op jit(solution)/shard_map/send_hidden/pallas_call | solution.py:126
  24.9 1.5 collective-permute-start.16
  26.4 8.4 %collective-permute-done.1.refs_0_ = bf16[48,1536]{1,0:T(8,128)(2,1)S(1)} collective-permute-done((bf16[48,1536]{1,0:T(8,128)(2,1)}, bf16[48,1536]{1,0:T(8,128)(2,1)S(1)}, u32[]{:S(2)}, u32[]{:S(2)}) %collective-permute-start.1) | collective-permute-done | bytes 147488 | tf_op jit(solution)/shard_map/ppermute | solution.py:38
  34.8 2.4 %collective-permute-done.6.refs_1_ = bf16[48,1536]{1,0:T(8,128)(2,1)S(1)} collective-permute-done((bf16[48,1536]{1,0:T(8,128)(2,1)}, bf16[48,1536]{1,0:T(8,128)(2,1)S(1)}, u32[]{:S(2)}, u32[]{:S(2)}) %collective-permute-start.6) | collective-permute-done | bytes 147488 | tf_op jit(solution)/shard_map/ppermute | solution.py:38
  37.2 1.5 collective-permute-start.17
  38.8 3.3 %collective-permute-start.2 = (bf16[48,2048]{1,0:T(8,128)(2,1)S(1)}, bf16[48,2048]{1,0:T(8,128)(2,1)S(1)}, u32[]{:S(2)}, u32[]{:S(2)}) collective-permute-start(bf16[48,2048]{1,0:T(8,128)(2,1)S(1)} %get-tuple-element.64), channel_id=1, source_target_pairs={{0,24},{4,28},{8,16},{12,20},{16,8},{20,12},{24,0},{28,4},{1,25},{... | collective-permute-start | bytes 589832 | tf_op jit(solution)/shard_map/ppermute | solution.py:38
  42.1 1.0 collective-permute-start.11
  43.0 4.1 %collective-permute-done.2.refs_6_ = bf16[48,2048]{1,0:T(8,128)(2,1)S(1)} collective-permute-done((bf16[48,2048]{1,0:T(8,128)(2,1)S(1)}, bf16[48,2048]{1,0:T(8,128)(2,1)S(1)}, u32[]{:S(2)}, u32[]{:S(2)}) %collective-permute-start.2) | collective-permute-done | bytes 196640 | tf_op jit(solution)/shard_map/ppermute | solution.py:38
  47.1 0.5 collective-permute-start.18
  47.6 3.0 %collective-permute-done.11.refs_7_ = bf16[48,2048]{1,0:T(8,128)(2,1)S(1)} collective-permute-done((bf16[48,2048]{1,0:T(8,128)(2,1)S(1)}, bf16[48,2048]{1,0:T(8,128)(2,1)S(1)}, u32[]{:S(2)}, u32[]{:S(2)}) %collective-permute-start.11) | collective-permute-done | bytes 196640 | tf_op jit(solution)/shard_map/ppermute | solution.py:38
  50.6 0.4 collective-permute-done.17.refs_5_
  51.0 5.8 %collective-permute-start.13 = (bf16[48,2048]{1,0:T(8,128)(2,1)S(1)}, bf16[48,2048]{1,0:T(8,128)(2,1)S(1)}, u32[]{:S(2)}, u32[]{:S(2)}) collective-permute-start(bf16[48,2048]{1,0:T(8,128)(2,1)S(1)} %get-tuple-element.80), channel_id=1, source_target_pairs={{0,20},{4,16},{8,28},{12,24},{16,4},{20,0},{24,12},{28,8},{1,21},{... | collective-permute-start | bytes 589832 | tf_op jit(solution)/shard_map/ppermute | solution.py:38
  56.8 0.4 collective-permute-start.3
  57.2 3.0 %collective-permute-start.12 = (bf16[48,2048]{1,0:T(8,128)(2,1)S(1)}, bf16[48,2048]{1,0:T(8,128)(2,1)S(1)}, u32[]{:S(2)}, u32[]{:S(2)}) collective-permute-start(bf16[48,2048]{1,0:T(8,128)(2,1)S(1)} %get-tuple-element.78), channel_id=1, source_target_pairs={{0,16},{4,20},{8,24},{12,28},{16,0},{20,4},{24,8},{28,12},{1,17},{... | collective-permute-start | bytes 589832 | tf_op jit(solution)/shard_map/ppermute | solution.py:38
  60.3 16.3 %back.1 = (bf16[384,2048]{1,0:T(8,128)(2,1)}, bf16[4,384,1536]{2,1,0:T(8,128)(2,1)S(1)}) custom-call(s32[1]{0:T(128)} %bitcast.dp_ref, s32[1]{0:T(128)} %bitcast.1.hid_ref, bf16[192,1536]{1,0:T(8,128)(2,1)S(1)} %stack.3.refs_0_, bf16[192,1536]{1,0:T(8,128)(2,1)S(1)} %stack.2.refs_1_, bf16[192,1536]{1,0:T(8,128)(2,1)S(1)} %collective-permute-done.15.refs_2_, ...), custom_call_target="tpu_custom_call" | custom-call | flops 9663676 | bytes 31457 | tf_op jit(solution)/shard_map/back/pallas_call | solution.py:304
  76.6 2.2 %copy-done.3 = bf16[4,384,1536]{2,1,0:T(8,128)(2,1)} copy-done((bf16[4,384,1536]{2,1,0:T(8,128)(2,1)}, bf16[4,384,1536]{2,1,0:T(8,128)(2,1)S(1)}, u32[]{:S(2)}) %copy-start.3) | copy-done | bytes 4718616
  78.8 4.3 %all-to-all-start = ((bf16[8,48,2048]{2,1,0:T(8,128)(2,1)}), bf16[8,48,2048]{2,1,0:T(8,128)(2,1)}, u32[]{:S(2)}, u32[]{:S(2)}) async-start(bf16[8,48,2048]{2,1,0:T(8,128)(2,1)} %bitcast.6), calls=%async_computation | async-start | bytes 3145728 | tf_op jit(solution)/shard_map/all_to_all | solution.py:447
  83.1 9.5 %first_down.1 = (bf16[384,1536]{1,0:T(8,128)(2,1)S(1)}, bf16[384,1536]{1,0:T(8,128)(2,1)S(1)}, bf16[384,2048]{1,0:T(8,128)(2,1)S(1)}) custom-call(s32[1]{0:T(128)} %bitcast.dp_ref, s32[1]{0:T(128)} %bitcast.1.hid_ref, bf16[48,2048]{1,0:T(8,128)(2,1)S(1)} %get-tuple-element.86.refs_0_, bf16[48,2048]{1,0:T(8,128)(2,1)S(1)} %collective-permute-done.3.refs_1_, ...), custom_call_target="tpu_custom_call" | custom-call | flops 2415919 | bytes 10223 | tf_op jit(solution)/shard_map/first_down/pallas_call | solution.py:202
  92.7 0.5 collective-permute-start.21
  93.2 2.3 %collective-permute-done.20.refs_0_ = bf16[384,1536]{1,0:T(8,128)(2,1)S(1)} collective-permute-done((bf16[384,1536]{1,0:T(8,128)(2,1)S(1)}, bf16[384,1536]{1,0:T(8,128)(2,1)S(1)}, u32[]{:S(2)}, u32[]{:S(2)}) %collective-permute-start.20) | collective-permute-done | bytes 1179680 | tf_op jit(solution)/shard_map/ppermute | solution.py:38
  95.6 5.4 %down.2 = bf16[384,1536]{1,0:T(8,128)(2,1)S(1)} custom-call(s32[1]{0:T(128)} %bitcast.1.hid_ref, bf16[384,2048]{1,0:T(8,128)(2,1)S(1)} %get-tuple-element.99.x_ref, bf16[2048,6144]{1,0:T(8,128)(2,1)} %bitcast.18, bf16[384,1536]{1,0:T(8,128)(2,1)S(1)} %collective-permute-done.20.refs_0_), custom_call_target="tpu_custom_call" | custom-call | flops 2415919 | bytes 9043 | tf_op jit(solution)/shard_map/down/pallas_call | solution.py:154
  101.0 1.1 collective-permute-start.22
  102.1 5.3 %down.3.a_ref = f32[384,1536]{1,0:T(8,128)S(1)} custom-call(s32[1]{0:T(128)} %bitcast.1.hid_ref, bf16[384,2048]{1,0:T(8,128)(2,1)S(1)} %get-tuple-element.99.x_ref, bf16[2048,6144]{1,0:T(8,128)(2,1)} %bitcast.19, bf16[384,1536]{1,0:T(8,128)(2,1)S(1)} %collective-permute-done.21.refs_0_), custom_call_target="tpu_custom_call" | custom-call | flops 2415919 | bytes 10223 | tf_op jit(solution)/shard_map/down/pallas_call | solution.py:154
  107.4 1.4 copy-done.2
  108.8 16.6 %outer.1.refs_0_ = bf16[1,2048,6144]{2,1,0:T(8,128)(2,1)} custom-call(s32[1]{0:T(128)} %bitcast.1.hid_ref, bf16[384,2048]{1,0:T(8,128)(2,1)S(1)} %get-tuple-element.99.x_ref, bf16[4,384,1536]{2,1,0:T(8,128)(2,1)S(1)} %bitcast.12), custom_call_target="tpu_custom_call" | custom-call | flops 9663676 | bytes 31457 | tf_op jit(solution)/shard_map/outer/pallas_call | solution.py:334
  125.4 3.8 %collective-permute-done.22.b_ref = bf16[384,1536]{1,0:T(8,128)(2,1)} collective-permute-done((bf16[384,1536]{1,0:T(8,128)(2,1)S(1)}, bf16[384,1536]{1,0:T(8,128)(2,1)}, u32[]{:S(2)}, u32[]{:S(2)}) %collective-permute-start.22) | collective-permute-done | bytes 1179680 | tf_op jit(solution)/shard_map/ppermute | solution.py:38
  129.1 2.9 %sum_of.1 = bf16[384,1536]{1,0:T(8,128)(2,1)} custom-call(f32[384,1536]{1,0:T(8,128)} %copy-done.2, bf16[384,1536]{1,0:T(8,128)(2,1)} %collective-permute-done.22.b_ref), custom_call_target="tpu_custom_call" | custom-call | bytes 4718 | tf_op jit(solution)/shard_map/sum_of/pallas_call | solution.py:235
  132.0 6.0 %all-to-all-start.1 = ((bf16[8,48,1536]{2,1,0:T(8,128)(2,1)}), bf16[8,48,1536]{2,1,0:T(8,128)(2,1)}, u32[]{:S(2)}, u32[]{:S(2)}) async-start(bf16[8,48,1536]{2,1,0:T(8,128)(2,1)} %bitcast.20), calls=%async_computation.1 | async-start | bytes 2359296 | tf_op jit(solution)/shard_map/all_to_all | solution.py:447
  138.1 5.4 %grads.1 = (bf16[256,2048]{1,0:T(8,128)(2,1)}, bf16[256,2048]{1,0:T(8,128)(2,1)}, f32[256,1]{1,0:T(8,128)}) custom-call(s32[1,256]{1,0:T(1,128)} %copy-done.8, bf16[256,2048]{1,0:T(8,128)(2,1)} %copy-done, bf16[256,2048]{1,0:T(8,128)(2,1)} %copy-done.1, bf16[384,2048]{1,0:T(8,128)(2,1)} %bitcast.7.back_ref), custom_call_target="tpu_custom_call" | custom-call | bytes 5767 | tf_op jit(solution)/shard_map/grads/pallas_call | solution.py:374
  143.6 1.0 reduce
  144.9 1.2 collective-permute-done.23
  146.1 1.2 collective-permute-start.24
  147.3 1.7 %reshape.43.refs_1_ = bf16[128,2,2048]{2,1,0:T(2,128)(2,1)S(1)} reshape(bf16[256,2048]{1,0:T(8,128)(2,1)} %get-tuple-element.106) | data formatting | bytes 2097152 | tf_op jit(solution)/shard_map/reshape | solution.py:505
  149.1 2.1 %reshape.44.refs_2_ = bf16[128,2,2048]{2,1,0:T(2,128)(2,1)S(1)} reshape(bf16[256,2048]{1,0:T(8,128)(2,1)} %get-tuple-element.107) | data formatting | bytes 2097152 | tf_op jit(solution)/shard_map/reshape | solution.py:505
  151.3 0.8 copy.16
  152.1 14.3 %all-to-all-done.1 = bf16[8,48,1536]{2,1,0:T(8,128)(2,1)} async-done(((bf16[8,48,1536]{2,1,0:T(8,128)(2,1)}), bf16[8,48,1536]{2,1,0:T(8,128)(2,1)}, u32[]{:S(2)}, u32[]{:S(2)}) %all-to-all-start.1) | async-done | bytes 1179680 | tf_op jit(solution)/shard_map/all_to_all | solution.py:447
  166.4 2.8 %mixed.1 = bf16[1,128,1536]{2,1,0:T(8,128)(2,1)} custom-call(s32[2,128]{1,0:T(2,128)S(1)} %copy-done.9, f32[2,128]{1,0:T(2,128)S(1)} %bitcast.14, bf16[384,1536]{1,0:T(8,128)(2,1)} %bitcast.9.x_ref, bf16[1,2048,6144]{2,1,0:T(8,128)(2,1)} %outer.1.refs_0_, bf16[128,2,2048]{2,1,0:T(2,128)(2,1)S(1)} %reshape.43.refs_1_, ...), custom_call_target="tpu_custom_call" | custom-call | bytes 1572 | tf_op jit(solution)/shard_map/mixed/pallas_call | solution.py:420
  (56 shorter events, 1.0 us)
Async XLA Ops:
  3.2 9.7 %collective-permute-start = (bf16[48,1536]{1,0:T(8,128)(2,1)}, bf16[48,1536]{1,0:T(8,128)(2,1)S(1)}, u32[]{:S(2)}, u32[]{:S(2)}) collective-permute-start(bf16[48,1536]{1,0:T(8,128)(2,1)} %get-tuple-element.62), channel_id=1, source_target_pairs={{0,8},{4,12},{8,0},{12,4},{16,24},{20,28},{24,16},{28,20},{1,9},{5... | collective-permute-start | bytes 442376 | tf_op jit(solution)/shard_map/ppermute | solution.py:38
  6.2 8.4 %collective-permute-start.5 = (bf16[48,1536]{1,0:T(8,128)(2,1)}, bf16[48,1536]{1,0:T(8,128)(2,1)S(1)}, u32[]{:S(2)}, u32[]{:S(2)}) collective-permute-start(bf16[48,1536]{1,0:T(8,128)(2,1)} %get-tuple-element.70), channel_id=1, source_target_pairs={{0,12},{4,8},{8,4},{12,0},{16,28},{20,24},{24,20},{28,16},{1,13},{... | collective-permute-start | bytes 442376 | tf_op jit(solution)/shard_map/ppermute | solution.py:38
  7.6 17.1 %collective-permute-start.14 = (bf16[48,1536]{1,0:T(8,128)(2,1)}, bf16[48,1536]{1,0:T(8,128)(2,1)S(1)}, u32[]{:S(2)}, u32[]{:S(2)}) collective-permute-start(bf16[48,1536]{1,0:T(8,128)(2,1)} %get-tuple-element.82), channel_id=1, source_target_pairs={{0,4},{4,0},{8,12},{12,8},{16,20},{20,16},{24,28},{28,24},{1,5},{5... | collective-permute-start | bytes 442376 | tf_op jit(solution)/shard_map/ppermute | solution.py:38
  7.8 18.6 %collective-permute-start.7 = (bf16[48,1536]{1,0:T(8,128)(2,1)}, bf16[48,1536]{1,0:T(8,128)(2,1)S(1)}, u32[]{:S(2)}, u32[]{:S(2)}) collective-permute-start(bf16[48,1536]{1,0:T(8,128)(2,1)} %get-tuple-element.72), channel_id=1, source_target_pairs={{0,24},{4,28},{8,16},{12,20},{16,8},{20,12},{24,0},{28,4},{1,25},{... | collective-permute-start | bytes 442376 | tf_op jit(solution)/shard_map/ppermute | solution.py:38
  11.8 14.6 %collective-permute-start.8 = (bf16[48,1536]{1,0:T(8,128)(2,1)}, bf16[48,1536]{1,0:T(8,128)(2,1)S(1)}, u32[]{:S(2)}, u32[]{:S(2)}) collective-permute-start(bf16[48,1536]{1,0:T(8,128)(2,1)} %get-tuple-element.73), channel_id=1, source_target_pairs={{0,28},{4,24},{8,20},{12,16},{16,12},{20,8},{24,4},{28,0},{1,29},{... | collective-permute-start | bytes 442376 | tf_op jit(solution)/shard_map/ppermute | solution.py:38
  12.9 21.9 %collective-permute-start.1 = (bf16[48,1536]{1,0:T(8,128)(2,1)}, bf16[48,1536]{1,0:T(8,128)(2,1)S(1)}, u32[]{:S(2)}, u32[]{:S(2)}) collective-permute-start(bf16[48,1536]{1,0:T(8,128)(2,1)} %get-tuple-element.63), channel_id=1, source_target_pairs={{0,16},{4,20},{8,24},{12,28},{16,0},{20,4},{24,8},{28,12},{1,17},{... | collective-permute-start | bytes 442376 | tf_op jit(solution)/shard_map/ppermute | solution.py:38
  14.7 22.5 %collective-permute-start.6 = (bf16[48,1536]{1,0:T(8,128)(2,1)}, bf16[48,1536]{1,0:T(8,128)(2,1)S(1)}, u32[]{:S(2)}, u32[]{:S(2)}) collective-permute-start(bf16[48,1536]{1,0:T(8,128)(2,1)} %get-tuple-element.71), channel_id=1, source_target_pairs={{0,20},{4,16},{8,28},{12,24},{16,4},{20,0},{24,12},{28,8},{1,21},{... | collective-permute-start | bytes 442376 | tf_op jit(solution)/shard_map/ppermute | solution.py:38
  19.4 3.4 %copy-start.8 = (s32[1,256]{1,0:T(1,128)}, s32[1,256]{1,0:T(1,128)S(1)}, u32[]{:S(2)}) copy-start(s32[1,256]{1,0:T(1,128)S(1)} %reshape.40.key_ref) | copy-start | bytes 3076
  20.9 3.9 %copy-start = (bf16[256,2048]{1,0:T(8,128)(2,1)}, bf16[256,2048]{1,0:T(8,128)(2,1)S(1)}, u32[]{:S(2)}) copy-start(bf16[256,2048]{1,0:T(8,128)(2,1)S(1)} %reshape.41.gate_ref) | copy-start | bytes 3145732
  22.8 2.1 %copy-start.1 = (bf16[256,2048]{1,0:T(8,128)(2,1)}, bf16[256,2048]{1,0:T(8,128)(2,1)S(1)}, u32[]{:S(2)}) copy-start(bf16[256,2048]{1,0:T(8,128)(2,1)S(1)} %reshape.42.up_ref) | copy-start | bytes 3145732
  22.8 2.0 %copy-start.6 = (bf16[48,1536]{1,0:T(8,128)(2,1)S(1)}, bf16[48,1536]{1,0:T(8,128)(2,1)}, u32[]{:S(2)}) copy-start(bf16[48,1536]{1,0:T(8,128)(2,1)} %get-tuple-element.81.refs_0_) | copy-start | bytes 442372
  24.9 22.3 %collective-permute-start.16 = (bf16[192,1536]{1,0:T(8,128)(2,1)S(1)}, bf16[192,1536]{1,0:T(8,128)(2,1)S(1)}, u32[]{:S(2)}, u32[]{:S(2)}) collective-permute-start(bf16[192,1536]{1,0:T(8,128)(2,1)S(1)} %stack.3.refs_0_), channel_id=1, source_target_pairs={{0,2},{1,3},{2,0},{3,1},{4,6},{5,7},{6,4},{7,5},{8,10},{9,11},{10,... | collective-permute-start | bytes 1769480 | tf_op jit(solution)/shard_map/ppermute | solution.py:38
  37.2 13.7 %collective-permute-start.17 = (bf16[192,1536]{1,0:T(8,128)(2,1)S(1)}, bf16[192,1536]{1,0:T(8,128)(2,1)S(1)}, u32[]{:S(2)}, u32[]{:S(2)}) collective-permute-start(bf16[192,1536]{1,0:T(8,128)(2,1)S(1)} %stack.2.refs_1_), channel_id=1, source_target_pairs={{0,2},{1,3},{2,0},{3,1},{4,6},{5,7},{6,4},{7,5},{8,10},{9,11},{10,... | collective-permute-start | bytes 1769480 | tf_op jit(solution)/shard_map/ppermute | solution.py:38
  38.8 8.3 %collective-permute-start.2 = (bf16[48,2048]{1,0:T(8,128)(2,1)S(1)}, bf16[48,2048]{1,0:T(8,128)(2,1)S(1)}, u32[]{:S(2)}, u32[]{:S(2)}) collective-permute-start(bf16[48,2048]{1,0:T(8,128)(2,1)S(1)} %get-tuple-element.64), channel_id=1, source_target_pairs={{0,24},{4,28},{8,16},{12,20},{16,8},{20,12},{24,0},{28,4},{1,25},{... | collective-permute-start | bytes 589832 | tf_op jit(solution)/shard_map/ppermute | solution.py:38
  42.1 8.5 %collective-permute-start.11 = (bf16[48,2048]{1,0:T(8,128)(2,1)S(1)}, bf16[48,2048]{1,0:T(8,128)(2,1)S(1)}, u32[]{:S(2)}, u32[]{:S(2)}) collective-permute-start(bf16[48,2048]{1,0:T(8,128)(2,1)S(1)} %get-tuple-element.77), channel_id=1, source_target_pairs={{0,28},{4,24},{8,20},{12,16},{16,12},{20,8},{24,4},{28,0},{1,29},{... | collective-permute-start | bytes 589832 | tf_op jit(solution)/shard_map/ppermute | solution.py:38
  43.0 13.7 %collective-permute-start.9 = (bf16[192,1536]{1,0:T(8,128)(2,1)S(1)}, bf16[192,1536]{1,0:T(8,128)(2,1)S(1)}, u32[]{:S(2)}, u32[]{:S(2)}) collective-permute-start(bf16[192,1536]{1,0:T(8,128)(2,1)S(1)} %stack.2.refs_1_), channel_id=1, source_target_pairs={{0,1},{1,0},{2,3},{3,2},{4,5},{5,4},{6,7},{7,6},{8,9},{9,8},{10,11... | collective-permute-start | bytes 1769480 | tf_op jit(solution)/shard_map/ppermute | solution.py:38
  47.1 10.1 %collective-permute-start.15 = (bf16[192,1536]{1,0:T(8,128)(2,1)S(1)}, bf16[192,1536]{1,0:T(8,128)(2,1)S(1)}, u32[]{:S(2)}, u32[]{:S(2)}) collective-permute-start(bf16[192,1536]{1,0:T(8,128)(2,1)S(1)} %stack.3.refs_0_), channel_id=1, source_target_pairs={{0,1},{1,0},{2,3},{3,2},{4,5},{5,4},{6,7},{7,6},{8,9},{9,8},{10,11... | collective-permute-start | bytes 1769480 | tf_op jit(solution)/shard_map/ppermute | solution.py:38
  47.1 10.1 %collective-permute-start.18 = (bf16[192,1536]{1,0:T(8,128)(2,1)S(1)}, bf16[192,1536]{1,0:T(8,128)(2,1)S(1)}, u32[]{:S(2)}, u32[]{:S(2)}) collective-permute-start(bf16[192,1536]{1,0:T(8,128)(2,1)S(1)} %collective-permute-done.16.refs_4_), channel_id=1, source_target_pairs={{0,1},{1,0},{2,3},{3,2},{4,5},{5,4},{6,7},{7,6},{8,9},{9,8},{10,11... | collective-permute-start | bytes 1769480 | tf_op jit(solution)/shard_map/ppermute | solution.py:38
  51.0 9.2 %collective-permute-start.19 = (bf16[192,1536]{1,0:T(8,128)(2,1)S(1)}, bf16[192,1536]{1,0:T(8,128)(2,1)S(1)}, u32[]{:S(2)}, u32[]{:S(2)}) collective-permute-start(bf16[192,1536]{1,0:T(8,128)(2,1)S(1)} %collective-permute-done.17.refs_5_), channel_id=1, source_target_pairs={{0,1},{1,0},{2,3},{3,2},{4,5},{5,4},{6,7},{7,6},{8,9},{9,8},{10,11... | collective-permute-start | bytes 1769480 | tf_op jit(solution)/shard_map/ppermute | solution.py:38
  51.0 27.8 %collective-permute-start.13 = (bf16[48,2048]{1,0:T(8,128)(2,1)S(1)}, bf16[48,2048]{1,0:T(8,128)(2,1)S(1)}, u32[]{:S(2)}, u32[]{:S(2)}) collective-permute-start(bf16[48,2048]{1,0:T(8,128)(2,1)S(1)} %get-tuple-element.80), channel_id=1, source_target_pairs={{0,20},{4,16},{8,28},{12,24},{16,4},{20,0},{24,12},{28,8},{1,21},{... | collective-permute-start | bytes 589832 | tf_op jit(solution)/shard_map/ppermute | solution.py:38
  56.8 22.0 %collective-permute-start.3 = (bf16[48,2048]{1,0:T(8,128)(2,1)S(1)}, bf16[48,2048]{1,0:T(8,128)(2,1)S(1)}, u32[]{:S(2)}, u32[]{:S(2)}) collective-permute-start(bf16[48,2048]{1,0:T(8,128)(2,1)S(1)} %get-tuple-element.65), channel_id=1, source_target_pairs={{0,4},{4,0},{8,12},{12,8},{16,20},{20,16},{24,28},{28,24},{1,5},{5... | collective-permute-start | bytes 589832 | tf_op jit(solution)/shard_map/ppermute | solution.py:38
  57.2 21.6 %collective-permute-start.4 = (bf16[48,2048]{1,0:T(8,128)(2,1)S(1)}, bf16[48,2048]{1,0:T(8,128)(2,1)S(1)}, u32[]{:S(2)}, u32[]{:S(2)}) collective-permute-start(bf16[48,2048]{1,0:T(8,128)(2,1)S(1)} %get-tuple-element.67), channel_id=1, source_target_pairs={{0,8},{4,12},{8,0},{12,4},{16,24},{20,28},{24,16},{28,20},{1,9},{5... | collective-permute-start | bytes 589832 | tf_op jit(solution)/shard_map/ppermute | solution.py:38
  57.2 21.6 %collective-permute-start.12 = (bf16[48,2048]{1,0:T(8,128)(2,1)S(1)}, bf16[48,2048]{1,0:T(8,128)(2,1)S(1)}, u32[]{:S(2)}, u32[]{:S(2)}) collective-permute-start(bf16[48,2048]{1,0:T(8,128)(2,1)S(1)} %get-tuple-element.78), channel_id=1, source_target_pairs={{0,16},{4,20},{8,24},{12,28},{16,0},{20,4},{24,8},{28,12},{1,17},{... | collective-permute-start | bytes 589832 | tf_op jit(solution)/shard_map/ppermute | solution.py:38
  60.2 18.6 %collective-permute-start.10 = (bf16[48,2048]{1,0:T(8,128)(2,1)S(1)}, bf16[48,2048]{1,0:T(8,128)(2,1)S(1)}, u32[]{:S(2)}, u32[]{:S(2)}) collective-permute-start(bf16[48,2048]{1,0:T(8,128)(2,1)S(1)} %get-tuple-element.74), channel_id=1, source_target_pairs={{0,12},{4,8},{8,4},{12,0},{16,28},{20,24},{24,20},{28,16},{1,13},{... | collective-permute-start | bytes 589832 | tf_op jit(solution)/shard_map/ppermute | solution.py:38
  76.6 2.2 %copy-start.3 = (bf16[4,384,1536]{2,1,0:T(8,128)(2,1)}, bf16[4,384,1536]{2,1,0:T(8,128)(2,1)S(1)}, u32[]{:S(2)}) copy-start(bf16[4,384,1536]{2,1,0:T(8,128)(2,1)S(1)} %get-tuple-element.100.y_ref) | copy-start | bytes 14155780
  78.8 46.5 %all-to-all-start = ((bf16[8,48,2048]{2,1,0:T(8,128)(2,1)}), bf16[8,48,2048]{2,1,0:T(8,128)(2,1)}, u32[]{:S(2)}, u32[]{:S(2)}) async-start(bf16[8,48,2048]{2,1,0:T(8,128)(2,1)} %bitcast.6), calls=%async_computation | async-start | bytes 3145728 | tf_op jit(solution)/shard_map/all_to_all | solution.py:447
  92.7 2.9 %collective-permute-start.20 = (bf16[384,1536]{1,0:T(8,128)(2,1)S(1)}, bf16[384,1536]{1,0:T(8,128)(2,1)S(1)}, u32[]{:S(2)}, u32[]{:S(2)}) collective-permute-start(bf16[384,1536]{1,0:T(8,128)(2,1)S(1)} %get-tuple-element.95), channel_id=1, source_target_pairs={{0,1},{1,0},{2,3},{3,2},{4,5},{5,4},{6,7},{7,6},{8,9},{9,8},{10,11... | collective-permute-start | bytes 3538952 | tf_op jit(solution)/shard_map/ppermute | solution.py:38
  92.7 9.3 %collective-permute-start.21 = (bf16[384,1536]{1,0:T(8,128)(2,1)S(1)}, bf16[384,1536]{1,0:T(8,128)(2,1)S(1)}, u32[]{:S(2)}, u32[]{:S(2)}) collective-permute-start(bf16[384,1536]{1,0:T(8,128)(2,1)S(1)} %get-tuple-element.97), channel_id=1, source_target_pairs={{0,1},{1,0},{2,3},{3,2},{4,5},{5,4},{6,7},{7,6},{8,9},{9,8},{10,11... | collective-permute-start | bytes 3538952 | tf_op jit(solution)/shard_map/ppermute | solution.py:38
  95.6 13.2 %slice-start = ((s8[4718592]{0:T(1024)(128)(4,1)}), s8[4194304]{0:T(1024)(128)(4,1)S(1)}, s32[]{:S(2)}) async-start(s8[4718592]{0:T(1024)(128)(4,1)} %bitcast.11), calls=%async_computation.2 | async-start | bytes 8388608
  100.9 7.9 %slice-start.1 = ((s8[4718592]{0:T(1024)(128)(4,1)}), s8[524288]{0:T(1024)(128)(4,1)S(1)}, s32[]{:S(2)}) async-start(s8[4718592]{0:T(1024)(128)(4,1)} %bitcast.11), calls=%async_computation.3 | async-start | bytes 1048576
  101.0 28.2 %collective-permute-start.22 = (bf16[384,1536]{1,0:T(8,128)(2,1)S(1)}, bf16[384,1536]{1,0:T(8,128)(2,1)}, u32[]{:S(2)}, u32[]{:S(2)}) collective-permute-start(bf16[384,1536]{1,0:T(8,128)(2,1)S(1)} %down.2), channel_id=1, source_target_pairs={{0,2},{1,3},{2,0},{3,1},{4,6},{5,7},{6,4},{7,5},{8,10},{9,11},{10,... | collective-permute-start | bytes 3538952 | tf_op jit(solution)/shard_map/ppermute | solution.py:38
  107.4 1.4 copy-start.2
  132.0 6.0 %copy-start.7 = (f32[128,2]{0,1:T(2,128)S(1)}, f32[128,2]{0,1:T(2,128)}, u32[]{:S(2)}) copy-start(f32[128,2]{0,1:T(2,128)} %param.9) | copy-start | bytes 3076
  132.0 34.3 %all-to-all-start.1 = ((bf16[8,48,1536]{2,1,0:T(8,128)(2,1)}), bf16[8,48,1536]{2,1,0:T(8,128)(2,1)}, u32[]{:S(2)}, u32[]{:S(2)}) async-start(bf16[8,48,1536]{2,1,0:T(8,128)(2,1)} %bitcast.20), calls=%async_computation.1 | async-start | bytes 2359296 | tf_op jit(solution)/shard_map/all_to_all | solution.py:447
  144.8 1.3 collective-permute-start.23
  146.1 5.1 %collective-permute-start.24 = (f32[128,2]{1,0:T(8,128)S(1)}, f32[128,2]{1,0:T(8,128)S(1)}, u32[]{:S(2)}, u32[]{:S(2)}) collective-permute-start(f32[128,2]{1,0:T(8,128)S(1)} %add.6), channel_id=1, source_target_pairs={{0,2},{1,3},{2,0},{3,1},{4,6},{5,7},{6,4},{7,5},{8,10},{9,11},{10,... | collective-permute-start | bytes 3080 | tf_op jit(solution)/shard_map/ppermute | solution.py:38
  149.1 20.1 %copy-start.4 = (bf16[128,2,2048]{2,1,0:T(2,128)(2,1)}, bf16[128,2,2048]{2,1,0:T(2,128)(2,1)S(1)}, u32[]{:S(2)}) copy-start(bf16[128,2,2048]{2,1,0:T(2,128)(2,1)S(1)} %reshape.43.refs_1_) | copy-start | bytes 3145732
  149.1 17.3 %copy-start.9 = (s32[2,128]{1,0:T(2,128)S(1)}, s32[2,128]{1,0:T(2,128)}, u32[]{:S(2)}) copy-start(s32[2,128]{1,0:T(2,128)} %get-tuple-element.57.key_ref) | copy-start | bytes 3076
  151.2 17.9 %copy-start.5 = (bf16[128,2,2048]{2,1,0:T(2,128)(2,1)}, bf16[128,2,2048]{2,1,0:T(2,128)(2,1)S(1)}, u32[]{:S(2)}) copy-start(bf16[128,2,2048]{2,1,0:T(2,128)(2,1)S(1)} %reshape.44.refs_2_) | copy-start | bytes 3145732

commit v6 on v5

--- a/solution.py
+++ b/solution.py
@@ -485,8 +485,12 @@
     got_back = over_dp(sent_back)
     others = []
     odd = list(range(hid_count - 1, 0, -2))
-    *away, x = first_down(my_dp, my_hid, got_hidden, weights, odd, quarter)
-    sums = {q: swap(made, "hid", 1) for q, made in zip(odd, away)}
+    made, x = first_down(my_dp, my_hid, got_hidden, weights, odd[:1], quarter)
+    sums = {odd[0]: swap(made, "hid", 1)}
+    for q in odd[1:]:
+        made = down(my_hid, x, weights, q, quarter, BF16, PARAMS)
+        sums[q] = swap(made, "hid", 1)
+    x = lax.optimization_barrier((x, made))[0]
     for q in range(hid_count - 2, 0, -2):
         made = down(my_hid, x, weights, q, quarter, BF16, PARAMS, sums[q + 1])
         others.append(swap(made, "hid", q))

time: 170 us -> 169 us (level)
  waiting for transfers between devices: 40.6 us -> 38.2 us
    pallas_call x2 -> x3, Pallas kernels: 10.6 us -> 15.8 us  [down(): pl.pallas_call(functools.partial(down_kernel, len(add)), grid_spec=pltpu....]
    pallas_call x1, Pallas kernels: 9.51 us -> 5.47 us  [first_down(): pl.pallas_call(functools.partial(first_down_kernel, len(blocks), per), gr...]
    ppermute x25, waiting for transfers between devices: 26.3 us -> 23.9 us  [swap(): return lax.ppermute(x, axis, [(i, i ^ bit) for i in range(count)])]
  transfers between devices with their start and end apart: 27 -> 27, of which waited for: 10 -> 9; matrix products, arithmetic and copies ran while one was open for 6% -> 6% of each run, Pallas kernels for 36% -> 37%
where the time goes in v6:
time: 169 us; the launch traced here: 168 us
  Pallas kernels  69.9 us (41%)
  starting transfers between devices  45.1 us (27%)
  waiting for transfers between devices  38.2 us (23%)
  local copies, waits for them, and re-layouts  12.8 us (8%)
    ppermute x25, starting transfers between devices, swap(): return lax.ppermute(x, axis, [(i, i ^ bit) for i in range(count)])  34.8 us
    ppermute x25, waiting for transfers between devices, swap(): return lax.ppermute(x, axis, [(i, i ^ bit) for i in range(count)])  23.9 us
    pallas_call x1, Pallas kernels, outer(): pl.pallas_call(outer_kernel, grid_spec=pltpu.PrefetchScalarGridSpec(num_s...  16.6 us
    pallas_call x1, Pallas kernels, back(): pl.pallas_call(back_kernel, grid_spec=pltpu.PrefetchScalarGridSpec(num_sc...  16.3 us
    pallas_call x3, Pallas kernels, down(): pl.pallas_call(functools.partial(down_kernel, len(add)), grid_spec=pltpu....  15.8 us
    all_to_all x2, waiting for transfers between devices, over_dp(): return lax.all_to_all(x, 'dp', split_axis=0, concat_axis=0, tiled=True)  14.2 us
    all_to_all x2, starting transfers between devices, over_dp(): return lax.all_to_all(x, 'dp', split_axis=0, concat_axis=0, tiled=True)  10.3 us
    pallas_call x1, Pallas kernels, first_down(): pl.pallas_call(functools.partial(first_down_kernel, len(blocks), per), gr...  5.47 us
  transfers between devices with their start and end apart: 27, of which 9 were waited for; matrix products, arithmetic and copies ran while one was open for 6% of the time, Pallas kernels for 37%

profile of v6, /device:TPU:0, one launch (start us, length us, event | category | flops | bytes accessed | tf_op | source)
XLA Modules:
  0.0 167.9 jit_solution(4516313680054476057)
XLA Ops:
  0.6 2.6 %send_scaled.1 = (bf16[48,1536]{1,0:T(8,128)(2,1)}, bf16[48,1536]{1,0:T(8,128)(2,1)}, bf16[48,1536]{1,0:T(8,128)(2,1)}, bf16[48,1536]{1,0:T(8,128)(2,1)}, bf16[4...) custom-call(s32[1]{0:T(128)} %bitcast.dp_ref, ...), custom_call_target="tpu_custom_call" | custom-call | bytes 1179 | tf_op jit(solution)/shard_map/send_scaled/pallas_call | solution.py:92
  3.2 3.0 %collective-permute-start = (bf16[48,1536]{1,0:T(8,128)(2,1)}, bf16[48,1536]{1,0:T(8,128)(2,1)S(1)}, u32[]{:S(2)}, u32[]{:S(2)}) collective-permute-start(bf16[48,1536]{1,0:T(8,128)(2,1)} %get-tuple-element.62), channel_id=1, source_target_pairs={{0,8},{4,12},{8,0},{12,4},{16,24},{20,28},{24,16},{28,20},{1,9},{5... | collective-permute-start | bytes 442376 | tf_op jit(solution)/shard_map/ppermute | solution.py:38
  6.2 1.4 collective-permute-start.5
  7.8 4.0 %collective-permute-start.7 = (bf16[48,1536]{1,0:T(8,128)(2,1)}, bf16[48,1536]{1,0:T(8,128)(2,1)S(1)}, u32[]{:S(2)}, u32[]{:S(2)}) collective-permute-start(bf16[48,1536]{1,0:T(8,128)(2,1)} %get-tuple-element.72), channel_id=1, source_target_pairs={{0,24},{4,28},{8,16},{12,20},{16,8},{20,12},{24,0},{28,4},{1,25},{... | collective-permute-start | bytes 442376 | tf_op jit(solution)/shard_map/ppermute | solution.py:38
  11.8 1.2 collective-permute-start.8
  12.9 1.0 collective-permute-start.1
  13.9 0.7 collective-permute-done.5.refs_3_
  14.7 3.8 %collective-permute-start.6 = (bf16[48,1536]{1,0:T(8,128)(2,1)}, bf16[48,1536]{1,0:T(8,128)(2,1)S(1)}, u32[]{:S(2)}, u32[]{:S(2)}) collective-permute-start(bf16[48,1536]{1,0:T(8,128)(2,1)} %get-tuple-element.71), channel_id=1, source_target_pairs={{0,20},{4,16},{8,28},{12,24},{16,4},{20,0},{24,12},{28,8},{1,21},{... | collective-permute-start | bytes 442376 | tf_op jit(solution)/shard_map/ppermute | solution.py:38
  18.5 0.8 copy.14
  19.4 1.5 reshape.41.gate_ref
  20.9 1.8 %reshape.42.up_ref = bf16[256,2048]{1,0:T(8,128)(2,1)S(1)} reshape(bf16[128,2,2048]{2,1,0:T(2,128)(2,1)} %param.7) | data formatting | bytes 2097152 | tf_op jit(solution)/shard_map/reshape | solution.py:450
  22.8 2.0 %send_hidden.1 = (bf16[48,2048]{1,0:T(8,128)(2,1)S(1)}, bf16[48,2048]{1,0:T(8,128)(2,1)S(1)}, bf16[48,2048]{1,0:T(8,128)(2,1)S(1)}, bf16[48,2048]{1,0:T(8,128)(2...) custom-call(s32[1]{0:T(128)} %bitcast.dp_ref, ...), custom_call_target="tpu_custom_call" | custom-call | bytes 3670 | tf_op jit(solution)/shard_map/send_hidden/pallas_call | solution.py:126
  24.9 1.5 collective-permute-start.16
  26.4 8.4 %collective-permute-done.1.refs_0_ = bf16[48,1536]{1,0:T(8,128)(2,1)S(1)} collective-permute-done((bf16[48,1536]{1,0:T(8,128)(2,1)}, bf16[48,1536]{1,0:T(8,128)(2,1)S(1)}, u32[]{:S(2)}, u32[]{:S(2)}) %collective-permute-start.1) | collective-permute-done | bytes 147488 | tf_op jit(solution)/shard_map/ppermute | solution.py:38
  34.8 2.4 %collective-permute-done.6.refs_1_ = bf16[48,1536]{1,0:T(8,128)(2,1)S(1)} collective-permute-done((bf16[48,1536]{1,0:T(8,128)(2,1)}, bf16[48,1536]{1,0:T(8,128)(2,1)S(1)}, u32[]{:S(2)}, u32[]{:S(2)}) %collective-permute-start.6) | collective-permute-done | bytes 147488 | tf_op jit(solution)/shard_map/ppermute | solution.py:38
  37.2 1.5 collective-permute-start.17
  38.8 3.3 %collective-permute-start.2 = (bf16[48,2048]{1,0:T(8,128)(2,1)S(1)}, bf16[48,2048]{1,0:T(8,128)(2,1)S(1)}, u32[]{:S(2)}, u32[]{:S(2)}) collective-permute-start(bf16[48,2048]{1,0:T(8,128)(2,1)S(1)} %get-tuple-element.64), channel_id=1, source_target_pairs={{0,24},{4,28},{8,16},{12,20},{16,8},{20,12},{24,0},{28,4},{1,25},{... | collective-permute-start | bytes 589832 | tf_op jit(solution)/shard_map/ppermute | solution.py:38
  42.1 1.0 collective-permute-start.11
  43.0 4.1 %collective-permute-done.2.refs_6_ = bf16[48,2048]{1,0:T(8,128)(2,1)S(1)} collective-permute-done((bf16[48,2048]{1,0:T(8,128)(2,1)S(1)}, bf16[48,2048]{1,0:T(8,128)(2,1)S(1)}, u32[]{:S(2)}, u32[]{:S(2)}) %collective-permute-start.2) | collective-permute-done | bytes 196640 | tf_op jit(solution)/shard_map/ppermute | solution.py:38
  47.1 0.5 collective-permute-start.18
  47.6 3.0 %collective-permute-done.11.refs_7_ = bf16[48,2048]{1,0:T(8,128)(2,1)S(1)} collective-permute-done((bf16[48,2048]{1,0:T(8,128)(2,1)S(1)}, bf16[48,2048]{1,0:T(8,128)(2,1)S(1)}, u32[]{:S(2)}, u32[]{:S(2)}) %collective-permute-start.11) | collective-permute-done | bytes 196640 | tf_op jit(solution)/shard_map/ppermute | solution.py:38
  50.6 0.4 collective-permute-done.17.refs_5_
  51.0 5.8 %collective-permute-start.13 = (bf16[48,2048]{1,0:T(8,128)(2,1)S(1)}, bf16[48,2048]{1,0:T(8,128)(2,1)S(1)}, u32[]{:S(2)}, u32[]{:S(2)}) collective-permute-start(bf16[48,2048]{1,0:T(8,128)(2,1)S(1)} %get-tuple-element.80), channel_id=1, source_target_pairs={{0,20},{4,16},{8,28},{12,24},{16,4},{20,0},{24,12},{28,8},{1,21},{... | collective-permute-start | bytes 589832 | tf_op jit(solution)/shard_map/ppermute | solution.py:38
  56.8 0.4 collective-permute-start.3
  57.2 3.0 %collective-permute-start.12 = (bf16[48,2048]{1,0:T(8,128)(2,1)S(1)}, bf16[48,2048]{1,0:T(8,128)(2,1)S(1)}, u32[]{:S(2)}, u32[]{:S(2)}) collective-permute-start(bf16[48,2048]{1,0:T(8,128)(2,1)S(1)} %get-tuple-element.78), channel_id=1, source_target_pairs={{0,16},{4,20},{8,24},{12,28},{16,0},{20,4},{24,8},{28,12},{1,17},{... | collective-permute-start | bytes 589832 | tf_op jit(solution)/shard_map/ppermute | solution.py:38
  60.3 16.3 %back.1 = (bf16[384,2048]{1,0:T(8,128)(2,1)}, bf16[4,384,1536]{2,1,0:T(8,128)(2,1)S(1)}) custom-call(s32[1]{0:T(128)} %bitcast.dp_ref, s32[1]{0:T(128)} %bitcast.1.hid_ref, bf16[192,1536]{1,0:T(8,128)(2,1)S(1)} %stack.3.refs_0_, bf16[192,1536]{1,0:T(8,128)(2,1)S(1)} %stack.2.refs_1_, bf16[192,1536]{1,0:T(8,128)(2,1)S(1)} %collective-permute-done.15.refs_2_, ...), custom_call_target="tpu_custom_call" | custom-call | flops 9663676 | bytes 31457 | tf_op jit(solution)/shard_map/back/pallas_call | solution.py:304
  76.6 2.2 %copy-done.3 = bf16[4,384,1536]{2,1,0:T(8,128)(2,1)} copy-done((bf16[4,384,1536]{2,1,0:T(8,128)(2,1)}, bf16[4,384,1536]{2,1,0:T(8,128)(2,1)S(1)}, u32[]{:S(2)}) %copy-start.3) | copy-done | bytes 4718616
  78.8 4.3 %all-to-all-start = ((bf16[8,48,2048]{2,1,0:T(8,128)(2,1)}), bf16[8,48,2048]{2,1,0:T(8,128)(2,1)}, u32[]{:S(2)}, u32[]{:S(2)}) async-start(bf16[8,48,2048]{2,1,0:T(8,128)(2,1)} %bitcast.6), calls=%async_computation | async-start | bytes 3145728 | tf_op jit(solution)/shard_map/all_to_all | solution.py:447
  83.1 5.5 %first_down.1 = (bf16[384,1536]{1,0:T(8,128)(2,1)S(1)}, bf16[384,2048]{1,0:T(8,128)(2,1)S(1)}) custom-call(s32[1]{0:T(128)} %bitcast.dp_ref, s32[1]{0:T(128)} %bitcast.1.hid_ref, bf16[48,2048]{1,0:T(8,128)(2,1)S(1)} %get-tuple-element.86.refs_0_, bf16[48,2048]{1,0:T(8,128)(2,1)S(1)} %collective-permute-done.3.refs_1_, ...), custom_call_target="tpu_custom_call" | custom-call | flops 2415919 | bytes 9043 | tf_op jit(solution)/shard_map/first_down/pallas_call | solution.py:202
  88.7 5.2 %down.3 = bf16[384,1536]{1,0:T(8,128)(2,1)S(1)} custom-call(s32[1]{0:T(128)} %bitcast.1.hid_ref, bf16[384,2048]{1,0:T(8,128)(2,1)S(1)} %get-tuple-element.99.x_ref, bf16[2048,6144]{1,0:T(8,128)(2,1)} %bitcast.18), custom_call_target="tpu_custom_call" | custom-call | flops 2415919 | bytes 9043 | tf_op jit(solution)/shard_map/down/pallas_call | solution.py:154
  93.9 0.5 collective-permute-start.21
  94.5 5.4 %down.4 = bf16[384,1536]{1,0:T(8,128)(2,1)S(1)} custom-call(s32[1]{0:T(128)} %bitcast.1.hid_ref, bf16[384,2048]{1,0:T(8,128)(2,1)S(1)} %get-tuple-element.99.x_ref, bf16[2048,6144]{1,0:T(8,128)(2,1)} %bitcast.19, bf16[384,1536]{1,0:T(8,128)(2,1)S(1)} %collective-permute-done.20.refs_0_), custom_call_target="tpu_custom_call" | custom-call | flops 2415919 | bytes 9043 | tf_op jit(solution)/shard_map/down/pallas_call | solution.py:154
  99.8 1.1 collective-permute-start.22
  101.0 5.3 %down.5.a_ref = f32[384,1536]{1,0:T(8,128)S(1)} custom-call(s32[1]{0:T(128)} %bitcast.1.hid_ref, bf16[384,2048]{1,0:T(8,128)(2,1)S(1)} %get-tuple-element.99.x_ref, bf16[2048,6144]{1,0:T(8,128)(2,1)} %bitcast.20, bf16[384,1536]{1,0:T(8,128)(2,1)S(1)} %collective-permute-done.21.refs_0_), custom_call_target="tpu_custom_call" | custom-call | flops 2415919 | bytes 10223 | tf_op jit(solution)/shard_map/down/pallas_call | solution.py:154
  106.2 1.4 copy-done.2
  107.7 16.6 %outer.1.refs_0_ = bf16[1,2048,6144]{2,1,0:T(8,128)(2,1)} custom-call(s32[1]{0:T(128)} %bitcast.1.hid_ref, bf16[384,2048]{1,0:T(8,128)(2,1)S(1)} %get-tuple-element.99.x_ref, bf16[4,384,1536]{2,1,0:T(8,128)(2,1)S(1)} %bitcast.12), custom_call_target="tpu_custom_call" | custom-call | flops 9663676 | bytes 31457 | tf_op jit(solution)/shard_map/outer/pallas_call | solution.py:334
  124.2 3.7 %collective-permute-done.22.b_ref = bf16[384,1536]{1,0:T(8,128)(2,1)} collective-permute-done((bf16[384,1536]{1,0:T(8,128)(2,1)S(1)}, bf16[384,1536]{1,0:T(8,128)(2,1)}, u32[]{:S(2)}, u32[]{:S(2)}) %collective-permute-start.22) | collective-permute-done | bytes 1179680 | tf_op jit(solution)/shard_map/ppermute | solution.py:38
  127.9 2.9 %sum_of.1 = bf16[384,1536]{1,0:T(8,128)(2,1)} custom-call(f32[384,1536]{1,0:T(8,128)} %copy-done.2, bf16[384,1536]{1,0:T(8,128)(2,1)} %collective-permute-done.22.b_ref), custom_call_target="tpu_custom_call" | custom-call | bytes 4718 | tf_op jit(solution)/shard_map/sum_of/pallas_call | solution.py:235
  130.8 6.0 %all-to-all-start.1 = ((bf16[8,48,1536]{2,1,0:T(8,128)(2,1)}), bf16[8,48,1536]{2,1,0:T(8,128)(2,1)}, u32[]{:S(2)}, u32[]{:S(2)}) async-start(bf16[8,48,1536]{2,1,0:T(8,128)(2,1)} %bitcast.21), calls=%async_computation.1 | async-start | bytes 2359296 | tf_op jit(solution)/shard_map/all_to_all | solution.py:447
  136.9 5.4 %grads.1 = (bf16[256,2048]{1,0:T(8,128)(2,1)}, bf16[256,2048]{1,0:T(8,128)(2,1)}, f32[256,1]{1,0:T(8,128)}) custom-call(s32[1,256]{1,0:T(1,128)} %copy-done.8, bf16[256,2048]{1,0:T(8,128)(2,1)} %copy-done, bf16[256,2048]{1,0:T(8,128)(2,1)} %copy-done.1, bf16[384,2048]{1,0:T(8,128)(2,1)} %bitcast.7.back_ref), custom_call_target="tpu_custom_call" | custom-call | bytes 5767 | tf_op jit(solution)/shard_map/grads/pallas_call | solution.py:374
  142.4 1.0 reduce
  143.7 1.2 collective-permute-done.23
  144.9 1.2 collective-permute-start.24
  146.1 1.7 %reshape.43.refs_1_ = bf16[128,2,2048]{2,1,0:T(2,128)(2,1)S(1)} reshape(bf16[256,2048]{1,0:T(8,128)(2,1)} %get-tuple-element.106) | data formatting | bytes 2097152 | tf_op jit(solution)/shard_map/reshape | solution.py:509
  147.9 2.1 %reshape.44.refs_2_ = bf16[128,2,2048]{2,1,0:T(2,128)(2,1)S(1)} reshape(bf16[256,2048]{1,0:T(8,128)(2,1)} %get-tuple-element.107) | data formatting | bytes 2097152 | tf_op jit(solution)/shard_map/reshape | solution.py:509
  150.1 0.8 copy.16
  150.9 14.2 %all-to-all-done.1 = bf16[8,48,1536]{2,1,0:T(8,128)(2,1)} async-done(((bf16[8,48,1536]{2,1,0:T(8,128)(2,1)}), bf16[8,48,1536]{2,1,0:T(8,128)(2,1)}, u32[]{:S(2)}, u32[]{:S(2)}) %all-to-all-start.1) | async-done | bytes 1179680 | tf_op jit(solution)/shard_map/all_to_all | solution.py:447
  165.1 2.8 %mixed.1 = bf16[1,128,1536]{2,1,0:T(8,128)(2,1)} custom-call(s32[2,128]{1,0:T(2,128)S(1)} %copy-done.9, f32[2,128]{1,0:T(2,128)S(1)} %bitcast.14, bf16[384,1536]{1,0:T(8,128)(2,1)} %bitcast.9.x_ref, bf16[1,2048,6144]{2,1,0:T(8,128)(2,1)} %outer.1.refs_0_, bf16[128,2,2048]{2,1,0:T(2,128)(2,1)S(1)} %reshape.43.refs_1_, ...), custom_call_target="tpu_custom_call" | custom-call | bytes 1572 | tf_op jit(solution)/shard_map/mixed/pallas_call | solution.py:420
  (57 shorter events, 1.0 us)
Async XLA Ops:
  3.2 9.7 %collective-permute-start = (bf16[48,1536]{1,0:T(8,128)(2,1)}, bf16[48,1536]{1,0:T(8,128)(2,1)S(1)}, u32[]{:S(2)}, u32[]{:S(2)}) collective-permute-start(bf16[48,1536]{1,0:T(8,128)(2,1)} %get-tuple-element.62), channel_id=1, source_target_pairs={{0,8},{4,12},{8,0},{12,4},{16,24},{20,28},{24,16},{28,20},{1,9},{5... | collective-permute-start | bytes 442376 | tf_op jit(solution)/shard_map/ppermute | solution.py:38
  6.2 8.4 %collective-permute-start.5 = (bf16[48,1536]{1,0:T(8,128)(2,1)}, bf16[48,1536]{1,0:T(8,128)(2,1)S(1)}, u32[]{:S(2)}, u32[]{:S(2)}) collective-permute-start(bf16[48,1536]{1,0:T(8,128)(2,1)} %get-tuple-element.70), channel_id=1, source_target_pairs={{0,12},{4,8},{8,4},{12,0},{16,28},{20,24},{24,20},{28,16},{1,13},{... | collective-permute-start | bytes 442376 | tf_op jit(solution)/shard_map/ppermute | solution.py:38
  7.6 17.1 %collective-permute-start.14 = (bf16[48,1536]{1,0:T(8,128)(2,1)}, bf16[48,1536]{1,0:T(8,128)(2,1)S(1)}, u32[]{:S(2)}, u32[]{:S(2)}) collective-permute-start(bf16[48,1536]{1,0:T(8,128)(2,1)} %get-tuple-element.82), channel_id=1, source_target_pairs={{0,4},{4,0},{8,12},{12,8},{16,20},{20,16},{24,28},{28,24},{1,5},{5... | collective-permute-start | bytes 442376 | tf_op jit(solution)/shard_map/ppermute | solution.py:38
  7.8 18.6 %collective-permute-start.7 = (bf16[48,1536]{1,0:T(8,128)(2,1)}, bf16[48,1536]{1,0:T(8,128)(2,1)S(1)}, u32[]{:S(2)}, u32[]{:S(2)}) collective-permute-start(bf16[48,1536]{1,0:T(8,128)(2,1)} %get-tuple-element.72), channel_id=1, source_target_pairs={{0,24},{4,28},{8,16},{12,20},{16,8},{20,12},{24,0},{28,4},{1,25},{... | collective-permute-start | bytes 442376 | tf_op jit(solution)/shard_map/ppermute | solution.py:38
  11.8 14.6 %collective-permute-start.8 = (bf16[48,1536]{1,0:T(8,128)(2,1)}, bf16[48,1536]{1,0:T(8,128)(2,1)S(1)}, u32[]{:S(2)}, u32[]{:S(2)}) collective-permute-start(bf16[48,1536]{1,0:T(8,128)(2,1)} %get-tuple-element.73), channel_id=1, source_target_pairs={{0,28},{4,24},{8,20},{12,16},{16,12},{20,8},{24,4},{28,0},{1,29},{... | collective-permute-start | bytes 442376 | tf_op jit(solution)/shard_map/ppermute | solution.py:38
  12.9 21.9 %collective-permute-start.1 = (bf16[48,1536]{1,0:T(8,128)(2,1)}, bf16[48,1536]{1,0:T(8,128)(2,1)S(1)}, u32[]{:S(2)}, u32[]{:S(2)}) collective-permute-start(bf16[48,1536]{1,0:T(8,128)(2,1)} %get-tuple-element.63), channel_id=1, source_target_pairs={{0,16},{4,20},{8,24},{12,28},{16,0},{20,4},{24,8},{28,12},{1,17},{... | collective-permute-start | bytes 442376 | tf_op jit(solution)/shard_map/ppermute | solution.py:38
  14.7 22.5 %collective-permute-start.6 = (bf16[48,1536]{1,0:T(8,128)(2,1)}, bf16[48,1536]{1,0:T(8,128)(2,1)S(1)}, u32[]{:S(2)}, u32[]{:S(2)}) collective-permute-start(bf16[48,1536]{1,0:T(8,128)(2,1)} %get-tuple-element.71), channel_id=1, source_target_pairs={{0,20},{4,16},{8,28},{12,24},{16,4},{20,0},{24,12},{28,8},{1,21},{... | collective-permute-start | bytes 442376 | tf_op jit(solution)/shard_map/ppermute | solution.py:38
  19.4 3.4 %copy-start.8 = (s32[1,256]{1,0:T(1,128)}, s32[1,256]{1,0:T(1,128)S(1)}, u32[]{:S(2)}) copy-start(s32[1,256]{1,0:T(1,128)S(1)} %reshape.40.key_ref) | copy-start | bytes 3076
  20.9 3.9 %copy-start = (bf16[256,2048]{1,0:T(8,128)(2,1)}, bf16[256,2048]{1,0:T(8,128)(2,1)S(1)}, u32[]{:S(2)}) copy-start(bf16[256,2048]{1,0:T(8,128)(2,1)S(1)} %reshape.41.gate_ref) | copy-start | bytes 3145732
  22.8 2.1 %copy-start.1 = (bf16[256,2048]{1,0:T(8,128)(2,1)}, bf16[256,2048]{1,0:T(8,128)(2,1)S(1)}, u32[]{:S(2)}) copy-start(bf16[256,2048]{1,0:T(8,128)(2,1)S(1)} %reshape.42.up_ref) | copy-start | bytes 3145732
  22.8 2.0 %copy-start.6 = (bf16[48,1536]{1,0:T(8,128)(2,1)S(1)}, bf16[48,1536]{1,0:T(8,128)(2,1)}, u32[]{:S(2)}) copy-start(bf16[48,1536]{1,0:T(8,128)(2,1)} %get-tuple-element.81.refs_0_) | copy-start | bytes 442372
  24.9 22.3 %collective-permute-start.16 = (bf16[192,1536]{1,0:T(8,128)(2,1)S(1)}, bf16[192,1536]{1,0:T(8,128)(2,1)S(1)}, u32[]{:S(2)}, u32[]{:S(2)}) collective-permute-start(bf16[192,1536]{1,0:T(8,128)(2,1)S(1)} %stack.3.refs_0_), channel_id=1, source_target_pairs={{0,2},{1,3},{2,0},{3,1},{4,6},{5,7},{6,4},{7,5},{8,10},{9,11},{10,... | collective-permute-start | bytes 1769480 | tf_op jit(solution)/shard_map/ppermute | solution.py:38
  37.2 13.7 %collective-permute-start.17 = (bf16[192,1536]{1,0:T(8,128)(2,1)S(1)}, bf16[192,1536]{1,0:T(8,128)(2,1)S(1)}, u32[]{:S(2)}, u32[]{:S(2)}) collective-permute-start(bf16[192,1536]{1,0:T(8,128)(2,1)S(1)} %stack.2.refs_1_), channel_id=1, source_target_pairs={{0,2},{1,3},{2,0},{3,1},{4,6},{5,7},{6,4},{7,5},{8,10},{9,11},{10,... | collective-permute-start | bytes 1769480 | tf_op jit(solution)/shard_map/ppermute | solution.py:38
  38.8 8.3 %collective-permute-start.2 = (bf16[48,2048]{1,0:T(8,128)(2,1)S(1)}, bf16[48,2048]{1,0:T(8,128)(2,1)S(1)}, u32[]{:S(2)}, u32[]{:S(2)}) collective-permute-start(bf16[48,2048]{1,0:T(8,128)(2,1)S(1)} %get-tuple-element.64), channel_id=1, source_target_pairs={{0,24},{4,28},{8,16},{12,20},{16,8},{20,12},{24,0},{28,4},{1,25},{... | collective-permute-start | bytes 589832 | tf_op jit(solution)/shard_map/ppermute | solution.py:38
  42.1 8.5 %collective-permute-start.11 = (bf16[48,2048]{1,0:T(8,128)(2,1)S(1)}, bf16[48,2048]{1,0:T(8,128)(2,1)S(1)}, u32[]{:S(2)}, u32[]{:S(2)}) collective-permute-start(bf16[48,2048]{1,0:T(8,128)(2,1)S(1)} %get-tuple-element.77), channel_id=1, source_target_pairs={{0,28},{4,24},{8,20},{12,16},{16,12},{20,8},{24,4},{28,0},{1,29},{... | collective-permute-start | bytes 589832 | tf_op jit(solution)/shard_map/ppermute | solution.py:38
  43.0 13.7 %collective-permute-start.9 = (bf16[192,1536]{1,0:T(8,128)(2,1)S(1)}, bf16[192,1536]{1,0:T(8,128)(2,1)S(1)}, u32[]{:S(2)}, u32[]{:S(2)}) collective-permute-start(bf16[192,1536]{1,0:T(8,128)(2,1)S(1)} %stack.2.refs_1_), channel_id=1, source_target_pairs={{0,1},{1,0},{2,3},{3,2},{4,5},{5,4},{6,7},{7,6},{8,9},{9,8},{10,11... | collective-permute-start | bytes 1769480 | tf_op jit(solution)/shard_map/ppermute | solution.py:38
  47.1 10.1 %collective-permute-start.15 = (bf16[192,1536]{1,0:T(8,128)(2,1)S(1)}, bf16[192,1536]{1,0:T(8,128)(2,1)S(1)}, u32[]{:S(2)}, u32[]{:S(2)}) collective-permute-start(bf16[192,1536]{1,0:T(8,128)(2,1)S(1)} %stack.3.refs_0_), channel_id=1, source_target_pairs={{0,1},{1,0},{2,3},{3,2},{4,5},{5,4},{6,7},{7,6},{8,9},{9,8},{10,11... | collective-permute-start | bytes 1769480 | tf_op jit(solution)/shard_map/ppermute | solution.py:38
  47.1 10.1 %collective-permute-start.18 = (bf16[192,1536]{1,0:T(8,128)(2,1)S(1)}, bf16[192,1536]{1,0:T(8,128)(2,1)S(1)}, u32[]{:S(2)}, u32[]{:S(2)}) collective-permute-start(bf16[192,1536]{1,0:T(8,128)(2,1)S(1)} %collective-permute-done.16.refs_4_), channel_id=1, source_target_pairs={{0,1},{1,0},{2,3},{3,2},{4,5},{5,4},{6,7},{7,6},{8,9},{9,8},{10,11... | collective-permute-start | bytes 1769480 | tf_op jit(solution)/shard_map/ppermute | solution.py:38
  51.0 9.2 %collective-permute-start.19 = (bf16[192,1536]{1,0:T(8,128)(2,1)S(1)}, bf16[192,1536]{1,0:T(8,128)(2,1)S(1)}, u32[]{:S(2)}, u32[]{:S(2)}) collective-permute-start(bf16[192,1536]{1,0:T(8,128)(2,1)S(1)} %collective-permute-done.17.refs_5_), channel_id=1, source_target_pairs={{0,1},{1,0},{2,3},{3,2},{4,5},{5,4},{6,7},{7,6},{8,9},{9,8},{10,11... | collective-permute-start | bytes 1769480 | tf_op jit(solution)/shard_map/ppermute | solution.py:38
  51.0 27.8 %collective-permute-start.13 = (bf16[48,2048]{1,0:T(8,128)(2,1)S(1)}, bf16[48,2048]{1,0:T(8,128)(2,1)S(1)}, u32[]{:S(2)}, u32[]{:S(2)}) collective-permute-start(bf16[48,2048]{1,0:T(8,128)(2,1)S(1)} %get-tuple-element.80), channel_id=1, source_target_pairs={{0,20},{4,16},{8,28},{12,24},{16,4},{20,0},{24,12},{28,8},{1,21},{... | collective-permute-start | bytes 589832 | tf_op jit(solution)/shard_map/ppermute | solution.py:38
  56.8 22.0 %collective-permute-start.3 = (bf16[48,2048]{1,0:T(8,128)(2,1)S(1)}, bf16[48,2048]{1,0:T(8,128)(2,1)S(1)}, u32[]{:S(2)}, u32[]{:S(2)}) collective-permute-start(bf16[48,2048]{1,0:T(8,128)(2,1)S(1)} %get-tuple-element.65), channel_id=1, source_target_pairs={{0,4},{4,0},{8,12},{12,8},{16,20},{20,16},{24,28},{28,24},{1,5},{5... | collective-permute-start | bytes 589832 | tf_op jit(solution)/shard_map/ppermute | solution.py:38
  57.2 21.6 %collective-permute-start.4 = (bf16[48,2048]{1,0:T(8,128)(2,1)S(1)}, bf16[48,2048]{1,0:T(8,128)(2,1)S(1)}, u32[]{:S(2)}, u32[]{:S(2)}) collective-permute-start(bf16[48,2048]{1,0:T(8,128)(2,1)S(1)} %get-tuple-element.67), channel_id=1, source_target_pairs={{0,8},{4,12},{8,0},{12,4},{16,24},{20,28},{24,16},{28,20},{1,9},{5... | collective-permute-start | bytes 589832 | tf_op jit(solution)/shard_map/ppermute | solution.py:38
  57.2 21.6 %collective-permute-start.12 = (bf16[48,2048]{1,0:T(8,128)(2,1)S(1)}, bf16[48,2048]{1,0:T(8,128)(2,1)S(1)}, u32[]{:S(2)}, u32[]{:S(2)}) collective-permute-start(bf16[48,2048]{1,0:T(8,128)(2,1)S(1)} %get-tuple-element.78), channel_id=1, source_target_pairs={{0,16},{4,20},{8,24},{12,28},{16,0},{20,4},{24,8},{28,12},{1,17},{... | collective-permute-start | bytes 589832 | tf_op jit(solution)/shard_map/ppermute | solution.py:38
  60.2 18.6 %collective-permute-start.10 = (bf16[48,2048]{1,0:T(8,128)(2,1)S(1)}, bf16[48,2048]{1,0:T(8,128)(2,1)S(1)}, u32[]{:S(2)}, u32[]{:S(2)}) collective-permute-start(bf16[48,2048]{1,0:T(8,128)(2,1)S(1)} %get-tuple-element.74), channel_id=1, source_target_pairs={{0,12},{4,8},{8,4},{12,0},{16,28},{20,24},{24,20},{28,16},{1,13},{... | collective-permute-start | bytes 589832 | tf_op jit(solution)/shard_map/ppermute | solution.py:38
  76.6 2.2 %copy-start.3 = (bf16[4,384,1536]{2,1,0:T(8,128)(2,1)}, bf16[4,384,1536]{2,1,0:T(8,128)(2,1)S(1)}, u32[]{:S(2)}) copy-start(bf16[4,384,1536]{2,1,0:T(8,128)(2,1)S(1)} %get-tuple-element.100.y_ref) | copy-start | bytes 14155780
  78.8 45.4 %all-to-all-start = ((bf16[8,48,2048]{2,1,0:T(8,128)(2,1)}), bf16[8,48,2048]{2,1,0:T(8,128)(2,1)}, u32[]{:S(2)}, u32[]{:S(2)}) async-start(bf16[8,48,2048]{2,1,0:T(8,128)(2,1)} %bitcast.6), calls=%async_computation | async-start | bytes 3145728 | tf_op jit(solution)/shard_map/all_to_all | solution.py:447
  88.6 5.8 %collective-permute-start.20 = (bf16[384,1536]{1,0:T(8,128)(2,1)S(1)}, bf16[384,1536]{1,0:T(8,128)(2,1)S(1)}, u32[]{:S(2)}, u32[]{:S(2)}) collective-permute-start(bf16[384,1536]{1,0:T(8,128)(2,1)S(1)} %get-tuple-element.96), channel_id=1, source_target_pairs={{0,1},{1,0},{2,3},{3,2},{4,5},{5,4},{6,7},{7,6},{8,9},{9,8},{10,11... | collective-permute-start | bytes 3538952 | tf_op jit(solution)/shard_map/ppermute | solution.py:38
  93.9 7.1 %collective-permute-start.21 = (bf16[384,1536]{1,0:T(8,128)(2,1)S(1)}, bf16[384,1536]{1,0:T(8,128)(2,1)S(1)}, u32[]{:S(2)}, u32[]{:S(2)}) collective-permute-start(bf16[384,1536]{1,0:T(8,128)(2,1)S(1)} %down.3), channel_id=1, source_target_pairs={{0,1},{1,0},{2,3},{3,2},{4,5},{5,4},{6,7},{7,6},{8,9},{9,8},{10,11... | collective-permute-start | bytes 3538952 | tf_op jit(solution)/shard_map/ppermute | solution.py:38
  94.5 13.2 %slice-start = ((s8[4718592]{0:T(1024)(128)(4,1)}), s8[4194304]{0:T(1024)(128)(4,1)S(1)}, s32[]{:S(2)}) async-start(s8[4718592]{0:T(1024)(128)(4,1)} %bitcast.11), calls=%async_computation.2 | async-start | bytes 8388608
  99.8 7.9 %slice-start.1 = ((s8[4718592]{0:T(1024)(128)(4,1)}), s8[524288]{0:T(1024)(128)(4,1)S(1)}, s32[]{:S(2)}) async-start(s8[4718592]{0:T(1024)(128)(4,1)} %bitcast.11), calls=%async_computation.3 | async-start | bytes 1048576
  99.8 28.1 %collective-permute-start.22 = (bf16[384,1536]{1,0:T(8,128)(2,1)S(1)}, bf16[384,1536]{1,0:T(8,128)(2,1)}, u32[]{:S(2)}, u32[]{:S(2)}) collective-permute-start(bf16[384,1536]{1,0:T(8,128)(2,1)S(1)} %down.4), channel_id=1, source_target_pairs={{0,2},{1,3},{2,0},{3,1},{4,6},{5,7},{6,4},{7,5},{8,10},{9,11},{10,... | collective-permute-start | bytes 3538952 | tf_op jit(solution)/shard_map/ppermute | solution.py:38
  106.2 1.4 copy-start.2
  130.8 6.0 %copy-start.7 = (f32[128,2]{0,1:T(2,128)S(1)}, f32[128,2]{0,1:T(2,128)}, u32[]{:S(2)}) copy-start(f32[128,2]{0,1:T(2,128)} %param.9) | copy-start | bytes 3076
  130.8 34.3 %all-to-all-start.1 = ((bf16[8,48,1536]{2,1,0:T(8,128)(2,1)}), bf16[8,48,1536]{2,1,0:T(8,128)(2,1)}, u32[]{:S(2)}, u32[]{:S(2)}) async-start(bf16[8,48,1536]{2,1,0:T(8,128)(2,1)} %bitcast.21), calls=%async_computation.1 | async-start | bytes 2359296 | tf_op jit(solution)/shard_map/all_to_all | solution.py:447
  143.6 1.3 collective-permute-start.23
  144.9 5.2 %collective-permute-start.24 = (f32[128,2]{1,0:T(8,128)S(1)}, f32[128,2]{1,0:T(8,128)S(1)}, u32[]{:S(2)}, u32[]{:S(2)}) collective-permute-start(f32[128,2]{1,0:T(8,128)S(1)} %add.6), channel_id=1, source_target_pairs={{0,2},{1,3},{2,0},{3,1},{4,6},{5,7},{6,4},{7,5},{8,10},{9,11},{10,... | collective-permute-start | bytes 3080 | tf_op jit(solution)/shard_map/ppermute | solution.py:38
  147.9 20.0 %copy-start.4 = (bf16[128,2,2048]{2,1,0:T(2,128)(2,1)}, bf16[128,2,2048]{2,1,0:T(2,128)(2,1)S(1)}, u32[]{:S(2)}) copy-start(bf16[128,2,2048]{2,1,0:T(2,128)(2,1)S(1)} %reshape.43.refs_1_) | copy-start | bytes 3145732
  147.9 17.2 %copy-start.9 = (s32[2,128]{1,0:T(2,128)S(1)}, s32[2,128]{1,0:T(2,128)}, u32[]{:S(2)}) copy-start(s32[2,128]{1,0:T(2,128)} %get-tuple-element.57.key_ref) | copy-start | bytes 3076
  150.0 17.9 %copy-start.5 = (bf16[128,2,2048]{2,1,0:T(2,128)(2,1)}, bf16[128,2,2048]{2,1,0:T(2,128)(2,1)S(1)}, u32[]{:S(2)}) copy-start(bf16[128,2,2048]{2,1,0:T(2,128)(2,1)S(1)} %reshape.44.refs_2_) | copy-start | bytes 3145732
